TPU v7x, 32 devices: a whole 2x2x4 slice. The times are simulated.
32 devices in a mesh: row: 4 (over z), col: 8 (over y, x, core).
Axes of the slice: x: 2, y: 2, z: 4, core: 2. Of those that a mesh axis runs over, the one named last changes fastest.
Arguments:
- inputs: bfloat16 [12288, 2560], P(('col', 'row')), may hold values from -6 to 6
- segments: int32 [12288], P('col'), may hold values from 0 to 4, as said below
- valid_mask: int32 [12288], P(('col', 'row')), may hold values from 0 to 1
- teacher: bfloat16 [12288, 2560], P(('col', 'row')), may hold values from -15 to 15
- cotangent: bfloat16 [12288, 2560], P(('col', 'row')), may hold values from -6 to 6
- query_down: bfloat16 [2560, 768], P(('row', 'col')), may hold values from -0.125 to 0.125
- latent_down: bfloat16 [2560, 288], P(('row', 'col')), may hold values from -0.125 to 0.125
- query_up: bfloat16 [768, 3840], P('col', 'row'), may hold values from -0.21875 to 0.21875
- latent_up: bfloat16 [256, 5120], P('col', 'row'), may hold values from -0.375 to 0.375
- output_weight: bfloat16 [2560, 2560], P('row', 'col'), may hold values from -6 to 6
- gate_weight: bfloat16 [2560, 6400], P('col', 'row'), may hold values from -0.125 to 0.125
- up_weight: bfloat16 [2560, 6400], P('col', 'row'), may hold values from -0.125 to 0.125
- down_weight: bfloat16 [6400, 2560], P('row', 'col'), may hold values from -0.4375 to 0.4375
- attn_gain: bfloat16 [2560], P(('row', 'col')), may hold values from 0.5 to 1.5
- query_gain: bfloat16 [768], P(('row', 'col')), may hold values from 0.5 to 1.5
- latent_gain: bfloat16 [256], P(('row', 'col')), may hold values from 0.5 to 1.5
- mlp_gain: bfloat16 [2560], P(('row', 'col')), may hold values from 0.5 to 1.5
Outputs:
- block_out: bfloat16 [12288, 2560], P(('col', 'row'))
- loss: float32 [], replicated
- inputs_grad: float32 [12288, 2560], P(('col', 'row'))
- query_down_grad: float32 [2560, 768], P(('row', 'col'))
- latent_down_grad: float32 [2560, 288], P(('row', 'col'))
- query_up_grad: float32 [768, 3840], P('col', 'row')
- latent_up_grad: float32 [256, 5120], P('col', 'row')
- output_weight_grad: float32 [2560, 2560], P('row', 'col')
- gate_weight_grad: float32 [2560, 6400], P('col', 'row')
- up_weight_grad: float32 [2560, 6400], P('col', 'row')
- down_weight_grad: float32 [6400, 2560], P('row', 'col')
- attention_gain_gradient: float32 [2560], P(('row', 'col'))
- query_gain_grad: float32 [768], P(('row', 'col'))
- latent_gain_grad: float32 [256], P(('row', 'col'))
- mlp_gain_grad: float32 [2560], P(('row', 'col'))
Inputs may be any that keep to these rules, and one draw needn't show every extreme that they name: `segments`: each group of 1536 consecutive tokens starts with its prompt (segment 0) of 256 to 512 tokens, then continuations 1 to 4 in order, each of 256 tokens or more; the last continuation ends the group, so that late tokens of a group read prompt keys from its first tokens.
All inputs are finite; a program needn't handle non-finite values.
Results may differ from a plain program's by a relative error of at most 0.019.
Values may be sent and summed in bfloat16 or wider, within the bound.
A program may use at most 256 MiB of HBM per device.

v0:
```python
import math

import jax
import jax.numpy as jnp
from jax import lax
from jax.sharding import PartitionSpec as P

NOPE = 64
ROPE = 32
VDIM = 64
KV_RANK = 256
CONTS = 4


EPS = 1e-05
RES = 1.4 / math.sqrt(62.0)
BASE = 10000.0


def dot_plain(left_op, right_op):
    return jnp.dot(left_op, right_op, preferred_element_type=jnp.float32)


def dot_trans_left(left_op, right_op):
    return lax.dot_general(
        left_op, right_op, (((0,), (0,)), ((), ())), preferred_element_type=jnp.float32
    )


def dot_trans_right(left_op, right_op):
    return lax.dot_general(
        left_op, right_op, (((1,), (1,)), ((), ())), preferred_element_type=jnp.float32
    )


def root_norm(values, gain):
    unit_rows = values * lax.rsqrt(jnp.mean(values * values, axis=-1, keepdims=True) + EPS)
    return (unit_rows * gain, unit_rows)


def norm_back(grad_rows, unit_rows, values, gain):
    factor = lax.rsqrt(jnp.mean(values * values, axis=-1, keepdims=True) + EPS)
    scaled = grad_rows * gain
    value_grad = factor * (
        scaled - unit_rows * jnp.mean(scaled * unit_rows, axis=-1, keepdims=True)
    )
    return (value_grad, jnp.sum(grad_rows * unit_rows, axis=0))


def rotary(segments):
    length = segments.shape[0]
    indices = jnp.arange(length, dtype=jnp.int32)
    labels = jnp.arange(CONTS + 1, dtype=jnp.int32)
    member = (segments[:, None] == labels[None, :]).astype(jnp.int32)
    counts = jnp.sum(member, axis=0)
    starts = jnp.cumsum(counts) - counts
    first_at = jnp.sum(member * starts[None, :], axis=1)
    places = jnp.where(segments == 0, indices, counts[0] + indices - first_at).astype(jnp.float32)
    freqs = BASE ** (-jnp.arange(ROPE // 2, dtype=jnp.float32) * 2.0 / ROPE)
    angles = places[:, None] * freqs[None, :]
    return (jnp.cos(angles), jnp.sin(angles))


def rotate(values, cosine, sine):
    half = values.shape[-1] // 2
    first_half = values[..., :half]
    second_half = values[..., half:]
    return jnp.concatenate(
        [first_half * cosine - second_half * sine, second_half * cosine + first_half * sine],
        axis=-1,
    )


def visible(positions, segments, begin, block):
    query_pos = begin + jnp.arange(block, dtype=jnp.int32)
    query_seg = lax.dynamic_slice_in_dim(segments, begin, block, 0)
    return (positions[None, :] <= query_pos[:, None]) & (
        (segments[None, :] == 0) | (segments[None, :] == query_seg[:, None])
    )


def head_forward(head_query, head_key, head_value, segments):
    length = head_key.shape[0]
    block = math.gcd(length, 512)
    scale = (NOPE + ROPE) ** (-0.5)
    positions = jnp.arange(length, dtype=jnp.int32)

    def one_block(block_idx):
        begin = block_idx * block
        query_rows = lax.dynamic_slice_in_dim(head_query, begin, block, 0)
        allowed = visible(positions, segments, begin, block)
        scores = jnp.where(allowed, dot_trans_right(query_rows, head_key) * scale, -jnp.inf)
        top_val = jnp.max(scores, axis=-1, keepdims=True)
        expo = jnp.exp(scores - top_val)
        total = jnp.sum(expo, axis=-1, keepdims=True)
        out_rows = dot_plain((expo / total).astype(jnp.bfloat16), head_value)
        return (out_rows, (top_val + jnp.log(total))[:, 0])

    out_blocks, lse_blocks = lax.map(one_block, jnp.arange(length // block, dtype=jnp.int32))
    return (out_blocks.reshape(length, head_value.shape[1]), lse_blocks.reshape(length))


def head_back(head_query, head_key, head_value, head_grad, head_lse, segments):
    length = head_key.shape[0]
    block = math.gcd(length, 512)
    scale = (NOPE + ROPE) ** (-0.5)
    positions = jnp.arange(length, dtype=jnp.int32)

    def one_block(carry, block_idx):
        key_acc, value_acc = carry
        begin = block_idx * block
        query_rows = lax.dynamic_slice_in_dim(head_query, begin, block, 0)
        grad_rows = lax.dynamic_slice_in_dim(head_grad, begin, block, 0)
        lse_rows = lax.dynamic_slice_in_dim(head_lse, begin, block, 0)
        allowed = visible(positions, segments, begin, block)
        scores = jnp.where(allowed, dot_trans_right(query_rows, head_key) * scale, -jnp.inf)
        weights_p = jnp.exp(scores - lse_rows[:, None])
        prob_grad = dot_trans_right(grad_rows, head_value)
        inner = jnp.sum(weights_p * prob_grad, axis=-1, keepdims=True)
        score_grad = (weights_p * (prob_grad - inner)).astype(jnp.bfloat16)
        query_grad = scale * dot_plain(score_grad, head_key)
        key_acc = key_acc + scale * dot_trans_left(score_grad, query_rows)
        value_acc = value_acc + dot_trans_left(weights_p.astype(jnp.bfloat16), grad_rows)
        return ((key_acc, value_acc), query_grad)

    start_acc = (jnp.zeros(head_key.shape, jnp.float32), jnp.zeros(head_value.shape, jnp.float32))
    (key_acc, value_acc), query_blocks = lax.scan(
        one_block, start_acc, jnp.arange(length // block, dtype=jnp.int32)
    )
    return (query_blocks.reshape(length, head_query.shape[1]), key_acc, value_acc)


def partial_rows(left_operand_rows, right_full):
    return lax.psum_scatter(
        dot_plain(left_operand_rows, right_full).astype(jnp.bfloat16),
        "row",
        scatter_dimension=0,
        tiled=True,
    ).astype(jnp.float32)


def token_rows(values):
    return lax.all_gather(values, "row", axis=0, tiled=True)


def body(
    inputs,
    segments,
    valid_mask,
    teacher,
    cotangent,
    query_down,
    latent_down,
    query_up,
    latent_up,
    output_weight,
    gate_weight,
    up_weight,
    down_weight,
    attn_gain,
    query_gain,
    latent_gain,
    mlp_gain,
):
    row_total = lax.axis_size("row")
    col_total = lax.axis_size("col")
    row_rank = lax.axis_index("row")
    local_rows = inputs.shape[0]
    length = segments.shape[0]
    heads_here = output_weight.shape[0] // VDIM
    offset = row_rank * local_rows
    valid_total = lax.psum(jnp.sum(valid_mask), ("row", "col")).astype(jnp.float32)
    qd_full, kvd_full, attn_g, query_g, latent_g, mlp_g = (
        lax.all_gather(query_down, ("row", "col"), axis=0, tiled=True),
        lax.all_gather(latent_down, ("row", "col"), axis=0, tiled=True),
        lax.all_gather(attn_gain, ("row", "col"), axis=0, tiled=True),
        lax.all_gather(query_gain, ("row", "col"), axis=0, tiled=True),
        lax.all_gather(latent_gain, ("row", "col"), axis=0, tiled=True),
        lax.all_gather(mlp_gain, ("row", "col"), axis=0, tiled=True),
    )
    attn_g = attn_g.astype(jnp.float32)
    query_g = query_g.astype(jnp.float32)
    latent_g = latent_g.astype(jnp.float32)
    mlp_g = mlp_g.astype(jnp.float32)
    qu_full, kvu_full, out_full = (
        lax.all_gather(query_up, "col", axis=0, tiled=True),
        lax.all_gather(latent_up, "col", axis=0, tiled=True),
        lax.all_gather(output_weight, "col", axis=1, tiled=True),
    )
    gate_full, up_full, down_full = (
        lax.all_gather(gate_weight, "col", axis=0, tiled=True),
        lax.all_gather(up_weight, "col", axis=0, tiled=True),
        lax.all_gather(down_weight, "col", axis=1, tiled=True),
    )
    cosine, sine = rotary(segments)
    cos_here = lax.dynamic_slice_in_dim(cosine, offset, local_rows, 0)
    sin_here = lax.dynamic_slice_in_dim(sine, offset, local_rows, 0)
    tokens_f = inputs.astype(jnp.float32)
    normed, normed_unit = root_norm(tokens_f, attn_g)
    normed_b = normed.astype(jnp.bfloat16)
    normed_all = lax.all_gather(normed_b, "row", axis=0, tiled=True)
    query_lat = dot_plain(normed_all, qd_full)
    kv_lat = dot_plain(normed_all, kvd_full)
    query_norm, query_unit = root_norm(query_lat, query_g)
    kv_norm, kv_unit = root_norm(kv_lat[:, :KV_RANK], latent_g)
    key_rope = rotate(kv_lat[:, KV_RANK:], cosine, sine)
    lat_all = (
        query_lat,
        kv_lat,
        query_unit,
        kv_unit,
        query_norm.astype(jnp.bfloat16),
        kv_norm.astype(jnp.bfloat16),
        key_rope.astype(jnp.bfloat16),
    )
    query_lat = lax.dynamic_slice_in_dim(lat_all[0], offset, local_rows, 0)
    kv_lat = lax.dynamic_slice_in_dim(lat_all[1], offset, local_rows, 0)
    query_unit = lax.dynamic_slice_in_dim(lat_all[2], offset, local_rows, 0)
    kv_unit = lax.dynamic_slice_in_dim(lat_all[3], offset, local_rows, 0)
    query_all = lat_all[4]
    kv_all = lat_all[5]
    rope_all = lat_all[6]
    query_proj = dot_plain(query_all, qu_full).reshape(length, heads_here, NOPE + ROPE)
    query_vectors = jnp.concatenate(
        [
            query_proj[:, :, :NOPE],
            rotate(query_proj[:, :, NOPE:], cosine[:, None, :], sine[:, None, :]),
        ],
        axis=-1,
    ).astype(jnp.bfloat16)
    kv_proj = dot_plain(kv_all, kvu_full).reshape(length, heads_here, NOPE + VDIM)
    key_rows = jnp.concatenate(
        [
            kv_proj[:, :, :NOPE].astype(jnp.bfloat16),
            jnp.broadcast_to(rope_all[:, None, :], (length, heads_here, ROPE)),
        ],
        axis=-1,
    )
    values = kv_proj[:, :, NOPE:].astype(jnp.bfloat16)
    head_query = jnp.transpose(query_vectors, (1, 0, 2))
    head_key = jnp.transpose(key_rows, (1, 0, 2))
    head_value = jnp.transpose(values, (1, 0, 2))
    head_out, head_lse = lax.map(
        lambda operands: head_forward(operands[0], operands[1], operands[2], segments),
        (head_query, head_key, head_value),
    )
    mixed_out = (
        jnp.transpose(head_out, (1, 0, 2)).reshape(length, heads_here * VDIM).astype(jnp.bfloat16)
    )
    attn_sum = partial_rows(mixed_out, out_full)
    residual = tokens_f + RES * attn_sum
    mlp_in, mlp_unit = root_norm(residual, mlp_g)
    mlp_all = token_rows(mlp_in.astype(jnp.bfloat16))
    gate_act = dot_plain(mlp_all, gate_full)
    up_act = dot_plain(mlp_all, up_full)
    gate_sig = jax.nn.sigmoid(gate_act)
    silu_val = gate_act * gate_sig
    hidden = (silu_val * up_act).astype(jnp.bfloat16)
    outputs = residual + RES * partial_rows(hidden, down_full)
    error_val = outputs - teacher.astype(jnp.float32)
    weight_v = valid_mask.astype(jnp.float32)[:, None]
    total_tokens = local_rows * row_total * col_total
    squared = lax.psum(0.5 * jnp.sum(weight_v * error_val * error_val), ("row", "col"))
    out_grad = cotangent.astype(jnp.float32) + total_tokens / valid_total * weight_v * error_val
    branch_grad = token_rows((RES * out_grad).astype(jnp.bfloat16))
    down_wg = dot_trans_left(hidden, branch_grad)
    hidden_grad = dot_trans_right(branch_grad, down_full)
    gate_grad = (hidden_grad * up_act * gate_sig * (1.0 + gate_act * (1.0 - gate_sig))).astype(
        jnp.bfloat16
    )
    up_grad = (hidden_grad * silu_val).astype(jnp.bfloat16)
    gate_wg = dot_trans_left(mlp_all, gate_grad)
    up_wg = dot_trans_left(mlp_all, up_grad)
    gate_wg, up_wg, down_wg = (
        lax.psum_scatter(
            gate_wg.astype(jnp.bfloat16), "col", scatter_dimension=0, tiled=True
        ).astype(jnp.float32),
        lax.psum_scatter(up_wg.astype(jnp.bfloat16), "col", scatter_dimension=0, tiled=True).astype(
            jnp.float32
        ),
        lax.psum_scatter(
            down_wg.astype(jnp.bfloat16), "col", scatter_dimension=1, tiled=True
        ).astype(jnp.float32),
    )
    mlp_in_grad = lax.psum_scatter(
        (dot_trans_right(gate_grad, gate_full) + dot_trans_right(up_grad, up_full)).astype(
            jnp.bfloat16
        ),
        "row",
        scatter_dimension=0,
        tiled=True,
    ).astype(jnp.float32)
    residual_part, mlp_gain_grad = norm_back(mlp_in_grad, mlp_unit, residual, mlp_g)
    residual_grad = out_grad + residual_part
    attn_grad_all = token_rows((RES * residual_grad).astype(jnp.bfloat16))
    out_wg = dot_trans_left(mixed_out, attn_grad_all)
    mixed_grad = (
        dot_trans_right(attn_grad_all, out_full)
        .astype(jnp.bfloat16)
        .reshape(length, heads_here, VDIM)
    )
    head_grad = jnp.transpose(mixed_grad, (1, 0, 2))
    query_back, key_back, value_back = lax.map(
        lambda operands: head_back(
            operands[0], operands[1], operands[2], operands[3], operands[4], segments
        ),
        (head_query, head_key, head_value, head_grad, head_lse),
    )
    query_back = jnp.transpose(query_back, (1, 0, 2))
    key_back = jnp.transpose(key_back, (1, 0, 2))
    value_back = jnp.transpose(value_back, (1, 0, 2))
    query_proj_grad = (
        jnp.concatenate(
            [
                query_back[:, :, :NOPE],
                rotate(query_back[:, :, NOPE:], cosine[:, None, :], -sine[:, None, :]),
            ],
            axis=-1,
        )
        .reshape(length, heads_here * (NOPE + ROPE))
        .astype(jnp.bfloat16)
    )
    rope_part = jnp.sum(key_back[:, :, NOPE:], axis=1)
    kv_proj_grad = (
        jnp.concatenate([key_back[:, :, :NOPE], value_back], axis=-1)
        .reshape(length, heads_here * (NOPE + VDIM))
        .astype(jnp.bfloat16)
    )
    qu_wg = dot_trans_left(query_all, query_proj_grad)
    kvu_wg = dot_trans_left(kv_all, kv_proj_grad)
    qu_wg, kvu_wg, out_wg = (
        lax.psum_scatter(qu_wg.astype(jnp.bfloat16), "col", scatter_dimension=0, tiled=True).astype(
            jnp.float32
        ),
        lax.psum_scatter(
            kvu_wg.astype(jnp.bfloat16), "col", scatter_dimension=0, tiled=True
        ).astype(jnp.float32),
        lax.psum_scatter(
            out_wg.astype(jnp.bfloat16), "col", scatter_dimension=1, tiled=True
        ).astype(jnp.float32),
    )
    query_norm_grad, kv_norm_grad, rope_grad = (
        lax.psum_scatter(
            dot_trans_right(query_proj_grad, qu_full).astype(jnp.bfloat16),
            "row",
            scatter_dimension=0,
            tiled=True,
        ).astype(jnp.float32),
        lax.psum_scatter(
            dot_trans_right(kv_proj_grad, kvu_full).astype(jnp.bfloat16),
            "row",
            scatter_dimension=0,
            tiled=True,
        ).astype(jnp.float32),
        lax.psum_scatter(
            rope_part.astype(jnp.bfloat16), "row", scatter_dimension=0, tiled=True
        ).astype(jnp.float32),
    )
    query_lat_grad, query_gain_grad = norm_back(query_norm_grad, query_unit, query_lat, query_g)
    kv_lat_part, latent_gain_grad = norm_back(kv_norm_grad, kv_unit, kv_lat[:, :KV_RANK], latent_g)
    kv_lat_grad = jnp.concatenate(
        [kv_lat_part, rotate(rope_grad, cos_here, -sin_here)], axis=-1
    ).astype(jnp.bfloat16)
    query_lat_gb = query_lat_grad.astype(jnp.bfloat16)
    qd_wg = dot_trans_left(normed_b, query_lat_gb)
    kvd_wg = dot_trans_left(normed_b, kv_lat_grad)
    normed_grad = dot_trans_right(query_lat_gb, qd_full) + dot_trans_right(kv_lat_grad, kvd_full)
    input_part, attention_gain_gradient = norm_back(normed_grad, normed_unit, tokens_f, attn_g)
    input_grad = residual_grad + input_part
    small_sums = (
        lax.psum_scatter(qd_wg, ("row", "col"), scatter_dimension=0, tiled=True),
        lax.psum_scatter(kvd_wg, ("row", "col"), scatter_dimension=0, tiled=True),
        lax.psum_scatter(attention_gain_gradient, ("row", "col"), scatter_dimension=0, tiled=True),
        lax.psum_scatter(query_gain_grad, ("row", "col"), scatter_dimension=0, tiled=True),
        lax.psum_scatter(latent_gain_grad, ("row", "col"), scatter_dimension=0, tiled=True),
        lax.psum_scatter(mlp_gain_grad, ("row", "col"), scatter_dimension=0, tiled=True),
    )
    return (
        outputs.astype(jnp.bfloat16),
        squared / valid_total,
        input_grad,
        small_sums[0],
        small_sums[1],
        qu_wg,
        kvu_wg,
        out_wg,
        gate_wg,
        up_wg,
        down_wg,
        small_sums[2],
        small_sums[3],
        small_sums[4],
        small_sums[5],
    )


def solution(mesh):
    in_specs = (
        P(("col", "row"), None),
        P("col"),
        P(("col", "row")),
        P(("col", "row"), None),
        P(("col", "row"), None),
        P(("row", "col"), None),
        P(("row", "col"), None),
        P("col", "row"),
        P("col", "row"),
        P("row", "col"),
        P("col", "row"),
        P("col", "row"),
        P("row", "col"),
        P(("row", "col")),
        P(("row", "col")),
        P(("row", "col")),
        P(("row", "col")),
    )
    out_specs = (
        P(("col", "row"), None),
        P(),
        P(("col", "row"), None),
        P(("row", "col"), None),
        P(("row", "col"), None),
        P("col", "row"),
        P("col", "row"),
        P("row", "col"),
        P("col", "row"),
        P("col", "row"),
        P("row", "col"),
        P(("row", "col")),
        P(("row", "col")),
        P(("row", "col")),
        P(("row", "col")),
    )
    return jax.shard_map(body, mesh=mesh, in_specs=in_specs, out_specs=out_specs, check_vma=False)
```

profile of v0, /device:TPU:0, one launch (start us, length us, event | category | flops | bytes accessed | tf_op | source)
XLA Modules:
  0.0 3000.5 jit_solution(17403957698042300100)
XLA Ops:
  11.4 42.4 %all-reduce.9 = (bf16[2560]{0:T(1024)(128)(2,1)}, bf16[2560]{0:T(1024)(128)(2,1)S(1)}, bf16[768]{0:T(1024)(128)(2,1)S(1)}, bf16[256]{0:T(256)(128)(2,1)S(1)}) all-reduce(bf16[2560]{0:T(1024)(128)(2,1)S(1)} %dynamic-update-slice.3, bf16[2560]{0:T(1024)(128)(2,1)S(1)} %dynamic-update-slice, ...), channel_id=1, replica_groups=mesh['row'=4,'col'=8] {'row','col'}, use_global_device_ids=true, to_apply=%add.3 | all-reduce | flops 6144 | bytes 24576
  75.0 142.0 %all-gather.12.cloned.1.call-done = bf16[1536,2560]{1,0:T(8,128)(2,1)} async-done(((bf16[384,2560]{1,0:T(8,128)(2,1)}), bf16[1536,2560]{1,0:T(8,128)(2,1)}) %all-gather.12.cloned.1.call-update) | async-done | bytes 7864336 | tf_op jit(solution)/shard_map/all_gather | solution.py:201
  252.3 49.4 %all-gather.18.cloned.1.call-done = bf16[2560,288]{1,0:T(8,128)(2,1)} async-done(((bf16[80,288]{1,0:T(8,128)(2,1)}), bf16[2560,288]{1,0:T(8,128)(2,1)}) %all-gather.18.cloned.1.call-update) | async-done | bytes 1474576 | tf_op jit(solution)/shard_map/all_gather | solution.py:175
  337.4 359.1 %while.55 = (s32[]{:T(128)}, bf16[10,1536,64]{1,2,0:T(8,128)(2,1)}, f32[10,1536]{1,0:T(8,128)}, bf16[10,1536,96]{2,1,0:T(8,128)(2,1)}, bf16[10,1536,96]{2,1,0:T(...) while((s32[]{:T(128)}, bf16[10,1536,64]{1,2,0:T(8,128)(2,1)}, ...), condition=%wide.region_11.12_spmd, body=%wide.region_6.11_spmd.sunk | while | flops 261096960 | bytes 13212100 | solution.py:243
  708.1 134.3 %reduce-scatter.21.cloned.1.call-done = bf16[384,2560]{1,0:T(8,128)(2,1)} async-done(((bf16[1536,2560]{1,0:T(8,128)(2,1)}), bf16[384,2560]{1,0:T(8,128)(2,1)}) %reduce-scatter.21.cloned.1.call-update) | async-done | bytes 1966096 | tf_op jit(solution)/shard_map/reduce_scatter | solution.py:134
  849.1 50.7 %all-gather.24.cloned.1.call-done = bf16[2560,1600]{1,0:T(8,128)(2,1)} async-done(((bf16[320,1600]{1,0:T(8,128)(2,1)}), bf16[2560,1600]{1,0:T(8,128)(2,1)}) %all-gather.24.cloned.1.call-update) | async-done | bytes 8192016 | tf_op jit(solution)/shard_map/all_gather | solution.py:191
  899.8 143.2 %all-gather.22.cloned.1.call-done = bf16[1536,2560]{1,0:T(8,128)(2,1)} async-done(((bf16[384,2560]{1,0:T(8,128)(2,1)}), bf16[1536,2560]{1,0:T(8,128)(2,1)}) %all-gather.22.cloned.1.call-update) | async-done | bytes 7864336 | tf_op jit(solution)/shard_map/all_gather | solution.py:143
  1062.4 35.7 %all-gather.26.cloned.1.call-done = bf16[2560,1600]{1,0:T(8,128)(2,1)} async-done(((bf16[320,1600]{1,0:T(8,128)(2,1)}), bf16[2560,1600]{1,0:T(8,128)(2,1)}) %all-gather.26.cloned.1.call-update) | async-done | bytes 8192016 | tf_op jit(solution)/shard_map/all_gather | solution.py:192
  1176.8 47.6 %psum.15 = s32[]{:T(128)} all-reduce(s32[]{:T(128)} %get-tuple-element.467), channel_id=1, replica_groups=mesh['row'=4,'col'=8] {'row','col'}, use_global_device_ids=true, to_apply=%region_18.19 | all-reduce | flops 1 | bytes 8 | tf_op jit(solution)/shard_map/psum | solution.py:172
  1225.1 87.9 %reduce-scatter.23.cloned.1.call-done = bf16[384,2560]{1,0:T(8,128)(2,1)} async-done(((bf16[1536,2560]{1,0:T(8,128)(2,1)}), bf16[384,2560]{1,0:T(8,128)(2,1)}) %reduce-scatter.23.cloned.1.call-update) | async-done | bytes 1966096 | tf_op jit(solution)/shard_map/reduce_scatter | solution.py:134
  1319.4 141.6 %all-gather.30.cloned.1.call-done = bf16[1536,2560]{1,0:T(8,128)(2,1)} async-done(((bf16[384,2560]{1,0:T(8,128)(2,1)}), bf16[1536,2560]{1,0:T(8,128)(2,1)}) %all-gather.30.cloned.1.call-update) | async-done | bytes 7864336 | tf_op jit(solution)/shard_map/all_gather | solution.py:143
  1532.3 134.6 %reduce-scatter.25.cloned.1.call-done = bf16[384,2560]{1,0:T(8,128)(2,1)} async-done(((bf16[1536,2560]{1,0:T(8,128)(2,1)}), bf16[384,2560]{1,0:T(8,128)(2,1)}) %reduce-scatter.25.cloned.1.call-update) | async-done | bytes 1966096 | tf_op jit(solution)/shard_map/reduce_scatter | solution.py:285
  1679.0 141.7 %all-gather.32.cloned.1.call-done = bf16[1536,2560]{1,0:T(8,128)(2,1)} async-done(((bf16[384,2560]{1,0:T(8,128)(2,1)}), bf16[1536,2560]{1,0:T(8,128)(2,1)}) %all-gather.32.cloned.1.call-update) | async-done | bytes 7864336 | tf_op jit(solution)/shard_map/all_gather | solution.py:143
  1834.2 461.8 %while.57 = (s32[]{:T(128)}, f32[10,1536,96]{1,2,0:T(8,128)}, f32[10,1536,96]{1,2,0:T(8,128)}, bf16[10,1536,64]{1,2,0:T(8,128)(2,1)}, bf16[10,1536,96]{2,1,0:T(8...) while((s32[]{:T(128)}, f32[10,1536,96]{1,2,0:T(8,128)}, ...), condition=%wide.region_26.27_spmd, body=%wide.region_22.26_spmd.sunk | while | flops 665224704 | bytes 59753560 | solution.py:303
  1840.7 36.3 %while.59 = (s32[]{:T(128)}, f32[1536,96]{0,1:T(8,128)S(1)}, f32[1536,64]{0,1:T(8,128)S(1)}, f32[3,512,96]{1,2,0:T(8,128)}, s32[3]{0:T(128)S(1)}, /*index=5*/s32...) while((s32[]{:T(128)}, f32[1536,96]{0,1:T(8,128)S(1)}, ...), condition=%wide.region_25.25_spmd.clone, body=%wide.region_23.24_spmd.clone.sunk | while | flops 665224704 | bytes 52268836 | solution.py:127
  1886.9 36.3 %while.59 = (s32[]{:T(128)}, f32[1536,96]{0,1:T(8,128)S(1)}, f32[1536,64]{0,1:T(8,128)S(1)}, f32[3,512,96]{1,2,0:T(8,128)}, s32[3]{0:T(128)S(1)}, /*index=5*/s32...) while((s32[]{:T(128)}, f32[1536,96]{0,1:T(8,128)S(1)}, ...), condition=%wide.region_25.25_spmd.clone, body=%wide.region_23.24_spmd.clone.sunk | while | flops 665224704 | bytes 52268836 | solution.py:127
  1933.0 36.3 %while.59 = (s32[]{:T(128)}, f32[1536,96]{0,1:T(8,128)S(1)}, f32[1536,64]{0,1:T(8,128)S(1)}, f32[3,512,96]{1,2,0:T(8,128)}, s32[3]{0:T(128)S(1)}, /*index=5*/s32...) while((s32[]{:T(128)}, f32[1536,96]{0,1:T(8,128)S(1)}, ...), condition=%wide.region_25.25_spmd.clone, body=%wide.region_23.24_spmd.clone.sunk | while | flops 665224704 | bytes 52268836 | solution.py:127
  1979.2 36.3 %while.59 = (s32[]{:T(128)}, f32[1536,96]{0,1:T(8,128)S(1)}, f32[1536,64]{0,1:T(8,128)S(1)}, f32[3,512,96]{1,2,0:T(8,128)}, s32[3]{0:T(128)S(1)}, /*index=5*/s32...) while((s32[]{:T(128)}, f32[1536,96]{0,1:T(8,128)S(1)}, ...), condition=%wide.region_25.25_spmd.clone, body=%wide.region_23.24_spmd.clone.sunk | while | flops 665224704 | bytes 52268836 | solution.py:127
  2025.4 36.3 %while.59 = (s32[]{:T(128)}, f32[1536,96]{0,1:T(8,128)S(1)}, f32[1536,64]{0,1:T(8,128)S(1)}, f32[3,512,96]{1,2,0:T(8,128)}, s32[3]{0:T(128)S(1)}, /*index=5*/s32...) while((s32[]{:T(128)}, f32[1536,96]{0,1:T(8,128)S(1)}, ...), condition=%wide.region_25.25_spmd.clone, body=%wide.region_23.24_spmd.clone.sunk | while | flops 665224704 | bytes 52268836 | solution.py:127
  2071.6 36.3 %while.59 = (s32[]{:T(128)}, f32[1536,96]{0,1:T(8,128)S(1)}, f32[1536,64]{0,1:T(8,128)S(1)}, f32[3,512,96]{1,2,0:T(8,128)}, s32[3]{0:T(128)S(1)}, /*index=5*/s32...) while((s32[]{:T(128)}, f32[1536,96]{0,1:T(8,128)S(1)}, ...), condition=%wide.region_25.25_spmd.clone, body=%wide.region_23.24_spmd.clone.sunk | while | flops 665224704 | bytes 52268836 | solution.py:127
  2117.8 36.3 %while.59 = (s32[]{:T(128)}, f32[1536,96]{0,1:T(8,128)S(1)}, f32[1536,64]{0,1:T(8,128)S(1)}, f32[3,512,96]{1,2,0:T(8,128)}, s32[3]{0:T(128)S(1)}, /*index=5*/s32...) while((s32[]{:T(128)}, f32[1536,96]{0,1:T(8,128)S(1)}, ...), condition=%wide.region_25.25_spmd.clone, body=%wide.region_23.24_spmd.clone.sunk | while | flops 665224704 | bytes 52268836 | solution.py:127
  2164.0 36.3 %while.59 = (s32[]{:T(128)}, f32[1536,96]{0,1:T(8,128)S(1)}, f32[1536,64]{0,1:T(8,128)S(1)}, f32[3,512,96]{1,2,0:T(8,128)}, s32[3]{0:T(128)S(1)}, /*index=5*/s32...) while((s32[]{:T(128)}, f32[1536,96]{0,1:T(8,128)S(1)}, ...), condition=%wide.region_25.25_spmd.clone, body=%wide.region_23.24_spmd.clone.sunk | while | flops 665224704 | bytes 52268836 | solution.py:127
  2210.1 36.3 %while.59 = (s32[]{:T(128)}, f32[1536,96]{0,1:T(8,128)S(1)}, f32[1536,64]{0,1:T(8,128)S(1)}, f32[3,512,96]{1,2,0:T(8,128)}, s32[3]{0:T(128)S(1)}, /*index=5*/s32...) while((s32[]{:T(128)}, f32[1536,96]{0,1:T(8,128)S(1)}, ...), condition=%wide.region_25.25_spmd.clone, body=%wide.region_23.24_spmd.clone.sunk | while | flops 665224704 | bytes 52268836 | solution.py:127
  2256.3 36.3 %while.59 = (s32[]{:T(128)}, f32[1536,96]{0,1:T(8,128)S(1)}, f32[1536,64]{0,1:T(8,128)S(1)}, f32[3,512,96]{1,2,0:T(8,128)}, s32[3]{0:T(128)S(1)}, /*index=5*/s32...) while((s32[]{:T(128)}, f32[1536,96]{0,1:T(8,128)S(1)}, ...), condition=%wide.region_25.25_spmd.clone, body=%wide.region_23.24_spmd.clone.sunk | while | flops 665224704 | bytes 52268836 | solution.py:127
  2429.7 39.6 %reduce-scatter.41.cloned.1.call-done = bf16[1600,320]{0,1:T(8,128)(2,1)} async-done(((bf16[1600,2560]{0,1:T(8,128)(2,1)}), bf16[1600,320]{0,1:T(8,128)(2,1)}) %reduce-scatter.41.cloned.1.call-update) | async-done | bytes 1024016 | tf_op jit(solution)/shard_map/reduce_scatter | solution.py:281
  2472.0 73.3 %reduce-scatter.37.cloned.1.call-done = bf16[320,1600]{1,0:T(8,128)(2,1)} async-done(((bf16[2560,1600]{1,0:T(8,128)(2,1)}), bf16[320,1600]{1,0:T(8,128)(2,1)}) %reduce-scatter.37.cloned.1.call-update) | async-done | bytes 1024016 | tf_op jit(solution)/shard_map/reduce_scatter | solution.py:275
  2548.0 73.2 %reduce-scatter.39.cloned.1.call-done = bf16[320,1600]{1,0:T(8,128)(2,1)} async-done(((bf16[2560,1600]{1,0:T(8,128)(2,1)}), bf16[320,1600]{1,0:T(8,128)(2,1)}) %reduce-scatter.39.cloned.1.call-update) | async-done | bytes 1024016 | tf_op jit(solution)/shard_map/reduce_scatter | solution.py:278
  2624.5 34.7 %reduce-scatter.33.cloned.1.call-done = bf16[32,1280]{1,0:T(8,128)(2,1)} async-done(((bf16[256,1280]{1,0:T(8,128)(2,1)}), bf16[32,1280]{1,0:T(8,128)(2,1)}) %reduce-scatter.33.cloned.1.call-update) | async-done | bytes 81936 | tf_op jit(solution)/shard_map/reduce_scatter | solution.py:335
  2660.7 41.2 %reduce-scatter.31.cloned.1.call-done = bf16[96,960]{1,0:T(8,128)(2,1)} async-done(((bf16[768,960]{1,0:T(8,128)(2,1)}), bf16[96,960]{1,0:T(8,128)(2,1)}) %reduce-scatter.31.cloned.1.call-update) | async-done | bytes 184336 | tf_op jit(solution)/shard_map/reduce_scatter | solution.py:332
  2712.2 40.3 %all-reduce.8 = (f32[]{:T(128)}, f32[2560]{0:T(1024)S(1)}, f32[768]{0:T(1024)S(1)}, f32[256]{0:T(256)S(1)}, f32[2560]{0:T(1024)S(1)}) all-reduce(f32[]{:T(128)S(6)} %mul_shard_map.3, f32[2560]{0:T(1024)S(1)} %get-tuple-element.350, f32[768]{0:T(1024)S(1)} %copy-done.46, ...), channel_id=1, replica_groups=mesh['row'=4,'col'=8] {'row','col'}, use_global_device_ids=true, to_apply=%region_16.17 | all-reduce | flops 6145 | bytes 49160 | tf_op jit(solution)/shard_map/psum | solution.py:263
  2763.7 100.2 %reduce-scatter.29.cloned.1.call-done = f32[80,288]{1,0:T(8,128)} async-done(((f32[2560,288]{1,0:T(8,128)}), f32[80,288]{1,0:T(8,128)}) %reduce-scatter.29.cloned.1.call-update) | async-done | bytes 92176 | tf_op jit(solution)/shard_map/reduce_scatter | solution.py:372
  2863.9 128.5 %reduce-scatter.27.cloned.1.call-done = f32[80,768]{1,0:T(8,128)} async-done(((f32[2560,768]{1,0:T(8,128)}), f32[80,768]{1,0:T(8,128)}) %reduce-scatter.27.cloned.1.call-update) | async-done | bytes 245776 | tf_op jit(solution)/shard_map/reduce_scatter | solution.py:371
  (1239 shorter events, 1532.9 us)
Async XLA Ops:
  7.2 67.8 %all-gather.14.cloned.1.call-start = ((), (), s32[]{:S(2)}) async-start(), calls=%async_computation.15 | async-start | bytes 4055040 | tf_op jit(solution)/shard_map/all_gather | solution.py:174
  7.9 209.0 %all-gather.12.cloned.1.call-start = ((), (), s32[]{:S(2)}) async-start(), calls=%async_computation.14 | async-start | bytes 9830400 | tf_op jit(solution)/shard_map/all_gather | solution.py:201
  60.0 182.8 %all-gather.16.cloned.1.call-start = ((), (), s32[]{:S(2)}) async-start(), calls=%async_computation.16 | async-start | bytes 1769472 | tf_op jit(solution)/shard_map/all_gather | solution.py:186
  60.7 241.0 %all-gather.18.cloned.1.call-start = ((), (), s32[]{:S(2)}) async-start(), calls=%async_computation.17 | async-start | bytes 2027520 | tf_op jit(solution)/shard_map/all_gather | solution.py:175
  61.3 635.2 %all-gather.20.cloned.1.call-start = ((), (), s32[]{:S(2)}) async-start(), calls=%async_computation.18 | async-start | bytes 3686400 | tf_op jit(solution)/shard_map/all_gather | solution.py:188
  61.9 780.6 %reduce-scatter.21.cloned.1.call-start = ((), (), s32[]{:S(2)}) async-start(), calls=%async_computation.19 | async-start | bytes 9830400 | tf_op jit(solution)/shard_map/reduce_scatter | solution.py:134
  62.0 180.8 %copy-start.40 = (f32[768]{0:T(1024)}, f32[768]{0:T(1024)S(1)}, u32[]{:S(2)}) copy-start(f32[768]{0:T(1024)S(1)} %convert_element_type.179) | copy-start | bytes 9220
  62.4 254.3 %copy-start.47 = (f32[256]{0:T(256)}, f32[256]{0:T(256)S(1)}, u32[]{:S(2)}) copy-start(f32[256]{0:T(256)S(1)} %convert_element_type.183) | copy-start | bytes 3076
  707.1 135.4 %copy-start.2 = (bf16[384,2560]{1,0:T(8,128)(2,1)S(1)}, bf16[384,2560]{1,0:T(8,128)(2,1)}, u32[]{:S(2)}) copy-start(bf16[384,2560]{1,0:T(8,128)(2,1)} %param.25) | copy-start | bytes 5898244
  707.1 192.7 %all-gather.24.cloned.1.call-start = ((), (), s32[]{:S(2)}) async-start(), calls=%async_computation.21 | async-start | bytes 9584640 | tf_op jit(solution)/shard_map/all_gather | solution.py:191
  707.8 335.2 %all-gather.22.cloned.1.call-start = ((), (), s32[]{:S(2)}) async-start(), calls=%async_computation.20 | async-start | bytes 9830400 | tf_op jit(solution)/shard_map/all_gather | solution.py:143
  708.1 139.6 %copy-start.33 = (f32[2560]{0:T(1024)}, f32[2560]{0:T(1024)S(1)}, u32[]{:S(2)}) copy-start(f32[2560]{0:T(1024)S(1)} %convert_element_type.190) | copy-start | bytes 30724
  847.8 250.4 %all-gather.26.cloned.1.call-start = ((), (), s32[]{:S(2)}) async-start(), calls=%async_computation.22 | async-start | bytes 9584640 | tf_op jit(solution)/shard_map/all_gather | solution.py:192
  848.5 306.4 %all-gather.28.cloned.1.call-start = ((), (), s32[]{:S(2)}) async-start(), calls=%async_computation.23 | async-start | bytes 9584640 | tf_op jit(solution)/shard_map/all_gather | solution.py:193
  849.1 463.9 %reduce-scatter.23.cloned.1.call-start = ((), (), s32[]{:S(2)}) async-start(), calls=%async_computation.24 | async-start | bytes 9830400 | tf_op jit(solution)/shard_map/reduce_scatter | solution.py:134
  1175.5 285.6 %all-gather.30.cloned.1.call-start = ((), (), s32[]{:S(2)}) async-start(), calls=%async_computation.25 | async-start | bytes 9830400 | tf_op jit(solution)/shard_map/all_gather | solution.py:143
  1319.4 347.5 %reduce-scatter.25.cloned.1.call-start = ((), (), s32[]{:S(2)}) async-start(), calls=%async_computation.26 | async-start | bytes 9830400 | tf_op jit(solution)/shard_map/reduce_scatter | solution.py:285
  1532.3 288.4 %all-gather.32.cloned.1.call-start = ((), (), s32[]{:S(2)}) async-start(), calls=%async_computation.27 | async-start | bytes 9830400 | tf_op jit(solution)/shard_map/all_gather | solution.py:143
  1679.0 725.3 %reduce-scatter.47.cloned.1.call-start = ((), (), s32[]{:S(2)}) async-start(), calls=%async_computation.38 | async-start | bytes 491520
  2301.0 107.0 %reduce-scatter.45.cloned.1.call-start = ((), (), s32[]{:S(2)}) async-start(), calls=%async_computation.37 | async-start | bytes 983040
  2307.0 112.0 %reduce-scatter.43.cloned.1.call-start = ((), (), s32[]{:S(2)}) async-start(), calls=%async_computation.36 | async-start | bytes 2949120
  2317.2 152.1 %reduce-scatter.41.cloned.1.call-start = ((), (), s32[]{:S(2)}) async-start(), calls=%async_computation.35 | async-start | bytes 9584640 | tf_op jit(solution)/shard_map/reduce_scatter | solution.py:281
  2338.1 207.2 %reduce-scatter.37.cloned.1.call-start = ((), (), s32[]{:S(2)}) async-start(), calls=%async_computation.33 | async-start | bytes 9584640 | tf_op jit(solution)/shard_map/reduce_scatter | solution.py:275
  2358.6 262.5 %reduce-scatter.39.cloned.1.call-start = ((), (), s32[]{:S(2)}) async-start(), calls=%async_computation.34 | async-start | bytes 9584640 | tf_op jit(solution)/shard_map/reduce_scatter | solution.py:278
  2379.3 279.9 %reduce-scatter.33.cloned.1.call-start = ((), (), s32[]{:S(2)}) async-start(), calls=%async_computation.31 | async-start | bytes 737280 | tf_op jit(solution)/shard_map/reduce_scatter | solution.py:335
  2384.9 317.0 %reduce-scatter.31.cloned.1.call-start = ((), (), s32[]{:S(2)}) async-start(), calls=%async_computation.30 | async-start | bytes 1769472 | tf_op jit(solution)/shard_map/reduce_scatter | solution.py:332
  2392.2 369.6 %reduce-scatter.35.cloned.1.call-start = ((), (), s32[]{:S(2)}) async-start(), calls=%async_computation.32 | async-start | bytes 3686400 | tf_op jit(solution)/shard_map/reduce_scatter | solution.py:338
  2402.4 461.5 %reduce-scatter.29.cloned.1.call-start = ((), (), s32[]{:S(2)}) async-start(), calls=%async_computation.29 | async-start | bytes 4055040 | tf_op jit(solution)/shard_map/reduce_scatter | solution.py:372
  2417.5 574.9 %reduce-scatter.27.cloned.1.call-start = ((), (), s32[]{:S(2)}) async-start(), calls=%async_computation.28 | async-start | bytes 8110080 | tf_op jit(solution)/shard_map/reduce_scatter | solution.py:371
  2472.0 231.6 %copy-start.20 = (bf16[384,768]{0,1:T(8,128)(2,1)S(1)}, bf16[384,768]{0,1:T(8,128)(2,1)}, u32[]{:S(2)}) copy-start(bf16[384,768]{0,1:T(8,128)(2,1)} %copy-done.19) | copy-start | bytes 1769476
  2472.0 231.6 %copy-start.51 = (f32[384]{0:T(512)S(1)}, f32[384]{0:T(512)}, u32[]{:S(2)}) copy-start(f32[384]{0:T(512)} %copy-done.50) | copy-start | bytes 4612
  2472.0 231.6 %copy-start.53 = (f32[384]{0:T(512)S(1)}, f32[384]{0:T(512)}, u32[]{:S(2)}) copy-start(f32[384]{0:T(512)} %copy-done.52) | copy-start | bytes 4612
  (108 other events, 594.6 us)
Sparse Core Ops, SparseCore 0:
  10.9 63.9 all-gather.13
  77.1 139.8 all-gather.11
  218.8 23.9 all-gather.15
  245.6 56.0 all-gather.17
  303.4 31.6 all-gather.19
  707.2 135.1 reduce-scatter.20
  844.3 55.4 all-gather.23
  901.9 141.0 all-gather.21
  1044.9 53.1 all-gather.25
  1099.9 54.9 all-gather.27
  1175.6 137.2 reduce-scatter.22
  1319.5 141.5 all-gather.29
  1532.4 134.4 reduce-scatter.24
  1679.1 141.5 all-gather.31
  2301.1 18.7 reduce-scatter.46
  2322.8 21.5 reduce-scatter.44
  2346.6 47.3 reduce-scatter.42
  2397.8 71.4 reduce-scatter.40
  2473.2 72.0 reduce-scatter.36
  2549.1 72.0 reduce-scatter.38
  2624.6 34.5 reduce-scatter.32
  2663.4 38.4 reduce-scatter.30
  2705.7 47.4 reduce-scatter.34
  2759.9 103.9 reduce-scatter.28
  2871.1 121.2 reduce-scatter.26
where the time goes:
time: 3020 us; the launch traced here: 3000 us
  waiting for transfers between devices  1600 us (53%)
  matrix products  686 us (23%)
  local copies, waits for them, and re-layouts  386 us (13%)
  blocking collectives  142 us (5%)
  other arithmetic  123 us (4%)
  loops' own time  42.7 us (1%)
    all_gather x3, waiting for transfers between devices, token_rows(): return lax.all_gather(values, 'row', axis=0, tiled=True)  427 us
    dot_general x98, matrix products, dot_trans_right(): lax.dot_general(left_op, right_op, (((1,), (1,)), ((), ())), preferred_el...  294 us
    reduce_scatter x2, waiting for transfers between devices, partial_rows(): lax.psum_scatter(dot_plain(left_operand_rows, right_full).astype(jnp.bflo...  222 us
    dot_general x68, matrix products, dot_plain(): return jnp.dot(left_op, right_op, preferred_element_type=jnp.float32)  211 us
    dot_general x68, matrix products, dot_trans_left(): lax.dot_general(left_op, right_op, (((0,), (0,)), ((), ())), preferred_el...  181 us
    all_gather x1, waiting for transfers between devices, body(): normed_all = lax.all_gather(normed_b, 'row', axis=0, tiled=True)  142 us
    reduce_scatter x1, waiting for transfers between devices, body(): lax.psum_scatter((dot_trans_right(gate_grad, gate_full) + dot_trans_right...  135 us
    reduce_scatter x1, waiting for transfers between devices, body(): lax.psum_scatter(qd_wg, ('row', 'col'), scatter_dimension=0, tiled=True)  129 us
  transfers between devices with their start and end apart: 25, of which 20 were waited for; matrix products, arithmetic and copies ran while one was open for 20% of the time, Pallas kernels for 0%

commit v1 on v0

v1 whole, which is shorter than its diff:
```python
import functools
import math

import jax
import jax.numpy as jnp
from jax import lax
from jax.experimental import pallas as pl
from jax.experimental.pallas import tpu as pltpu
from jax.sharding import PartitionSpec as P

NOPE = 64
ROPE = 32
VDIM = 64
KV_RANK = 256
CONTS = 4
HEAD = 128

EPS = 1e-05
RES = 1.4 / math.sqrt(62.0)
BASE = 10000.0
SCALE = (NOPE + ROPE) ** (-0.5)
LOG2E = math.log2(math.e)
HIDE = -1e30
BF = jnp.bfloat16
F32 = jnp.float32


def dot_plain(left_op, right_op):
    return jnp.dot(left_op, right_op, preferred_element_type=F32)


def dot_dims(left_op, right_op, left_dims, right_dims):
    return lax.dot_general(
        left_op, right_op, ((left_dims, right_dims), ((), ())), preferred_element_type=F32
    )


def dot_trans_left(left_op, right_op):
    return dot_dims(left_op, right_op, (0,), (0,))


def dot_trans_right(left_op, right_op):
    return dot_dims(left_op, right_op, (1,), (1,))


def root_norm(values, gain):
    unit_rows = values * lax.rsqrt(jnp.mean(values * values, axis=-1, keepdims=True) + EPS)
    return (unit_rows * gain, unit_rows)


def norm_back(grad_rows, unit_rows, values, gain):
    factor = lax.rsqrt(jnp.mean(values * values, axis=-1, keepdims=True) + EPS)
    scaled = grad_rows * gain
    value_grad = factor * (
        scaled - unit_rows * jnp.mean(scaled * unit_rows, axis=-1, keepdims=True)
    )
    return (value_grad, jnp.sum(grad_rows * unit_rows, axis=0))


def rotary(segments):
    length = segments.shape[0]
    indices = jnp.arange(length, dtype=jnp.int32)
    labels = jnp.arange(CONTS + 1, dtype=jnp.int32)
    member = (segments[:, None] == labels[None, :]).astype(jnp.int32)
    counts = jnp.sum(member, axis=0)
    starts = jnp.cumsum(counts) - counts
    first_at = jnp.sum(member * starts[None, :], axis=1)
    places = jnp.where(segments == 0, indices, counts[0] + indices - first_at).astype(F32)
    freqs = BASE ** (-jnp.arange(ROPE // 2, dtype=F32) * 2.0 / ROPE)
    angles = places[:, None] * freqs[None, :]
    return (jnp.cos(angles), jnp.sin(angles))


def rotate(values, cosine, sine):
    half = values.shape[-1] // 2
    first_half = values[..., :half]
    second_half = values[..., half:]
    return jnp.concatenate(
        [first_half * cosine - second_half * sine, second_half * cosine + first_half * sine],
        axis=-1,
    )


def head_weights(weights_ref, query_rows):
    block = weights_ref[0]
    col_total = block.shape[0]
    query_w = block[:, :query_rows, :].reshape(col_total * query_rows, HEAD)
    latent_w = block[:, query_rows:, :].reshape(-1, HEAD)
    return (query_w, latent_w)


def head_vectors(weights_ref, query_t_ref, latent_ref, rope_ref, cos_ref, sin_ref, query_rows):
    query_w, latent_w = head_weights(weights_ref, query_rows)
    half = ROPE // 2
    proj_t = dot_plain(query_w.T, query_t_ref[...])
    first, second = proj_t[NOPE : NOPE + half], proj_t[NOPE + half : NOPE + ROPE]
    cosine, sine = cos_ref[...], sin_ref[...]
    query_t = jnp.concatenate(
        [
            proj_t[:NOPE],
            first * cosine - second * sine,
            second * cosine + first * sine,
            proj_t[NOPE + ROPE :],
        ],
        axis=0,
    ).astype(BF)
    both = dot_plain(latent_ref[...], latent_w).astype(BF)
    lane = lax.broadcasted_iota(jnp.int32, both.shape, 1)
    keys = jnp.where(lane < NOPE, both, rope_ref[...])
    return (query_w, latent_w, query_t, keys, both)


def attend_kernel(
    query_rows, tile, weights_ref, query_t_ref, latent_ref, rope_ref, cos_ref, sin_ref, bias_ref,
    mixed_ref, lse_ref, scores_ref,
):
    _, _, query_t, keys, both = head_vectors(
        weights_ref, query_t_ref, latent_ref, rope_ref, cos_ref, sin_ref, query_rows
    )
    values_t = both.T[NOPE:]
    length = keys.shape[0]
    top = None
    for begin in range(0, length, tile):
        part = dot_plain(keys[begin : begin + tile], query_t) * (SCALE * LOG2E)
        part = part + bias_ref[begin : begin + tile, :]
        scores_ref[begin : begin + tile, :] = part
        tile_top = jnp.max(part, axis=0, keepdims=True)
        top = tile_top if top is None else jnp.maximum(top, tile_top)
    total, out_t = None, None
    for begin in range(0, length, tile):
        expo = jnp.exp2(scores_ref[begin : begin + tile, :] - top)
        tile_sum = jnp.sum(expo, axis=0, keepdims=True)
        term = dot_plain(values_t[:, begin : begin + tile], expo.astype(BF))
        total = tile_sum if total is None else total + tile_sum
        out_t = term if out_t is None else out_t + term
    mixed_ref[...] = (out_t / total).astype(BF)
    lse_ref[0] = top + jnp.log2(total)


def attend_back_kernel(
    query_rows, tile, weights_ref, query_t_ref, latent_ref, latent_t_ref, rope_ref, cos_ref,
    sin_ref, bias_ref, mixed_ref, grad_ref, lse_ref,
    weights_grad_ref, query_grad_ref, latent_grad_ref, rope_grad_ref,
    query_acc, latent_acc, rope_acc, both_scr,
):
    head = pl.program_id(0)
    query_w, latent_w, query_t, keys, both = head_vectors(
        weights_ref, query_t_ref, latent_ref, rope_ref, cos_ref, sin_ref, query_rows
    )

    @pl.when(head == 0)
    def _():
        query_acc[...] = jnp.zeros_like(query_acc)
        latent_acc[...] = jnp.zeros_like(latent_acc)
        rope_acc[...] = jnp.zeros_like(rope_acc)

    keys_t = keys.T
    query = query_t.T
    grad_t = grad_ref[...]
    delta = jnp.sum(
        grad_t.astype(F32) * mixed_ref[...].astype(F32), axis=0, keepdims=True
    )
    grad_pad_t = jnp.concatenate([jnp.zeros_like(grad_t), grad_t], axis=0)
    grad_pad = grad_pad_t.T
    lse = lse_ref[0]
    length = keys.shape[0]
    query_back_t = None
    for begin in range(0, length, tile):
        rows = slice(begin, begin + tile)
        scores = dot_plain(keys[rows], query_t) * (SCALE * LOG2E)
        probs = jnp.exp2(scores + bias_ref[rows, :] - lse)
        prob_grad = dot_plain(both[rows], grad_pad_t)
        score_grad = (probs * (prob_grad - delta)).astype(BF)
        term = dot_plain(keys_t[:, rows], score_grad)
        query_back_t = term if query_back_t is None else query_back_t + term
        key_back = dot_plain(score_grad, query) * SCALE
        value_back = dot_plain(probs.astype(BF), grad_pad)
        lane = lax.broadcasted_iota(jnp.int32, key_back.shape, 1)
        rope_acc[rows, :] += key_back
        both_scr[rows, :] = jnp.where(lane < NOPE, key_back, value_back).astype(BF)
    query_back_t = query_back_t * SCALE
    half = ROPE // 2
    first, second = query_back_t[NOPE : NOPE + half], query_back_t[NOPE + half : NOPE + ROPE]
    cosine, sine = cos_ref[...], sin_ref[...]
    query_back_t = jnp.concatenate(
        [
            query_back_t[:NOPE],
            first * cosine + second * sine,
            second * cosine - first * sine,
            jnp.zeros_like(query_back_t[NOPE + ROPE :]),
        ],
        axis=0,
    ).astype(BF)
    both_back = both_scr[...]
    query_acc[...] += dot_plain(query_w, query_back_t)
    latent_acc[...] += dot_trans_right(both_back, latent_w)
    query_wg = dot_trans_right(query_t_ref[...], query_back_t)
    latent_wg = dot_plain(latent_t_ref[...], both_back)
    col_total = weights_ref.shape[1]
    weights_grad_ref[0, :, :query_rows, :] = query_wg.astype(BF).reshape(col_total, query_rows, HEAD)
    weights_grad_ref[0, :, query_rows:, :] = latent_wg.astype(BF).reshape(col_total, -1, HEAD)

    @pl.when(head == pl.num_programs(0) - 1)
    def _():
        query_grad_ref[...] = query_acc[...]
        latent_grad_ref[...] = latent_acc[...].astype(BF)
        rope_grad_ref[...] = rope_acc[...].astype(BF)


def whole(shape):
    return pl.BlockSpec(shape, lambda head: (0,) * len(shape))


def attend(weights, query_t, latent, rope, cos_t, sin_t, bias_t, query_rows):
    row_total, col_total, pack_rows, pack_cols = weights.shape
    here = pack_cols // HEAD
    heads = row_total * here
    length, local = bias_t.shape
    tile = math.gcd(length, 256)
    return pl.pallas_call(
        functools.partial(attend_kernel, query_rows, tile),
        grid=(heads,),
        in_specs=[
            pl.BlockSpec(
                (1, col_total, pack_rows, HEAD), lambda head: (head // here, 0, 0, head % here)
            ),
            whole(query_t.shape),
            whole(latent.shape),
            whole(rope.shape),
            whole(cos_t.shape),
            whole(sin_t.shape),
            whole(bias_t.shape),
        ],
        out_specs=[
            pl.BlockSpec((VDIM, local), lambda head: (head, 0)),
            pl.BlockSpec((1, 1, local), lambda head: (head, 0, 0)),
        ],
        out_shape=[
            jax.ShapeDtypeStruct((heads * VDIM, local), BF),
            jax.ShapeDtypeStruct((heads, 1, local), F32),
        ],
        scratch_shapes=[pltpu.VMEM((length, local), F32)],
        compiler_params=pltpu.CompilerParams(
            dimension_semantics=("arbitrary",), vmem_limit_bytes=48 * 1024 * 1024
        ),
        cost_estimate=pl.CostEstimate(
            flops=heads * 2 * local * length * 512,
            bytes_accessed=weights.size * 2,
            transcendentals=heads * local * length,
        ),
        name="attend",
    )(weights, query_t, latent, rope, cos_t, sin_t, bias_t)


def attend_back(
    weights, query_t, latent, latent_t, rope, cos_t, sin_t, bias_t, mixed_t, grad_t, lse, query_rows
):
    row_total, col_total, pack_rows, pack_cols = weights.shape
    here = pack_cols // HEAD
    heads = row_total * here
    length, local = bias_t.shape
    tile = math.gcd(length, 256)
    pack_spec = pl.BlockSpec(
        (1, col_total, pack_rows, HEAD), lambda head: (head // here, 0, 0, head % here)
    )
    return pl.pallas_call(
        functools.partial(attend_back_kernel, query_rows, tile),
        grid=(heads,),
        in_specs=[
            pack_spec,
            whole(query_t.shape),
            whole(latent.shape),
            whole(latent_t.shape),
            whole(rope.shape),
            whole(cos_t.shape),
            whole(sin_t.shape),
            whole(bias_t.shape),
            pl.BlockSpec((VDIM, local), lambda head: (head, 0)),
            pl.BlockSpec((VDIM, local), lambda head: (head, 0)),
            pl.BlockSpec((1, 1, local), lambda head: (head, 0, 0)),
        ],
        out_specs=[
            pack_spec,
            whole(query_t.shape),
            whole(latent.shape),
            whole(rope.shape),
        ],
        out_shape=[
            jax.ShapeDtypeStruct(weights.shape, BF),
            jax.ShapeDtypeStruct(query_t.shape, F32),
            jax.ShapeDtypeStruct(latent.shape, BF),
            jax.ShapeDtypeStruct(rope.shape, BF),
        ],
        scratch_shapes=[
            pltpu.VMEM(query_t.shape, F32),
            pltpu.VMEM(latent.shape, F32),
            pltpu.VMEM(rope.shape, F32),
            pltpu.VMEM((length, HEAD), BF),
        ],
        compiler_params=pltpu.CompilerParams(
            dimension_semantics=("arbitrary",), vmem_limit_bytes=48 * 1024 * 1024
        ),
        cost_estimate=pl.CostEstimate(
            flops=heads * 2 * local * length * 1280,
            bytes_accessed=weights.size * 4,
            transcendentals=heads * local * length,
        ),
        name="attend_back",
    )(weights, query_t, latent, latent_t, rope, cos_t, sin_t, bias_t, mixed_t, grad_t, lse)


def partial_rows(product):
    return lax.psum_scatter(
        product.astype(BF), "row", scatter_dimension=0, tiled=True
    ).astype(F32)


def token_rows(values):
    return lax.all_gather(values, "row", axis=0, tiled=True)


def pad_to(values, width):
    return jnp.pad(values, ((0, 0), (0, width - values.shape[1])))


def body(
    inputs,
    segments,
    valid_mask,
    teacher,
    cotangent,
    query_down,
    latent_down,
    query_up,
    latent_up,
    output_weight,
    gate_weight,
    up_weight,
    down_weight,
    attn_gain,
    query_gain,
    latent_gain,
    mlp_gain,
):
    both_axes = ("row", "col")
    row_total = lax.axis_size("row")
    col_total = lax.axis_size("col")
    devices = row_total * col_total
    row_rank = lax.axis_index("row")
    local_rows, width = inputs.shape
    length = segments.shape[0]
    q_rank = query_down.shape[1]
    kv_wide = latent_down.shape[1]
    lat_wide = q_rank + kv_wide
    down_rows = query_down.shape[0]
    q_part, kv_part = query_gain.shape[0], latent_gain.shape[0]
    heads_here = output_weight.shape[0] // VDIM
    query_rows = query_up.shape[0]
    offset = row_rank * local_rows

    count = jnp.sum(valid_mask)
    count_parts = jnp.stack([count // 256, count % 256]).astype(F32)
    misc = jnp.concatenate(
        [query_gain.astype(F32), latent_gain.astype(F32), count_parts]
    )
    misc = jnp.pad(misc, (0, down_rows - misc.shape[0])).astype(BF)
    down_pack = jnp.concatenate(
        [query_down, latent_down, attn_gain[:, None], mlp_gain[:, None], misc[:, None]], axis=1
    )
    pack_wide = -(-(lat_wide + 3) // 128) * 128
    down_all = lax.all_gather(pad_to(down_pack, pack_wide), both_axes, axis=0, tiled=True)
    down_w = down_all[:, :lat_wide]
    attn_g = down_all[:, lat_wide].astype(F32)
    mlp_g = down_all[:, lat_wide + 1].astype(F32)
    misc_all = down_all[:, lat_wide + 2].astype(F32).reshape(devices, down_rows)
    query_g = misc_all[:, :q_part].reshape(-1)
    latent_g = misc_all[:, q_part : q_part + kv_part].reshape(-1)
    counts = jnp.sum(misc_all[:, q_part + kv_part : q_part + kv_part + 2], axis=0)
    valid_total = counts[0] * 256.0 + counts[1]

    query_pack = jnp.pad(
        query_up.reshape(query_rows, heads_here, NOPE + ROPE),
        ((0, 0), (0, 0), (0, HEAD - NOPE - ROPE)),
    ).reshape(query_rows, heads_here * HEAD)
    up_pack = jnp.concatenate([query_pack, latent_up], axis=0)
    pack_rows = up_pack.shape[0]
    head_w = lax.all_gather(up_pack, both_axes, axis=0, tiled=True).reshape(
        row_total, col_total, pack_rows, heads_here * HEAD
    )
    out_all = lax.all_gather(output_weight.T, both_axes, axis=0, tiled=True).reshape(
        row_total, width, heads_here * VDIM
    )
    gate_full, up_full, down_t = (
        lax.all_gather(gate_weight, "col", axis=0, tiled=True),
        lax.all_gather(up_weight, "col", axis=0, tiled=True),
        lax.all_gather(down_weight.T, "col", axis=0, tiled=True),
    )

    cosine, sine = rotary(segments)
    cos_here = lax.dynamic_slice_in_dim(cosine, offset, local_rows, 0)
    sin_here = lax.dynamic_slice_in_dim(sine, offset, local_rows, 0)
    tokens_f = inputs.astype(F32)
    normed, normed_unit = root_norm(tokens_f, attn_g)
    normed_b = normed.astype(BF)
    lat = dot_plain(normed_b, down_w)
    query_lat, kv_lat = lat[:, :q_rank], lat[:, q_rank:]
    query_norm, query_unit = root_norm(query_lat, query_g)
    kv_norm, kv_unit = root_norm(kv_lat[:, :KV_RANK], latent_g)
    key_rope = rotate(kv_lat[:, KV_RANK:], cos_here, sin_here)
    query_nb = query_norm.astype(BF)
    latent_pack = jnp.concatenate(
        [
            kv_norm,
            jnp.zeros((local_rows, NOPE), F32),
            key_rope,
            jnp.zeros((local_rows, HEAD - NOPE - ROPE), F32),
        ],
        axis=1,
    ).astype(BF)
    latent_all = token_rows(latent_pack)
    kv_all = latent_all[:, :KV_RANK]
    rope_all = latent_all[:, KV_RANK:]

    query_at = offset + jnp.arange(local_rows, dtype=jnp.int32)
    query_seg = lax.dynamic_slice_in_dim(segments, offset, local_rows, 0)
    key_at = jnp.arange(length, dtype=jnp.int32)
    allowed_t = (key_at[:, None] <= query_at[None, :]) & (
        (segments[:, None] == 0) | (segments[:, None] == query_seg[None, :])
    )
    bias_t = jnp.where(allowed_t, 0.0, HIDE).astype(F32)
    query_t = query_nb.T
    cos_t, sin_t = cos_here.T, sin_here.T
    mixed_t, lse = attend(head_w, query_t, kv_all, rope_all, cos_t, sin_t, bias_t, query_rows)
    mixed_heads = mixed_t.reshape(row_total, heads_here * VDIM, local_rows)
    attn_sum = dot_dims(mixed_heads, out_all, (0, 1), (0, 2))

    residual = tokens_f + RES * attn_sum
    mlp_in, mlp_unit = root_norm(residual, mlp_g)
    mlp_all = token_rows(mlp_in.astype(BF))
    gate_act = dot_plain(mlp_all, gate_full)
    up_act = dot_plain(mlp_all, up_full)
    gate_sig = jax.nn.sigmoid(gate_act)
    silu_val = gate_act * gate_sig
    hidden = (silu_val * up_act).astype(BF)
    outputs = residual + RES * partial_rows(dot_trans_right(hidden, down_t))
    error_val = outputs - teacher.astype(F32)
    weight_v = valid_mask.astype(F32)[:, None]
    total_tokens = local_rows * row_total * col_total
    squared = 0.5 * jnp.sum(weight_v * error_val * error_val)
    out_grad = cotangent.astype(F32) + total_tokens / valid_total * weight_v * error_val
    branch_grad = token_rows((RES * out_grad).astype(BF))
    hidden_grad = dot_plain(branch_grad, down_t)
    gate_grad = (hidden_grad * up_act * gate_sig * (1.0 + gate_act * (1.0 - gate_sig))).astype(BF)
    up_grad = (hidden_grad * silu_val).astype(BF)
    mlp_in_grad = partial_rows(
        dot_trans_right(gate_grad, gate_full) + dot_trans_right(up_grad, up_full)
    )
    gate_wg = dot_trans_left(mlp_all, gate_grad).astype(BF)
    up_wg = dot_trans_left(mlp_all, up_grad).astype(BF)
    down_wg = dot_trans_left(branch_grad, hidden).astype(BF)
    gate_wg, up_wg, down_wg = (
        lax.psum_scatter(gate_wg, "col", scatter_dimension=0, tiled=True).astype(F32),
        lax.psum_scatter(up_wg, "col", scatter_dimension=0, tiled=True).astype(F32),
        lax.psum_scatter(down_wg, "col", scatter_dimension=0, tiled=True).astype(F32).T,
    )
    residual_part, mlp_gain_grad = norm_back(mlp_in_grad, mlp_unit, residual, mlp_g)
    residual_grad = out_grad + residual_part

    attn_grad_in = (RES * residual_grad).astype(BF)
    grad_t = dot_dims(out_all, attn_grad_in, (1,), (1,)).astype(BF)
    out_wg = dot_dims(attn_grad_in, mixed_heads, (0,), (2,)).astype(BF)
    out_wg = jnp.transpose(out_wg, (1, 0, 2)).reshape(row_total * width, heads_here * VDIM)
    out_wg = lax.psum_scatter(out_wg, both_axes, scatter_dimension=0, tiled=True).astype(F32).T
    head_wg, query_back_t, kv_back, rope_back = attend_back(
        head_w, query_t, kv_all, kv_all.T, rope_all, cos_t, sin_t, bias_t, mixed_t,
        grad_t.reshape(mixed_t.shape), lse, query_rows,
    )
    head_wg = lax.psum_scatter(
        head_wg.reshape(devices * pack_rows, heads_here * HEAD),
        both_axes, scatter_dimension=0, tiled=True,
    ).astype(F32)
    qu_wg = head_wg[:query_rows].reshape(query_rows, heads_here, HEAD)[:, :, : NOPE + ROPE]
    qu_wg = qu_wg.reshape(query_rows, heads_here * (NOPE + ROPE))
    kvu_wg = head_wg[query_rows:]
    latent_back = partial_rows(jnp.concatenate([kv_back, rope_back], axis=1))
    kv_norm_grad = latent_back[:, :KV_RANK]
    rope_grad = latent_back[:, KV_RANK + NOPE : KV_RANK + NOPE + ROPE]
    query_norm_grad = query_back_t.T
    query_lat_grad, query_gain_grad = norm_back(query_norm_grad, query_unit, query_lat, query_g)
    kv_lat_part, latent_gain_grad = norm_back(kv_norm_grad, kv_unit, kv_lat[:, :KV_RANK], latent_g)
    lat_grad = jnp.concatenate(
        [query_lat_grad, kv_lat_part, rotate(rope_grad, cos_here, -sin_here)], axis=-1
    ).astype(BF)
    lat_wg = dot_trans_left(normed_b, lat_grad)
    normed_grad = dot_trans_right(lat_grad, down_w)
    input_part, attention_gain_gradient = norm_back(normed_grad, normed_unit, tokens_f, attn_g)
    input_grad = residual_grad + input_part

    loss_high = squared.astype(BF).astype(F32)
    loss_low = squared - loss_high
    misc_grad = jnp.concatenate(
        [
            query_gain_grad.reshape(devices, q_part),
            latent_gain_grad.reshape(devices, kv_part),
            jnp.broadcast_to(loss_high, (devices, 1)),
            jnp.broadcast_to(loss_low, (devices, 1)),
        ],
        axis=1,
    )
    misc_grad = pad_to(misc_grad, down_rows).reshape(devices * down_rows, 1)
    small = jnp.concatenate(
        [lat_wg, attention_gain_gradient[:, None], mlp_gain_grad[:, None], misc_grad], axis=1
    )
    small = lax.psum_scatter(
        pad_to(small, pack_wide), both_axes, scatter_dimension=0, tiled=True
    )
    misc_sum = small[:, lat_wide + 2]
    at = q_part + kv_part
    loss = (misc_sum[at] + misc_sum[at + 1]) / valid_total
    return (
        outputs.astype(BF),
        loss,
        input_grad,
        small[:, :q_rank],
        small[:, q_rank:lat_wide],
        qu_wg,
        kvu_wg,
        out_wg,
        gate_wg,
        up_wg,
        down_wg,
        small[:, lat_wide],
        misc_sum[:q_part],
        misc_sum[q_part : q_part + kv_part],
        small[:, lat_wide + 1],
    )


def solution(mesh):
    in_specs = (
        P(("col", "row"), None),
        P("col"),
        P(("col", "row")),
        P(("col", "row"), None),
        P(("col", "row"), None),
        P(("row", "col"), None),
        P(("row", "col"), None),
        P("col", "row"),
        P("col", "row"),
        P("row", "col"),
        P("col", "row"),
        P("col", "row"),
        P("row", "col"),
        P(("row", "col")),
        P(("row", "col")),
        P(("row", "col")),
        P(("row", "col")),
    )
    out_specs = (
        P(("col", "row"), None),
        P(),
        P(("col", "row"), None),
        P(("row", "col"), None),
        P(("row", "col"), None),
        P("col", "row"),
        P("col", "row"),
        P("row", "col"),
        P("col", "row"),
        P("col", "row"),
        P("row", "col"),
        P(("row", "col")),
        P(("row", "col")),
        P(("row", "col")),
        P(("row", "col")),
    )
    return jax.shard_map(body, mesh=mesh, in_specs=in_specs, out_specs=out_specs, check_vma=False)
```

time: 3020 us -> 2080 us (0.69)
  matrix products: 686 us -> 249 us
  local copies, waits for them, and re-layouts: 386 us -> 108 us
  Pallas kernels: 0 us -> 225 us
  waiting for transfers between devices: 1600 us -> 1410 us
  blocking collectives: 142 us -> 0 us
  other arithmetic: 123 us -> 58.6 us
  loops' own time: 42.7 us -> 0 us
    dot_general x234 -> x15, matrix products: 686 us -> 249 us  [the longest x11 176 us: dot_dims(): lax.dot_general(left_op, right_op, ((left_dims, right_dims), ((), ())), p...]
    pallas_call x0 -> x2, Pallas kernels: none -> 225 us  [the longest x1 161 us: attend_back(): pl.pallas_call(functools.partial(attend_back_kernel, query_rows, tile), g...]
    reduce_scatter x11 -> x7, waiting for transfers between devices: 847 us -> 664 us  [the longest x2 269 us: partial_rows(): lax.psum_scatter(product.astype(BF), 'row', scatter_dimension=0, tiled=True)]
    unnamed x28 -> x20, waiting for transfers between devices: 4.65 us -> 148 us
    all_gather x3, waiting for transfers between devices: 427 us -> 305 us  [token_rows(): return lax.all_gather(values, 'row', axis=0, tiled=True)]
    squeeze x60 -> x0, local copies, waits for them, and re-layouts: 92.9 us -> none  [body(): lax.map(lambda operands: head_forward(operands[0], operands[1], operands[...]
    psum x2 -> x0, blocking collectives: 87.9 us -> none  [the longest x1 47.6 us: body(): lax.psum(jnp.sum(valid_mask), ('row', 'col')).astype(jnp.float32)]
    while x151 -> x0, local copies, waits for them, and re-layouts: 86.2 us -> none
  transfers between devices with their start and end apart: 25 -> 18, of which waited for: 20 -> 16; matrix products, arithmetic and copies ran while one was open for 20% -> 13% of each run, Pallas kernels for 0% -> 3%
where the time goes in v1:
time: 2080 us
  waiting for transfers between devices  1410 us (68%)
  matrix products  249 us (12%)
  Pallas kernels  225 us (11%)
  local copies, waits for them, and re-layouts  108 us (5%)
  other arithmetic  58.6 us (3%)
  between operations  22.2 us (1%)
    all_gather x3, waiting for transfers between devices, token_rows(): return lax.all_gather(values, 'row', axis=0, tiled=True)  305 us
    reduce_scatter x2, waiting for transfers between devices, partial_rows(): lax.psum_scatter(product.astype(BF), 'row', scatter_dimension=0, tiled=True)  269 us
    dot_general x11, matrix products, dot_dims(): lax.dot_general(left_op, right_op, ((left_dims, right_dims), ((), ())), p...  176 us
    pallas_call x1, Pallas kernels, attend_back(): pl.pallas_call(functools.partial(attend_back_kernel, query_rows, tile), g...  161 us
    reduce_scatter x1, waiting for transfers between devices, body(): lax.psum_scatter(out_wg, both_axes, scatter_dimension=0, tiled=True)  153 us
    unnamed x20, waiting for transfers between devices  148 us
    reduce_scatter x1, waiting for transfers between devices, body(): lax.psum_scatter(head_wg.reshape(devices * pack_rows, heads_here * HEAD),...  144 us
    all_gather x1, waiting for transfers between devices, body(): lax.all_gather(up_pack, both_axes, axis=0, tiled=True)  104 us
  transfers between devices with their start and end apart: 18, of which 16 were waited for; matrix products, arithmetic and copies ran while one was open for 13% of the time, Pallas kernels for 3%

profile of v1, /device:TPU:0, one launch (start us, length us, event | category | flops | bytes accessed | tf_op | source)
XLA Modules:
  0.0 2076.7 jit_solution(6462381276413716099)
XLA Ops:
  21.4 65.2 %all-gather.12.cloned.1.call-done = bf16[2560,1152]{1,0:T(8,128)(2,1)} async-done(((bf16[80,1152]{1,0:T(8,128)(2,1)}), bf16[2560,1152]{1,0:T(8,128)(2,1)}) %all-gather.12.cloned.1.call-update) | async-done | bytes 5898256 | tf_op jit(solution)/shard_map/all_gather | solution.py:371
  107.8 19.8 all-gather.14.cloned.1.call-done
  132.6 103.5 %all-gather.10.cloned.1.call-done = bf16[4096,1280]{0,1:T(8,128)(2,1)} async-done(((bf16[128,1280]{0,1:T(8,128)(2,1)}), bf16[4096,1280]{0,1:T(8,128)(2,1)}) %all-gather.10.cloned.1.call-update) | async-done | bytes 10485776 | tf_op jit(solution)/shard_map/all_gather | solution.py:387
  236.2 14.5 copy.85
  253.2 64.3 %attend.1 = (bf16[2560,384]{1,0:T(8,128)(2,1)S(1)}, f32[40,1,384]{2,1,0:T(1,128)S(1)}) custom-call(bf16[4,8,128,1280]{3,2,1,0:T(8,128)(2,1)} %bitcast.98, bf16[768,384]{1,0:T(8,128)(2,1)S(1)} %copy-done.2, bf16[1536,256]{1,0:T(8,128)(2,1)S(1)} %copy.89.latent_ref, bf16[1536,128]{1,0:T(8,128)(2,1)S(1)} %copy.90.rope_ref, f32[16,384]{1,0:T(8,128)S(1)} %copy-done.6, ...), custom_call_target="tpu_custom_call" | custom-call | flops 24159191040 | bytes 10485760 | tf_op jit(solution)/shard_map/attend/pallas_call | solution.py:220
  319.4 16.2 all-gather.16.cloned.1.call-done
  350.5 40.4 %all-gather.20.cloned.1.call-done = bf16[2560,1600]{1,0:T(8,128)(2,1)} async-done(((bf16[320,1600]{1,0:T(8,128)(2,1)}), bf16[2560,1600]{1,0:T(8,128)(2,1)}) %all-gather.20.cloned.1.call-update) | async-done | bytes 8192016 | tf_op jit(solution)/shard_map/all_gather | solution.py:394
  390.9 143.1 %all-gather.18.cloned.1.call-done = bf16[1536,2560]{1,0:T(8,128)(2,1)} async-done(((bf16[384,2560]{1,0:T(8,128)(2,1)}), bf16[1536,2560]{1,0:T(8,128)(2,1)}) %all-gather.18.cloned.1.call-update) | async-done | bytes 7864336 | tf_op jit(solution)/shard_map/all_gather | solution.py:319
  534.0 19.3 fusion.50
  553.3 35.8 %all-gather.22.cloned.1.call-done = bf16[2560,1600]{1,0:T(8,128)(2,1)} async-done(((bf16[320,1600]{1,0:T(8,128)(2,1)}), bf16[2560,1600]{1,0:T(8,128)(2,1)}) %all-gather.22.cloned.1.call-update) | async-done | bytes 8192016 | tf_op jit(solution)/shard_map/all_gather | solution.py:395
  589.1 22.2 %multiply_convert_fusion.2 = (bf16[1536,1600]{0,1:T(8,128)(2,1)}, f32[1536,1600]{0,1:T(8,128)}) fusion(f32[1536,1600]{0,1:T(8,128)} %fusion.50, bf16[1536,2560]{1,0:T(8,128)(2,1)} %all-gather.18.cloned.1.call-done, bf16[2560,1600]{1,0:T(8,128)(2,1)} %all-gather.22.cloned.1.call-done), kind=kOutput, calls=%fused_computation.7 | convolution fusion | flops 12597657600 | bytes 40632320 | tf_op jit(solution)/shard_map/dot_general | solution.py:29
  611.2 34.7 %all-gather.24.cloned.1.call-done = bf16[2560,1600]{1,0:T(8,128)(2,1)} async-done(((bf16[320,1600]{1,0:T(8,128)(2,1)}), bf16[2560,1600]{1,0:T(8,128)(2,1)}) %all-gather.24.cloned.1.call-update) | async-done | bytes 8192016 | tf_op jit(solution)/shard_map/all_gather | solution.py:396
  645.9 20.6 convolution_convert_fusion
  668.7 134.3 %reduce-scatter.14.cloned.1.call-done = bf16[384,2560]{1,0:T(8,128)(2,1)} async-done(((bf16[1536,2560]{1,0:T(8,128)(2,1)}), bf16[384,2560]{1,0:T(8,128)(2,1)}) %reduce-scatter.14.cloned.1.call-update) | async-done | bytes 1966096 | tf_op jit(solution)/shard_map/reduce_scatter | solution.py:313
  809.0 141.7 %all-gather.26.cloned.1.call-done = bf16[1536,2560]{1,0:T(8,128)(2,1)} async-done(((bf16[384,2560]{1,0:T(8,128)(2,1)}), bf16[1536,2560]{1,0:T(8,128)(2,1)}) %all-gather.26.cloned.1.call-update) | async-done | bytes 7864336 | tf_op jit(solution)/shard_map/all_gather | solution.py:319
  950.7 26.1 %multiply_convert_fusion = (bf16[1536,1600]{0,1:T(8,128)(2,1)}, bf16[1536,1600]{0,1:T(8,128)(2,1)}) fusion(f32[1536,1600]{0,1:T(8,128)} %fusion.50, f32[1536,1600]{0,1:T(8,128)} %get-tuple-element.122, bf16[1536,2560]{1,0:T(8,128)(2,1)} %all-gather.26.cloned.1.call-done, bf16[2560,1600]{1,0:T(8,128)(2,1)} %all-gather.24.cloned.1.call-done), kind=kOutput, calls=%fused_computation.5 | convolution fusion | flops 12614860800 | bytes 45547520 | tf_op jit(solution)/shard_map/dot_general | solution.py:29
  976.9 21.9 %fusion.51 = f32[1536,2560]{1,0:T(8,128)} fusion(bf16[1536,1600]{0,1:T(8,128)(2,1)} %get-tuple-element.102, bf16[2560,1600]{1,0:T(8,128)(2,1)} %all-gather.20.cloned.1.call-done), kind=kOutput, calls=%fused_computation.128 | convolution fusion | flops 12582912000 | bytes 28835840 | tf_op jit(solution)/shard_map/dot_general | solution.py:33
  998.7 23.2 %add_convert_fusion = bf16[1536,2560]{1,0:T(8,128)(2,1)} fusion(f32[1536,2560]{1,0:T(8,128)} %fusion.51, bf16[1536,1600]{0,1:T(8,128)(2,1)} %get-tuple-element.101, bf16[2560,1600]{1,0:T(8,128)(2,1)} %all-gather.22.cloned.1.call-done), kind=kOutput, calls=%fused_computation | convolution fusion | flops 12590776320 | bytes 36700160 | tf_op jit(solution)/shard_map/dot_general | solution.py:33
  1022.0 134.6 %reduce-scatter.16.cloned.1.call-done = bf16[384,2560]{1,0:T(8,128)(2,1)} async-done(((bf16[1536,2560]{1,0:T(8,128)(2,1)}), bf16[384,2560]{1,0:T(8,128)(2,1)}) %reduce-scatter.16.cloned.1.call-update) | async-done | bytes 1966096 | tf_op jit(solution)/shard_map/reduce_scatter | solution.py:313
  1168.2 9.8 convert_bitcast_fusion.1
  1185.3 160.8 %attend_back.1 = (bf16[4,8,128,1280]{3,2,1,0:T(8,128)(2,1)}, f32[768,384]{1,0:T(8,128)S(1)}, bf16[1536,256]{1,0:T(8,128)(2,1)S(1)}, bf16[1536,128]{1,0:T(8,128)(2,1)S(1)}) custom-call(bf16[4,8,128,1280]{3,2,1,0:T(8,128)(2,1)} %bitcast.99, bf16[768,384]{1,0:T(8,128)(2,1)S(1)} %copy-done.3, bf16[1536,256]{1,0:T(8,128)(2,1)S(1)} %copy.89.latent_ref, ...), custom_call_target="tpu_custom_call" | custom-call | flops 60397977600 | bytes 20971520 | tf_op jit(solution)/shard_map/attend_back/pallas_call | solution.py:266
  1347.3 20.5 convolution_convert_fusion.2
  1367.9 21.1 %convolution_convert_fusion.3 = bf16[2560,1600]{1,0:T(8,128)(2,1)} fusion(bf16[1536,2560]{1,0:T(8,128)(2,1)} %all-gather.18.cloned.1.call-done, bf16[1536,1600]{0,1:T(8,128)(2,1)} %get-tuple-element.102), kind=kOutput, calls=%fused_computation.4 | convolution fusion | flops 12587008000 | bytes 20971520 | tf_op jit(solution)/shard_map/dot_general | solution.py:33
  1389.1 22.4 %convolution_convert_fusion.1 = bf16[2560,1600]{1,0:T(8,128)(2,1)} fusion(bf16[1536,2560]{1,0:T(8,128)(2,1)} %all-gather.26.cloned.1.call-done, bf16[1536,1600]{0,1:T(8,128)(2,1)} %get-tuple-element.121), kind=kOutput, calls=%fused_computation.2 | convolution fusion | flops 12587008000 | bytes 20971520 | tf_op jit(solution)/shard_map/dot_general | solution.py:33
  1435.3 26.8 %concatenate.34 = f32[2560,1059]{0,1:T(8,128)} concatenate(f32[2560,1056]{0,1:T(8,128)} %fusion.30, f32[2560,1]{0,1:T(1,128)S(1)} %broadcast_in_dim.33, f32[2560,1]{0,1:T(1,128)S(1)} %broadcast_in_dim.34, f32[2560,1]{0,1:T(1,128)S(1)} %reshape.204), dimensions={1} | concatenate | bytes 21688320 | tf_op jit(solution)/shard_map/concatenate | solution.py:511
  1462.1 13.5 copy.116
  1486.6 12.1 convolution_convert_fusion.4
  1501.5 25.4 %reduce-scatter.22.cloned.1.call-done = bf16[320,1600]{1,0:T(8,128)(2,1)} async-done(((bf16[2560,1600]{1,0:T(8,128)(2,1)}), bf16[320,1600]{1,0:T(8,128)(2,1)}) %reduce-scatter.22.cloned.1.call-update) | async-done | bytes 1024016 | tf_op jit(solution)/shard_map/reduce_scatter | solution.py:462
  1529.6 72.7 %reduce-scatter.26.cloned.1.call-done = bf16[320,1600]{1,0:T(8,128)(2,1)} async-done(((bf16[2560,1600]{1,0:T(8,128)(2,1)}), bf16[320,1600]{1,0:T(8,128)(2,1)}) %reduce-scatter.26.cloned.1.call-update) | async-done | bytes 1024016 | tf_op jit(solution)/shard_map/reduce_scatter | solution.py:464
  1611.2 145.1 %reduce-scatter.30.cloned.1.call-done = f32[80,1152]{1,0:T(8,128)} async-done(((f32[2560,1152]{1,0:T(8,128)}), f32[80,1152]{1,0:T(8,128)}) %reduce-scatter.30.cloned.1.call-update) | async-done | bytes 368656
  1767.1 143.5 %reduce-scatter.18.cloned.1.call-done = bf16[128,1280]{1,0:T(8,128)(2,1)} async-done(((bf16[4096,1280]{1,0:T(8,128)(2,1)}), bf16[128,1280]{1,0:T(8,128)(2,1)}) %reduce-scatter.18.cloned.1.call-update) | async-done | bytes 327696 | tf_op jit(solution)/shard_map/reduce_scatter | solution.py:478
  1913.6 153.0 %reduce-scatter.20.cloned.1.call-done = bf16[320,640]{1,0:T(8,128)(2,1)} async-done(((bf16[10240,640]{1,0:T(8,128)(2,1)}), bf16[320,640]{1,0:T(8,128)(2,1)}) %reduce-scatter.20.cloned.1.call-update) | async-done | bytes 409616 | tf_op jit(solution)/shard_map/reduce_scatter | solution.py:473
  (235 shorter events, 146.3 us)
Async XLA Ops:
  7.2 83.2 %copy-start.17 = (bf16[384,2560]{1,0:T(8,128)(2,1)S(1)}, bf16[384,2560]{1,0:T(8,128)(2,1)}, u32[]{:S(2)}) copy-start(bf16[384,2560]{1,0:T(8,128)(2,1)} %param.17) | copy-start | bytes 5898244
  7.2 79.4 %all-gather.12.cloned.1.call-start = ((), (), s32[]{:S(2)}) async-start(), calls=%async_computation.10 | async-start | bytes 6082560 | tf_op jit(solution)/shard_map/all_gather | solution.py:371
  16.1 111.5 %all-gather.14.cloned.1.call-start = ((), (), s32[]{:S(2)}) async-start(), calls=%async_computation.11 | async-start | bytes 1474560 | tf_op jit(solution)/shard_map/all_gather | solution.py:319
  20.0 76.3 %copy-start.42 = (f32[384]{0:T(512)}, f32[384]{0:T(512)S(1)}, u32[]{:S(2)}) copy-start(f32[384]{0:T(512)S(1)} %add_rsqrt_fusion.3) | copy-start | bytes 4612
  21.4 80.4 %copy-start.25 = (f32[1536,16]{0,1:T(8,128)}, f32[1536,16]{0,1:T(8,128)S(1)}, u32[]{:S(2)}) copy-start(f32[1536,16]{0,1:T(8,128)S(1)} %broadcast_multiply_fusion) | copy-start | bytes 294916
  90.4 8.3 copy-start.32
  98.3 137.8 %all-gather.10.cloned.1.call-start = ((), (), s32[]{:S(2)}) async-start(), calls=%async_computation.9 | async-start | bytes 10813440 | tf_op jit(solution)/shard_map/all_gather | solution.py:387
  99.9 235.8 %all-gather.16.cloned.1.call-start = ((), (), s32[]{:S(2)}) async-start(), calls=%async_computation.12 | async-start | bytes 13516800 | tf_op jit(solution)/shard_map/all_gather | solution.py:390
  100.4 290.5 %all-gather.20.cloned.1.call-start = ((), (), s32[]{:S(2)}) async-start(), calls=%async_computation.14 | async-start | bytes 9584640 | tf_op jit(solution)/shard_map/all_gather | solution.py:394
  101.0 433.0 %all-gather.18.cloned.1.call-start = ((), (), s32[]{:S(2)}) async-start(), calls=%async_computation.13 | async-start | bytes 9830400 | tf_op jit(solution)/shard_map/all_gather | solution.py:319
  103.2 147.5 %copy-start = (f32[1536,384]{1,0:T(8,128)}, f32[1536,384]{1,0:T(8,128)S(1)}, u32[]{:S(2)}) copy-start(f32[1536,384]{1,0:T(8,128)S(1)} %fusion.25.bias_ref) | copy-start | bytes 7077892
  103.3 24.4 %copy-start.33 = (f32[768]{0:T(1024)}, f32[768]{0:T(1024)S(1)}, u32[]{:S(2)}) copy-start(f32[768]{0:T(1024)S(1)} %mul.309) | copy-start | bytes 9220
  105.5 22.1 %copy-start.38 = (f32[384]{0:T(512)}, f32[384]{0:T(512)S(1)}, u32[]{:S(2)}) copy-start(f32[384]{0:T(512)S(1)} %add_rsqrt_fusion.2) | copy-start | bytes 4612
  335.6 11.4 copy-start.27
  348.8 240.3 %all-gather.22.cloned.1.call-start = ((), (), s32[]{:S(2)}) async-start(), calls=%async_computation.15 | async-start | bytes 9584640 | tf_op jit(solution)/shard_map/all_gather | solution.py:395
  349.5 296.4 %all-gather.24.cloned.1.call-start = ((), (), s32[]{:S(2)}) async-start(), calls=%async_computation.16 | async-start | bytes 9584640 | tf_op jit(solution)/shard_map/all_gather | solution.py:396
  350.3 452.7 %reduce-scatter.14.cloned.1.call-start = ((), (), s32[]{:S(2)}) async-start(), calls=%async_computation.17 | async-start | bytes 9830400 | tf_op jit(solution)/shard_map/reduce_scatter | solution.py:313
  666.6 136.4 %copy-start.15 = (bf16[384,2560]{1,0:T(8,128)(2,1)S(1)}, bf16[384,2560]{1,0:T(8,128)(2,1)}, u32[]{:S(2)}) copy-start(bf16[384,2560]{1,0:T(8,128)(2,1)} %param.20) | copy-start | bytes 5898244
  666.6 284.1 %all-gather.26.cloned.1.call-start = ((), (), s32[]{:S(2)}) async-start(), calls=%async_computation.18 | async-start | bytes 9830400 | tf_op jit(solution)/shard_map/all_gather | solution.py:319
  809.0 347.7 %reduce-scatter.16.cloned.1.call-start = ((), (), s32[]{:S(2)}) async-start(), calls=%async_computation.19 | async-start | bytes 9830400 | tf_op jit(solution)/shard_map/reduce_scatter | solution.py:313
  1022.0 134.7 %copy-start.28 = (f32[2560]{0:T(1024)S(1)}, f32[2560]{0:T(1024)}, u32[]{:S(2)}) copy-start(f32[2560]{0:T(1024)} %get-tuple-element.91) | copy-start | bytes 30724
  1022.0 134.7 %copy-start.41 = (f32[384]{0:T(512)S(1)}, f32[384]{0:T(512)}, u32[]{:S(2)}) copy-start(f32[384]{0:T(512)} %copy-done.40) | copy-start | bytes 4612
  1022.0 134.7 %copy-start.46 = (f32[384]{0:T(512)S(1)}, f32[384]{0:T(512)}, u32[]{:S(2)}) copy-start(f32[384]{0:T(512)} %get-tuple-element.115) | copy-start | bytes 4612
  1022.0 394.0 %reduce-scatter.28.cloned.1.call-start = ((), (), s32[]{:S(2)}) async-start(), calls=%async_computation.25 | async-start | bytes 1474560
  1347.3 151.5 %reduce-scatter.24.cloned.1.call-start = ((), (), s32[]{:S(2)}) async-start(), calls=%async_computation.23 | async-start | bytes 9584640 | tf_op jit(solution)/shard_map/reduce_scatter | solution.py:463
  1367.9 159.0 %reduce-scatter.22.cloned.1.call-start = ((), (), s32[]{:S(2)}) async-start(), calls=%async_computation.22 | async-start | bytes 9584640 | tf_op jit(solution)/shard_map/reduce_scatter | solution.py:462
  1389.0 213.2 %reduce-scatter.26.cloned.1.call-start = ((), (), s32[]{:S(2)}) async-start(), calls=%async_computation.24 | async-start | bytes 9584640 | tf_op jit(solution)/shard_map/reduce_scatter | solution.py:464
  1411.5 344.8 %reduce-scatter.30.cloned.1.call-start = ((), (), s32[]{:S(2)}) async-start(), calls=%async_computation.26 | async-start | bytes 12165120
  1420.5 9.0 copy-start.18
  1485.0 425.6 %reduce-scatter.18.cloned.1.call-start = ((), (), s32[]{:S(2)}) async-start(), calls=%async_computation.20 | async-start | bytes 10813440 | tf_op jit(solution)/shard_map/reduce_scatter | solution.py:478
  1485.6 581.0 %reduce-scatter.20.cloned.1.call-start = ((), (), s32[]{:S(2)}) async-start(), calls=%async_computation.21 | async-start | bytes 13516800 | tf_op jit(solution)/shard_map/reduce_scatter | solution.py:473
  1501.5 103.5 %copy-start.19 = (bf16[384,2560]{1,0:T(8,128)(2,1)S(1)}, bf16[384,2560]{1,0:T(8,128)(2,1)}, u32[]{:S(2)}) copy-start(bf16[384,2560]{1,0:T(8,128)(2,1)} %param.17) | copy-start | bytes 5898244
  (35 other events, 117.8 us)
Sparse Core Ops, SparseCore 0:
  16.2 70.3 all-gather.11
  98.5 29.0 all-gather.13
  131.0 105.0 all-gather.9
  238.9 96.7 all-gather.15
  337.4 53.4 all-gather.19
  392.9 141.0 all-gather.17
  535.9 53.1 all-gather.21
  591.0 54.9 all-gather.23
  666.7 136.2 reduce-scatter.13
  809.1 141.5 all-gather.25
  1022.1 134.4 reduce-scatter.15
  1347.4 29.6 reduce-scatter.27
  1380.6 70.7 reduce-scatter.23
  1454.8 72.0 reduce-scatter.21
  1530.2 71.9 reduce-scatter.25
  1608.2 148.1 reduce-scatter.29
  1758.6 151.9 reduce-scatter.17
  1912.9 153.6 reduce-scatter.19

commit v2 on v1

--- a/solution.py
+++ b/solution.py
@@ -203,27 +203,24 @@
     @pl.when(head == pl.num_programs(0) - 1)
     def _():
         query_grad_ref[...] = query_acc[...]
-        latent_grad_ref[...] = latent_acc[...].astype(BF)
-        rope_grad_ref[...] = rope_acc[...].astype(BF)
+        latent_grad_ref[...] = latent_acc[...]
+        rope_grad_ref[...] = rope_acc[...]
 
 
 def whole(shape):
     return pl.BlockSpec(shape, lambda head: (0,) * len(shape))
 
 
-def attend(weights, query_t, latent, rope, cos_t, sin_t, bias_t, query_rows):
-    row_total, col_total, pack_rows, pack_cols = weights.shape
-    here = pack_cols // HEAD
-    heads = row_total * here
+def attend(weights, query_t, latent, rope, cos_t, sin_t, bias_t, query_rows, block):
+    _, col_total, pack_rows, pack_cols = weights.shape
+    heads = pack_cols // HEAD
     length, local = bias_t.shape
     tile = math.gcd(length, 256)
     return pl.pallas_call(
         functools.partial(attend_kernel, query_rows, tile),
         grid=(heads,),
         in_specs=[
-            pl.BlockSpec(
-                (1, col_total, pack_rows, HEAD), lambda head: (head // here, 0, 0, head % here)
-            ),
+            pl.BlockSpec((1, col_total, pack_rows, HEAD), lambda head: (block, 0, 0, head)),
             whole(query_t.shape),
             whole(latent.shape),
             whole(rope.shape),
@@ -244,8 +241,8 @@
             dimension_semantics=("arbitrary",), vmem_limit_bytes=48 * 1024 * 1024
         ),
         cost_estimate=pl.CostEstimate(
-            flops=heads * 2 * local * length * 512,
-            bytes_accessed=weights.size * 2,
+            flops=heads * 1_700_000_000,
+            bytes_accessed=weights[0].size * 2,
             transcendentals=heads * local * length,
         ),
         name="attend",
@@ -253,21 +250,18 @@
 
 
 def attend_back(
-    weights, query_t, latent, latent_t, rope, cos_t, sin_t, bias_t, mixed_t, grad_t, lse, query_rows
+    weights, query_t, latent, latent_t, rope, cos_t, sin_t, bias_t, mixed_t, grad_t, lse,
+    query_rows, block,
 ):
-    row_total, col_total, pack_rows, pack_cols = weights.shape
-    here = pack_cols // HEAD
-    heads = row_total * here
+    _, col_total, pack_rows, pack_cols = weights.shape
+    heads = pack_cols // HEAD
     length, local = bias_t.shape
     tile = math.gcd(length, 256)
-    pack_spec = pl.BlockSpec(
-        (1, col_total, pack_rows, HEAD), lambda head: (head // here, 0, 0, head % here)
-    )
     return pl.pallas_call(
         functools.partial(attend_back_kernel, query_rows, tile),
         grid=(heads,),
         in_specs=[
-            pack_spec,
+            pl.BlockSpec((1, col_total, pack_rows, HEAD), lambda head: (block, 0, 0, head)),
             whole(query_t.shape),
             whole(latent.shape),
             whole(latent_t.shape),
@@ -276,20 +270,20 @@
             whole(sin_t.shape),
             whole(bias_t.shape),
             pl.BlockSpec((VDIM, local), lambda head: (head, 0)),
-            pl.BlockSpec((VDIM, local), lambda head: (head, 0)),
+            pl.BlockSpec((VDIM, local), lambda head: (block * heads + head, 0)),
             pl.BlockSpec((1, 1, local), lambda head: (head, 0, 0)),
         ],
         out_specs=[
-            pack_spec,
+            pl.BlockSpec((1, col_total, pack_rows, HEAD), lambda head: (0, 0, 0, head)),
             whole(query_t.shape),
             whole(latent.shape),
             whole(rope.shape),
         ],
         out_shape=[
-            jax.ShapeDtypeStruct(weights.shape, BF),
+            jax.ShapeDtypeStruct((1,) + weights.shape[1:], BF),
             jax.ShapeDtypeStruct(query_t.shape, F32),
-            jax.ShapeDtypeStruct(latent.shape, BF),
-            jax.ShapeDtypeStruct(rope.shape, BF),
+            jax.ShapeDtypeStruct(latent.shape, F32),
+            jax.ShapeDtypeStruct(rope.shape, F32),
         ],
         scratch_shapes=[
             pltpu.VMEM(query_t.shape, F32),
@@ -301,18 +295,179 @@
             dimension_semantics=("arbitrary",), vmem_limit_bytes=48 * 1024 * 1024
         ),
         cost_estimate=pl.CostEstimate(
-            flops=heads * 2 * local * length * 1280,
-            bytes_accessed=weights.size * 4,
+            flops=heads * 4_200_000_000,
+            bytes_accessed=weights[0].size * 4,
             transcendentals=heads * local * length,
         ),
         name="attend_back",
     )(weights, query_t, latent, latent_t, rope, cos_t, sin_t, bias_t, mixed_t, grad_t, lse)
 
 
-def partial_rows(product):
-    return lax.psum_scatter(
-        product.astype(BF), "row", scatter_dimension=0, tiled=True
-    ).astype(F32)
+def weight_grad_kernel(chunks, *refs):
+    lefts, rights, out_ref = refs[:chunks], refs[chunks : 2 * chunks], refs[2 * chunks]
+    total = None
+    for left_ref, right_ref in zip(lefts, rights):
+        term = dot_plain(left_ref[...].T, right_ref[...])
+        total = term if total is None else total + term
+    out_ref[...] = total.astype(out_ref.dtype)
+
+
+def weight_grad(lefts, rights, name):
+    chunks = len(lefts)
+    rows, width = lefts[0].shape
+    units = rights[0].shape[1]
+    tile = math.gcd(width, 256)
+    return pl.pallas_call(
+        functools.partial(weight_grad_kernel, chunks),
+        grid=(width // tile,),
+        in_specs=[pl.BlockSpec((rows, tile), lambda step: (0, step))] * chunks
+        + [pl.BlockSpec((rows, units), lambda step: (0, 0))] * chunks,
+        out_specs=pl.BlockSpec((tile, units), lambda step: (step, 0)),
+        out_shape=jax.ShapeDtypeStruct((width, units), BF),
+        compiler_params=pltpu.CompilerParams(
+            dimension_semantics=("arbitrary",), vmem_limit_bytes=48 * 1024 * 1024
+        ),
+        cost_estimate=pl.CostEstimate(
+            flops=2 * chunks * rows * width * units,
+            bytes_accessed=2 * (chunks * rows + units) * width,
+            transcendentals=0,
+        ),
+        name=name,
+    )(*lefts, *rights)
+
+
+together = lax.optimization_barrier
+
+
+class Task:
+    def __init__(self, steps):
+        self.steps, self.state, self.value, self.over = steps, None, None, False
+
+    def advance(self):
+        if not self.over:
+            try:
+                return self.steps.send(self.state)
+            except StopIteration as stop:
+                self.value, self.over = stop.value, True
+        return ()
+
+    def result(self):
+        self.advance()
+        assert self.over
+        return self.value
+
+
+def slot(*tasks):
+    states = together(tuple(task.advance() for task in tasks))
+    for task, state in zip(tasks, states):
+        task.state = state
+
+
+def slots(count, *tasks):
+    for _ in range(count):
+        slot(*tasks)
+
+
+def gather_steps(values):
+    total = lax.axis_size("row")
+    up, down = [None], [None]
+    ways = (values, values)
+    for step in range(1, total):
+        ways = yield (
+            lax.ppermute(ways[0], "row", [(i, i + 1) for i in range(step - 1, total - 1)]),
+            lax.ppermute(ways[1], "row", [(i, i - 1) for i in range(1, total - step + 1)]),
+        )
+        up.append(ways[0])
+        down.append(ways[1])
+    return jnp.concatenate([values] + [up[step] + down[total - step] for step in range(1, total)])
+
+
+def add_parts(left_op, right_op):
+    return (left_op.astype(F32) + right_op.astype(F32)).astype(BF)
+
+
+def reduce_steps(parts):
+    total = lax.axis_size("row")
+    ways = None
+    for step in range(total - 1):
+        sends = (parts[step + 1], parts[total - 1 - step])
+        if step > 0:
+            sends = (add_parts(sends[0], ways[0]), add_parts(sends[1], ways[1]))
+        ways = yield (
+            lax.ppermute(sends[0], "row", [(i, i + 1) for i in range(step + 1)]),
+            lax.ppermute(sends[1], "row", [(i, i - 1) for i in range(total - 1 - step, total)]),
+        )
+    return parts[0].astype(F32) + ways[0].astype(F32) + ways[1].astype(F32)
+
+
+def reduce_row_steps(line):
+    total = lax.axis_size("row")
+    row_rank = lax.axis_index("row")
+    parts = [pick(line, lax.rem(row_rank + total - step, total), 0) for step in range(total)]
+    return (yield from reduce_steps(parts))
+
+
+def product_steps(product):
+    total = lax.axis_size("row")
+    rows = product.shape[0] // total
+    parts = [product[at * rows : (at + 1) * rows] for at in range(total)]
+    return (yield from reduce_steps(parts))
+
+
+def swap(values, bit):
+    total = lax.axis_size("col")
+    return lax.ppermute(values, "col", [(i, i ^ bit) for i in range(total)])
+
+
+def pick(values, index, axis):
+    return lax.dynamic_index_in_dim(values, index, axis, keepdims=False)
+
+
+def far_bits():
+    bits, bit = [], 2
+    while bit < lax.axis_size("col"):
+        bits.append(bit)
+        bit *= 2
+    return bits
+
+
+def gather_col_steps(first, second):
+    halves = [[(0, first)], [(0, second)]]
+    orders = [far_bits()[::-1] + [1], far_bits() + [1]]
+    for step in range(len(orders[0])):
+        got = yield tuple(
+            tuple(swap(part, order[step]) for _, part in half)
+            for half, order in zip(halves, orders)
+        )
+        halves = [
+            half + [(away + order[step], part) for (away, _), part in zip(half, parts)]
+            for half, order, parts in zip(halves, orders, got)
+        ]
+    return halves
+
+
+def reduce_col_steps(blocks):
+    col_rank = lax.axis_index("col")
+    bits = far_bits()
+    dims = [bits[::-1] + [1] for _ in blocks]
+    orders = [[1] + (bits if at % 2 == 0 else bits[::-1]) for at in range(len(blocks))]
+    blocks = [block.reshape((2,) * len(dims[0]) + block.shape[1:]) for block in blocks]
+    for step in range(len(dims[0])):
+        keeps, sends = [], []
+        for block, dim, order in zip(blocks, dims, orders):
+            bit = order[step]
+            axis, own = dim.index(bit), lax.rem(col_rank // bit, 2)
+            keeps.append(pick(block, own, axis))
+            sends.append(swap(pick(block, 1 - own, axis), bit))
+            dim.remove(bit)
+        sends = yield tuple(sends)
+        blocks = [add_parts(keep, send) for keep, send in zip(keeps, sends)]
+    return jnp.stack(blocks)
+
+
+def reduce_all_steps(blocks):
+    line = yield from reduce_col_steps(blocks)
+    return (yield from reduce_row_steps(line))
 
 
 def token_rows(values):
@@ -369,7 +524,23 @@
     )
     pack_wide = -(-(lat_wide + 3) // 128) * 128
     down_all = lax.all_gather(pad_to(down_pack, pack_wide), both_axes, axis=0, tiled=True)
-    down_w = down_all[:, :lat_wide]
+
+    query_pack = jnp.pad(
+        query_up.reshape(query_rows, heads_here, NOPE + ROPE),
+        ((0, 0), (0, 0), (0, HEAD - NOPE - ROPE)),
+    ).reshape(query_rows, heads_here * HEAD)
+    up_pack = jnp.concatenate([query_pack, latent_up], axis=0)
+    pack_rows = up_pack.shape[0]
+    mlp_pack = jnp.concatenate([gate_weight, up_weight, down_weight.T], axis=0)
+    part_rows = gate_weight.shape[0]
+    half_rows = part_rows // 2
+    down_all, mlp_pack = together((down_all, mlp_pack))
+    mlp_w = Task(
+        gather_col_steps(
+            mlp_pack[: part_rows + half_rows], mlp_pack[part_rows + half_rows :]
+        )
+    )
+
     attn_g = down_all[:, lat_wide].astype(F32)
     mlp_g = down_all[:, lat_wide + 1].astype(F32)
     misc_all = down_all[:, lat_wide + 2].astype(F32).reshape(devices, down_rows)
@@ -378,32 +549,14 @@
     counts = jnp.sum(misc_all[:, q_part + kv_part : q_part + kv_part + 2], axis=0)
     valid_total = counts[0] * 256.0 + counts[1]
 
-    query_pack = jnp.pad(
-        query_up.reshape(query_rows, heads_here, NOPE + ROPE),
-        ((0, 0), (0, 0), (0, HEAD - NOPE - ROPE)),
-    ).reshape(query_rows, heads_here * HEAD)
-    up_pack = jnp.concatenate([query_pack, latent_up], axis=0)
-    pack_rows = up_pack.shape[0]
-    head_w = lax.all_gather(up_pack, both_axes, axis=0, tiled=True).reshape(
-        row_total, col_total, pack_rows, heads_here * HEAD
-    )
-    out_all = lax.all_gather(output_weight.T, both_axes, axis=0, tiled=True).reshape(
-        row_total, width, heads_here * VDIM
-    )
-    gate_full, up_full, down_t = (
-        lax.all_gather(gate_weight, "col", axis=0, tiled=True),
-        lax.all_gather(up_weight, "col", axis=0, tiled=True),
-        lax.all_gather(down_weight.T, "col", axis=0, tiled=True),
-    )
-
     cosine, sine = rotary(segments)
     cos_here = lax.dynamic_slice_in_dim(cosine, offset, local_rows, 0)
     sin_here = lax.dynamic_slice_in_dim(sine, offset, local_rows, 0)
     tokens_f = inputs.astype(F32)
     normed, normed_unit = root_norm(tokens_f, attn_g)
     normed_b = normed.astype(BF)
-    lat = dot_plain(normed_b, down_w)
-    query_lat, kv_lat = lat[:, :q_rank], lat[:, q_rank:]
+    lat = dot_plain(normed_b, down_all)
+    query_lat, kv_lat = lat[:, :q_rank], lat[:, q_rank:lat_wide]
     query_norm, query_unit = root_norm(query_lat, query_g)
     kv_norm, kv_unit = root_norm(kv_lat[:, :KV_RANK], latent_g)
     key_rope = rotate(kv_lat[:, KV_RANK:], cos_here, sin_here)
@@ -418,6 +571,17 @@
         axis=1,
     ).astype(BF)
     latent_all = token_rows(latent_pack)
+    got = mlp_w.advance()
+    latent_all, up_pack, got = together((latent_all, up_pack, got))
+    mlp_w.state = got
+    head_w = lax.all_gather(up_pack, both_axes, axis=0, tiled=True)
+    got = mlp_w.advance()
+    head_w, out_here, got = together((head_w, output_weight.T, got))
+    mlp_w.state = got
+    head_w = head_w.reshape(row_total, col_total, pack_rows, heads_here * HEAD)
+    out_all = lax.all_gather(out_here, both_axes, axis=0, tiled=True).reshape(
+        row_total, width, heads_here * VDIM
+    )
     kv_all = latent_all[:, :KV_RANK]
     rope_all = latent_all[:, KV_RANK:]
 
@@ -430,34 +594,126 @@
     bias_t = jnp.where(allowed_t, 0.0, HIDE).astype(F32)
     query_t = query_nb.T
     cos_t, sin_t = cos_here.T, sin_here.T
-    mixed_t, lse = attend(head_w, query_t, kv_all, rope_all, cos_t, sin_t, bias_t, query_rows)
-    mixed_heads = mixed_t.reshape(row_total, heads_here * VDIM, local_rows)
-    attn_sum = dot_dims(mixed_heads, out_all, (0, 1), (0, 2))
+    mixed = [
+        attend(head_w, query_t, kv_all, rope_all, cos_t, sin_t, bias_t, query_rows, block)
+        for block in range(row_total)
+    ]
+    while not mlp_w.over:
+        mlp_w.state = mlp_w.advance()
+    gate_full = jnp.zeros((col_total, part_rows, mlp_pack.shape[1]), BF)
+    up_full, down_t = gate_full, gate_full
+    col_rank = lax.axis_index("col")
+
+    def put(array, part, away, row):
+        return lax.dynamic_update_slice(
+            array, part[None], (jnp.bitwise_xor(col_rank, away), row, 0)
+        )
+
+    for (away, one), (away_b, two) in zip(*[sorted(h, key=lambda p: p[0]) for h in mlp_w.value]):
+        gate_full = put(gate_full, one[:part_rows], away, 0)
+        up_full = put(up_full, one[part_rows:], away, 0)
+        up_full = put(up_full, two[: part_rows - half_rows], away_b, half_rows)
+        down_t = put(down_t, two[part_rows - half_rows :], away_b, 0)
+    gate_full, up_full, down_t = (
+        gate_full.reshape(width, -1), up_full.reshape(width, -1), down_t.reshape(width, -1)
+    )
+    mixed, out_all, gate_full, up_full, down_t = together(
+        (mixed, out_all, gate_full, up_full, down_t)
+    )
+    attn_sum = None
+    for block in range(row_total):
+        term = dot_dims(mixed[block][0], out_all[block], (0,), (1,))
+        attn_sum = term if attn_sum is None else attn_sum + term
 
     residual = tokens_f + RES * attn_sum
     mlp_in, mlp_unit = root_norm(residual, mlp_g)
-    mlp_all = token_rows(mlp_in.astype(BF))
-    gate_act = dot_plain(mlp_all, gate_full)
-    up_act = dot_plain(mlp_all, up_full)
-    gate_sig = jax.nn.sigmoid(gate_act)
-    silu_val = gate_act * gate_sig
-    hidden = (silu_val * up_act).astype(BF)
-    outputs = residual + RES * partial_rows(dot_trans_right(hidden, down_t))
-    error_val = outputs - teacher.astype(F32)
+    mlp_b = mlp_in.astype(BF)
     weight_v = valid_mask.astype(F32)[:, None]
-    total_tokens = local_rows * row_total * col_total
-    squared = 0.5 * jnp.sum(weight_v * error_val * error_val)
-    out_grad = cotangent.astype(F32) + total_tokens / valid_total * weight_v * error_val
-    branch_grad = token_rows((RES * out_grad).astype(BF))
-    hidden_grad = dot_plain(branch_grad, down_t)
-    gate_grad = (hidden_grad * up_act * gate_sig * (1.0 + gate_act * (1.0 - gate_sig))).astype(BF)
-    up_grad = (hidden_grad * silu_val).astype(BF)
-    mlp_in_grad = partial_rows(
-        dot_trans_right(gate_grad, gate_full) + dot_trans_right(up_grad, up_full)
-    )
-    gate_wg = dot_trans_left(mlp_all, gate_grad).astype(BF)
-    up_wg = dot_trans_left(mlp_all, up_grad).astype(BF)
-    down_wg = dot_trans_left(branch_grad, hidden).astype(BF)
+    out_scale = local_rows * devices / valid_total
+    rows = local_rows // 2
+    parts = [slice(0, rows), slice(rows, 2 * rows)]
+
+    def forward_steps(tokens):
+        gate_act = yield dot_plain(tokens, gate_full)
+        up_act = dot_plain(tokens, up_full)
+        hidden = yield (gate_act * jax.nn.sigmoid(gate_act) * up_act).astype(BF)
+        product = yield dot_trans_right(hidden, down_t).astype(BF)
+        return (gate_act, up_act, hidden, product)
+
+    def judge(part, down_sum):
+        out_rows = residual[part] + RES * down_sum
+        error_val = out_rows - teacher[part].astype(F32)
+        squared = 0.5 * jnp.sum(weight_v[part] * error_val * error_val)
+        grad_rows = cotangent[part].astype(F32) + out_scale * weight_v[part] * error_val
+        return (out_rows.astype(BF), squared, grad_rows, (RES * grad_rows).astype(BF))
+
+    def backward_steps(branch, gate_act, up_act):
+        gate_sig = jax.nn.sigmoid(gate_act)
+        hidden_grad = dot_plain(branch, down_t)
+        gate_grad, up_grad = yield (
+            (hidden_grad * up_act * gate_sig * (1.0 + gate_act * (1.0 - gate_sig))).astype(BF),
+            (hidden_grad * gate_act * gate_sig).astype(BF),
+        )
+        product = yield dot_trans_right(gate_grad, gate_full)
+        product = yield (product + dot_trans_right(up_grad, up_full)).astype(BF)
+        return (gate_grad, up_grad, product)
+
+    def weight_steps(work):
+        got = []
+        for lefts, rights, name in work:
+            got.append((yield weight_grad(lefts, rights, name)))
+        return got
+
+    hops = row_total - 1
+    mlp_b = mlp_in.astype(BF)
+    give_0, give_1 = [Task(gather_steps(mlp_b[part])) for part in parts]
+    slots(hops, give_0)
+    tokens_0 = give_0.result()
+    fore_0 = Task(forward_steps(tokens_0))
+    slots(hops, give_1, fore_0)
+    tokens_1 = give_1.result()
+    fore_0 = fore_0.result()
+    take_0 = Task(product_steps(fore_0[3]))
+    fore_1 = Task(forward_steps(tokens_1))
+    slots(hops, take_0, fore_1)
+    judged_0 = judge(parts[0], take_0.result())
+    fore_1 = fore_1.result()
+    take_1 = Task(product_steps(fore_1[3]))
+    give_0 = Task(gather_steps(judged_0[3]))
+    slot(give_0)
+    slots(hops - 1, give_0, take_1)
+    branch_0 = give_0.result()
+    back_0 = Task(backward_steps(branch_0, fore_0[0], fore_0[1]))
+    slot(take_1, back_0)
+    judged_1 = judge(parts[1], take_1.result())
+    give_1 = Task(gather_steps(judged_1[3]))
+    slots(hops - 1, give_1, back_0)
+    back_0 = back_0.result()
+    take_0 = Task(product_steps(back_0[2]))
+    slot(give_1, take_0)
+    branch_1 = give_1.result()
+    back_1 = Task(backward_steps(branch_1, fore_1[0], fore_1[1]))
+    slots(hops - 1, take_0, back_1)
+    grad_0 = take_0.result()
+    slot(back_1)
+    back_1 = back_1.result()
+    take_1 = Task(product_steps(back_1[2]))
+    work = Task(
+        weight_steps(
+            [
+                ([branch_0, branch_1], [fore_0[2], fore_1[2]], "down_wg"),
+                ([tokens_0, tokens_1], [back_0[0], back_1[0]], "gate_wg"),
+                ([tokens_0, tokens_1], [back_0[1], back_1[1]], "up_wg"),
+            ]
+        )
+    )
+    slots(max(hops, 3), take_1, work)
+    grad_1 = take_1.result()
+    down_wg, gate_wg, up_wg = work.result()
+    outputs = jnp.concatenate([judged_0[0], judged_1[0]])
+    squared = judged_0[1] + judged_1[1]
+    out_grad = jnp.concatenate([judged_0[2], judged_1[2]])
+    mlp_in_grad = jnp.concatenate([grad_0, grad_1])
     gate_wg, up_wg, down_wg = (
         lax.psum_scatter(gate_wg, "col", scatter_dimension=0, tiled=True).astype(F32),
         lax.psum_scatter(up_wg, "col", scatter_dimension=0, tiled=True).astype(F32),
@@ -468,31 +724,53 @@
 
     attn_grad_in = (RES * residual_grad).astype(BF)
     grad_t = dot_dims(out_all, attn_grad_in, (1,), (1,)).astype(BF)
-    out_wg = dot_dims(attn_grad_in, mixed_heads, (0,), (2,)).astype(BF)
-    out_wg = jnp.transpose(out_wg, (1, 0, 2)).reshape(row_total * width, heads_here * VDIM)
-    out_wg = lax.psum_scatter(out_wg, both_axes, scatter_dimension=0, tiled=True).astype(F32).T
-    head_wg, query_back_t, kv_back, rope_back = attend_back(
-        head_w, query_t, kv_all, kv_all.T, rope_all, cos_t, sin_t, bias_t, mixed_t,
-        grad_t.reshape(mixed_t.shape), lse, query_rows,
-    )
-    head_wg = lax.psum_scatter(
-        head_wg.reshape(devices * pack_rows, heads_here * HEAD),
-        both_axes, scatter_dimension=0, tiled=True,
-    ).astype(F32)
-    qu_wg = head_wg[:query_rows].reshape(query_rows, heads_here, HEAD)[:, :, : NOPE + ROPE]
-    qu_wg = qu_wg.reshape(query_rows, heads_here * (NOPE + ROPE))
-    kvu_wg = head_wg[query_rows:]
-    latent_back = partial_rows(jnp.concatenate([kv_back, rope_back], axis=1))
+    out_wg = [
+        dot_dims(attn_grad_in, mixed_t, (0,), (1,))
+        .astype(BF)
+        .reshape(col_total, -1, heads_here * VDIM)
+        for mixed_t, _ in mixed
+    ]
+    latent_t = kv_all.T
+    grad_t, out_wg = together((grad_t.reshape(-1, local_rows), out_wg))
+
+    def back_steps():
+        got = []
+        for block in range(row_total):
+            mixed_t, lse = mixed[block]
+            wg, query_part, kv_part_back, rope_part = yield attend_back(
+                head_w, query_t, kv_all, latent_t, rope_all, cos_t, sin_t, bias_t, mixed_t,
+                grad_t, lse, query_rows, block,
+            )
+            got.append((wg[0], query_part, jnp.concatenate([kv_part_back, rope_part], axis=1)))
+        return got
+
+    steps = len(far_bits()) + 1
+    backs = Task(back_steps())
+    out_reduce = Task(reduce_all_steps(out_wg))
+    slots(row_total, backs, out_reduce)
+    backs = backs.result()
+    query_back_t = sum(query_part for _, query_part, _ in backs)
+    latent_back = sum(part for _, _, part in backs).astype(BF)
+    latent_reduce = Task(reduce_row_steps(latent_back.reshape(row_total, local_rows, -1)))
+    head_reduce = Task(reduce_all_steps([wg for wg, _, _ in backs]))
+    slots(hops, latent_reduce, head_reduce, out_reduce)
+    latent_back = latent_reduce.result()
     kv_norm_grad = latent_back[:, :KV_RANK]
     rope_grad = latent_back[:, KV_RANK + NOPE : KV_RANK + NOPE + ROPE]
     query_norm_grad = query_back_t.T
     query_lat_grad, query_gain_grad = norm_back(query_norm_grad, query_unit, query_lat, query_g)
     kv_lat_part, latent_gain_grad = norm_back(kv_norm_grad, kv_unit, kv_lat[:, :KV_RANK], latent_g)
     lat_grad = jnp.concatenate(
-        [query_lat_grad, kv_lat_part, rotate(rope_grad, cos_here, -sin_here)], axis=-1
+        [
+            query_lat_grad,
+            kv_lat_part,
+            rotate(rope_grad, cos_here, -sin_here),
+            jnp.zeros((local_rows, pack_wide - lat_wide), F32),
+        ],
+        axis=-1,
     ).astype(BF)
     lat_wg = dot_trans_left(normed_b, lat_grad)
-    normed_grad = dot_trans_right(lat_grad, down_w)
+    normed_grad = dot_trans_right(lat_grad, down_all)
     input_part, attention_gain_gradient = norm_back(normed_grad, normed_unit, tokens_f, attn_g)
     input_grad = residual_grad + input_part
 
@@ -508,17 +786,23 @@
         axis=1,
     )
     misc_grad = pad_to(misc_grad, down_rows).reshape(devices * down_rows, 1)
-    small = jnp.concatenate(
-        [lat_wg, attention_gain_gradient[:, None], mlp_gain_grad[:, None], misc_grad], axis=1
-    )
-    small = lax.psum_scatter(
-        pad_to(small, pack_wide), both_axes, scatter_dimension=0, tiled=True
-    )
+    lane = lax.broadcasted_iota(jnp.int32, lat_wg.shape, 1)
+    small = jnp.where(lane == lat_wide, attention_gain_gradient[:, None], lat_wg)
+    small = jnp.where(lane == lat_wide + 1, mlp_gain_grad[:, None], small)
+    small = jnp.where(lane == lat_wide + 2, misc_grad, small).astype(BF)
+    small = small.reshape(row_total, col_total, down_rows, pack_wide)
+    small_reduce = Task(reduce_all_steps([small[block] for block in range(row_total)]))
+    slots(steps + hops, small_reduce, head_reduce, out_reduce)
+    small, head_wg, out_wg = small_reduce.result(), head_reduce.result(), out_reduce.result()
+    out_wg = out_wg.T
+    qu_wg = head_wg[:query_rows].reshape(query_rows, heads_here, HEAD)[:, :, : NOPE + ROPE]
+    qu_wg = qu_wg.reshape(query_rows, heads_here * (NOPE + ROPE))
+    kvu_wg = head_wg[query_rows:]
     misc_sum = small[:, lat_wide + 2]
     at = q_part + kv_part
     loss = (misc_sum[at] + misc_sum[at + 1]) / valid_total
     return (
-        outputs.astype(BF),
+        outputs,
         loss,
         input_grad,
         small[:, :q_rank],

time: 2080 us -> 1600 us (0.77)
  waiting for transfers between devices: 1410 us -> 475 us
  starting transfers between devices: 1.87 us -> 213 us
  other arithmetic: 58.6 us -> 181 us
  local copies, waits for them, and re-layouts: 108 us -> 200 us
  Pallas kernels: 225 us -> 295 us
  matrix products: 249 us -> 203 us
    reduce_scatter x4 -> x0, waiting for transfers between devices: 565 us -> none  [the longest x2 269 us: partial_rows(): lax.psum_scatter(product.astype(BF), 'row', scatter_dimension=0, tiled=True)]
    ppermute x0 -> x122, waiting for transfers between devices: none -> 372 us  [the longest x50 155 us: swap(): return lax.ppermute(values, 'col', [(i, i ^ bit) for i in range(total)])]
    all_gather x3 -> x1, waiting for transfers between devices: 305 us -> 0.01 us  [token_rows(): return lax.all_gather(values, 'row', axis=0, tiled=True)]
    ppermute x0 -> x122, starting transfers between devices: none -> 212 us  [the longest x24 110 us: reduce_steps(): lax.ppermute(sends[0], 'row', [(i, i + 1) for i in range(step + 1)])]
    all_gather x5 -> x2, waiting for transfers between devices: 231 us -> 39.9 us  [the longest x1 39.9 us: body(): head_w = lax.all_gather(up_pack, both_axes, axis=0, tiled=True)]
    unnamed x20 -> x7, waiting for transfers between devices: 148 us -> 0.12 us
    convert_element_type x4 -> x52, other arithmetic: 9.7 us -> 91.9 us  [the longest x44 63.7 us: add_parts(): return (left_op.astype(F32) + right_op.astype(F32)).astype(BF)]
    reduce_scatter x1, waiting for transfers between devices: 72.7 us -> 0.01 us  [body(): lax.psum_scatter(down_wg, 'col', scatter_dimension=0, tiled=True)]
  transfers between devices with their start and end apart: 18 -> 129, of which waited for: 16 -> 48; matrix products, arithmetic and copies ran while one was open for 13% -> 28% of each run, Pallas kernels for 3% -> 19%
where the time goes in v2:
time: 1600 us; the launch traced here: 1590 us
  waiting for transfers between devices  475 us (30%)
  Pallas kernels  295 us (18%)
  starting transfers between devices  213 us (13%)
  matrix products  203 us (13%)
  local copies, waits for them, and re-layouts  200 us (12%)
  other arithmetic  181 us (11%)
  between operations  25.7 us (2%)
    pallas_call x4, Pallas kernels, attend_back(): pl.pallas_call(functools.partial(attend_back_kernel, query_rows, tile), g...  171 us
    ppermute x50, waiting for transfers between devices, swap(): return lax.ppermute(values, 'col', [(i, i ^ bit) for i in range(total)])  155 us
    ppermute x24, starting transfers between devices, reduce_steps(): lax.ppermute(sends[0], 'row', [(i, i + 1) for i in range(step + 1)])  110 us
    dot_general x17, matrix products, dot_dims(): lax.dot_general(left_op, right_op, ((left_dims, right_dims), ((), ())), p...  109 us
    ppermute x12, waiting for transfers between devices, gather_steps(): lax.ppermute(ways[1], 'row', [(i, i - 1) for i in range(1, total - step +...  107 us
    dot_general x7, matrix products, dot_plain(): return jnp.dot(left_op, right_op, preferred_element_type=F32)  93.6 us
    pallas_call x4, Pallas kernels, attend(): pl.pallas_call(functools.partial(attend_kernel, query_rows, tile), grid=(...  67.6 us
    convert_element_type x44, other arithmetic, add_parts(): return (left_op.astype(F32) + right_op.astype(F32)).astype(BF)  63.7 us
  transfers between devices with their start and end apart: 129, of which 48 were waited for; matrix products, arithmetic and copies ran while one was open for 28% of the time, Pallas kernels for 19%

profile of v2, /device:TPU:0, one launch (start us, length us, event | category | flops | bytes accessed | tf_op | source)
XLA Modules:
  0.0 1591.0 jit_solution(3096039048394748447)
XLA Ops:
  23.6 62.9 %all-gather.5.cloned.1.call-done = bf16[2560,1152]{1,0:T(8,128)(2,1)} async-done(((bf16[80,1152]{1,0:T(8,128)(2,1)}), bf16[2560,1152]{1,0:T(8,128)(2,1)}) %all-gather.5.cloned.1.call-update) | async-done | bytes 5898256 | tf_op jit(solution)/shard_map/all_gather | solution.py:526
  107.7 34.0 %collective-permute-done = bf16[480,1600]{1,0:T(8,128)(2,1)} collective-permute-done((bf16[480,1600]{1,0:T(8,128)(2,1)}, bf16[480,1600]{1,0:T(8,128)(2,1)}, u32[]{:S(2)}, u32[]{:S(2)}) %collective-permute-start) | collective-permute-done | bytes 1536032 | tf_op jit(solution)/shard_map/ppermute | solution.py:419
  147.0 37.7 %collective-permute-done.2 = bf16[480,1600]{1,0:T(8,128)(2,1)} collective-permute-done((bf16[480,1600]{1,0:T(8,128)(2,1)}, bf16[480,1600]{1,0:T(8,128)(2,1)}, u32[]{:S(2)}, u32[]{:S(2)}) %collective-permute-start.2) | collective-permute-done | bytes 1536032 | tf_op jit(solution)/shard_map/ppermute | solution.py:419
  192.2 34.6 %collective-permute-done.3 = bf16[480,1600]{1,0:T(8,128)(2,1)} collective-permute-done((bf16[480,1600]{1,0:T(8,128)(2,1)}, bf16[480,1600]{1,0:T(8,128)(2,1)}, u32[]{:S(2)}, u32[]{:S(2)}) %collective-permute-start.3) | collective-permute-done | bytes 1536032 | tf_op jit(solution)/shard_map/ppermute | solution.py:419
  226.8 39.9 %all-gather.9.cloned.1.call-done = bf16[4096,1280]{0,1:T(8,128)(2,1)} async-done(((bf16[128,1280]{0,1:T(8,128)(2,1)}), bf16[4096,1280]{0,1:T(8,128)(2,1)}) %all-gather.9.cloned.1.call-update) | async-done | bytes 10485776 | tf_op jit(solution)/shard_map/all_gather | solution.py:577
  304.8 14.4 copy.161
  326.8 16.7 %attend.7 = (bf16[640,384]{1,0:T(8,128)(2,1)S(1)}, f32[10,1,384]{2,1,0:T(1,128)S(1)}) custom-call(bf16[4,8,128,1280]{3,2,1,0:T(8,128)(2,1)} %bitcast.511, bf16[768,384]{1,0:T(8,128)(2,1)S(1)} %copy-done.19, bf16[1536,256]{1,0:T(8,128)(2,1)S(1)} %copy.163.latent_ref, bf16[1536,128]{1,0:T(8,128)(2,1)S(1)} %copy.164.rope_ref, f32[16,384]{1,0:T(8,128)S(1)} %copy-done.29, ...), custom_call_target="tpu_custom_call" | custom-call | flops 16999999488 | bytes 2621440 | tf_op jit(solution)/shard_map/attend/pallas_call | solution.py:219
  344.6 16.8 %attend.6 = (bf16[640,384]{1,0:T(8,128)(2,1)S(1)}, f32[10,1,384]{2,1,0:T(1,128)S(1)}) custom-call(bf16[4,8,128,1280]{3,2,1,0:T(8,128)(2,1)} %bitcast.512, bf16[768,384]{1,0:T(8,128)(2,1)S(1)} %copy-done.19, bf16[1536,256]{1,0:T(8,128)(2,1)S(1)} %copy-done.12, bf16[1536,128]{1,0:T(8,128)(2,1)S(1)} %copy.164.rope_ref, f32[16,384]{1,0:T(8,128)S(1)} %copy-done.29, ...), custom_call_target="tpu_custom_call" | custom-call | flops 16999999488 | bytes 2621440 | tf_op jit(solution)/shard_map/attend/pallas_call | solution.py:219
  363.0 16.8 %attend.5 = (bf16[640,384]{1,0:T(8,128)(2,1)S(1)}, f32[10,1,384]{2,1,0:T(1,128)S(1)}) custom-call(bf16[4,8,128,1280]{3,2,1,0:T(8,128)(2,1)} %bitcast.513, bf16[768,384]{1,0:T(8,128)(2,1)S(1)} %copy-done.19, bf16[1536,256]{1,0:T(8,128)(2,1)S(1)} %copy-done.12, bf16[1536,128]{1,0:T(8,128)(2,1)S(1)} %copy-done.25, f32[16,384]{1,0:T(8,128)S(1)} %copy-done.29, ...), custom_call_target="tpu_custom_call" | custom-call | flops 16999999488 | bytes 2621440 | tf_op jit(solution)/shard_map/attend/pallas_call | solution.py:219
  379.9 17.2 %attend.4 = (bf16[640,384]{1,0:T(8,128)(2,1)S(1)}, f32[10,1,384]{2,1,0:T(1,128)S(1)}) custom-call(bf16[4,8,128,1280]{3,2,1,0:T(8,128)(2,1)} %bitcast.514, bf16[768,384]{1,0:T(8,128)(2,1)S(1)} %copy-done.19, bf16[1536,256]{1,0:T(8,128)(2,1)S(1)} %copy-done.12, bf16[1536,128]{1,0:T(8,128)(2,1)S(1)} %copy-done.25, f32[16,384]{1,0:T(8,128)S(1)} %copy-done.29, ...), custom_call_target="tpu_custom_call" | custom-call | flops 16999999488 | bytes 2621440 | tf_op jit(solution)/shard_map/attend/pallas_call | solution.py:219
  453.0 20.3 %collective-permute-done.16 = bf16[192,2560]{1,0:T(8,128)(2,1)S(1)} collective-permute-done((bf16[192,2560]{1,0:T(8,128)(2,1)S(1)}, bf16[192,2560]{1,0:T(8,128)(2,1)S(1)}, u32[]{:S(2)}, u32[]{:S(2)}) %collective-permute-start.16) | collective-permute-done | bytes 983072 | tf_op jit(solution)/shard_map/ppermute | solution.py:377
  479.6 25.2 %collective-permute-done.19 = bf16[192,2560]{1,0:T(8,128)(2,1)} collective-permute-done((bf16[192,2560]{1,0:T(8,128)(2,1)S(1)}, bf16[192,2560]{1,0:T(8,128)(2,1)}, u32[]{:S(2)}, u32[]{:S(2)}) %collective-permute-start.19) | collective-permute-done | bytes 983072 | tf_op jit(solution)/shard_map/ppermute | solution.py:378
  519.4 13.9 collective-permute-done.21
  536.6 12.7 fusion.140
  559.8 15.4 multiply_convert_fusion.5
  611.7 12.8 fusion.138
  639.7 15.5 multiply_convert_fusion.4
  693.1 15.3 collective-permute-done.32
  711.3 12.9 collective-permute-done.36
  752.2 11.9 collective-permute-done.39
  775.9 15.4 multiply_convert_fusion.2
  838.9 18.2 %collective-permute-done.47 = bf16[192,2560]{1,0:T(8,128)(2,1)} collective-permute-done((bf16[192,2560]{1,0:T(8,128)(2,1)}, bf16[192,2560]{1,0:T(8,128)(2,1)}, u32[]{:S(2)}, u32[]{:S(2)}) %collective-permute-start.47) | collective-permute-done | bytes 983072 | tf_op jit(solution)/shard_map/ppermute | solution.py:378
  887.4 15.2 multiply_convert_fusion
  907.3 12.1 fusion.154
  957.1 18.6 %down_wg.1 = bf16[2560,1600]{1,0:T(8,128)(2,1)} custom-call(bf16[768,2560]{1,0:T(8,128)(2,1)} %pad_maximum_fusion.2.refs_0_, bf16[768,2560]{1,0:T(8,128)(2,1)} %pad_maximum_fusion.3.refs_1_, bf16[768,1600]{1,0:T(8,128)(2,1)S(1)} %copy-done.38, bf16[768,1600]{1,0:T(8,128)(2,1)S(1)} %copy-done.40), custom_call_target="tpu_custom_call" | custom-call | flops 12582912000 | bytes 16056320 | tf_op jit(solution)/shard_map/down_wg/pallas_call | solution.py:320
  985.0 18.5 %gate_wg.1 = bf16[2560,1600]{1,0:T(8,128)(2,1)} custom-call(bf16[768,2560]{1,0:T(8,128)(2,1)} %pad_maximum_fusion.refs_0_, bf16[768,2560]{1,0:T(8,128)(2,1)} %pad_maximum_fusion.1.refs_1_, bf16[768,1600]{1,0:T(8,128)(2,1)S(1)} %copy-done.32, bf16[768,1600]{1,0:T(8,128)(2,1)S(1)} %copy-done.36), custom_call_target="tpu_custom_call" | custom-call | flops 12582912000 | bytes 16056320 | tf_op jit(solution)/shard_map/gate_wg/pallas_call | solution.py:320
  1011.1 18.6 %up_wg.1 = bf16[2560,1600]{1,0:T(8,128)(2,1)} custom-call(bf16[768,2560]{1,0:T(8,128)(2,1)} %pad_maximum_fusion.refs_0_, bf16[768,2560]{1,0:T(8,128)(2,1)} %pad_maximum_fusion.1.refs_1_, bf16[768,1600]{1,0:T(8,128)(2,1)S(1)} %get-tuple-element.276.refs_2_, bf16[768,1600]{1,0:T(8,128)(2,1)S(1)} %copy-done.34), custom_call_target="tpu_custom_call" | custom-call | flops 12582912000 | bytes 16056320 | tf_op jit(solution)/shard_map/up_wg/pallas_call | solution.py:320
  1069.3 42.9 %attend_back.4 = (bf16[1,8,128,1280]{3,2,1,0:T(8,128)(2,1)}, f32[768,384]{1,0:T(8,128)S(1)}, f32[1536,256]{1,0:T(8,128)}, f32[1536,128]{1,0:T(8,128)S(1)}) custom-call(bf16[4,8,128,1280]{3,2,1,0:T(8,128)(2,1)} %bitcast.515, bf16[768,384]{1,0:T(8,128)(2,1)S(1)} %copy-done.20, bf16[1536,256]{1,0:T(8,128)(2,1)S(1)} %copy-done.13, ...), custom_call_target="tpu_custom_call" | custom-call | flops 41999998976 | bytes 5242880 | tf_op jit(solution)/shard_map/attend_back/pallas_call | solution.py:260
  1113.0 43.2 %attend_back.5 = (bf16[1,8,128,1280]{3,2,1,0:T(8,128)(2,1)}, f32[768,384]{1,0:T(8,128)S(1)}, f32[1536,256]{1,0:T(8,128)}, f32[1536,128]{1,0:T(8,128)S(1)}) custom-call(bf16[4,8,128,1280]{3,2,1,0:T(8,128)(2,1)} %bitcast.516, bf16[768,384]{1,0:T(8,128)(2,1)S(1)} %copy-done.20, bf16[1536,256]{1,0:T(8,128)(2,1)S(1)} %copy-done.13, ...), custom_call_target="tpu_custom_call" | custom-call | flops 41999998976 | bytes 5242880 | tf_op jit(solution)/shard_map/attend_back/pallas_call | solution.py:260
  1171.2 42.6 %attend_back.6 = (bf16[1,8,128,1280]{3,2,1,0:T(8,128)(2,1)}, f32[768,384]{1,0:T(8,128)S(1)}, f32[1536,256]{1,0:T(8,128)}, f32[1536,128]{1,0:T(8,128)S(1)}) custom-call(bf16[4,8,128,1280]{3,2,1,0:T(8,128)(2,1)} %bitcast.517, bf16[768,384]{1,0:T(8,128)(2,1)S(1)} %copy-done.20, bf16[1536,256]{1,0:T(8,128)(2,1)S(1)} %copy-done.13, ...), custom_call_target="tpu_custom_call" | custom-call | flops 41999998976 | bytes 5242880 | tf_op jit(solution)/shard_map/attend_back/pallas_call | solution.py:260
  1225.6 42.8 %attend_back.7 = (bf16[1,8,128,1280]{3,2,1,0:T(8,128)(2,1)}, f32[768,384]{1,0:T(8,128)S(1)}, f32[1536,256]{1,0:T(8,128)}, f32[1536,128]{1,0:T(8,128)S(1)}) custom-call(bf16[4,8,128,1280]{3,2,1,0:T(8,128)(2,1)} %bitcast.518, bf16[768,384]{1,0:T(8,128)(2,1)S(1)} %copy-done.20, bf16[1536,256]{1,0:T(8,128)(2,1)S(1)} %copy-done.13, ...), custom_call_target="tpu_custom_call" | custom-call | flops 41999998976 | bytes 5242880 | tf_op jit(solution)/shard_map/attend_back/pallas_call | solution.py:260
  1387.6 14.4 collective-permute-done.87
  (950 shorter events, 815.9 us)
Async XLA Ops:
  7.2 79.4 %all-gather.5.cloned.1.call-start = ((), (), s32[]{:S(2)}) async-start(), calls=%async_computation.3 | async-start | bytes 6082560 | tf_op jit(solution)/shard_map/all_gather | solution.py:526
  16.0 126.8 %all-gather.7.cloned.1.call-start = ((), (), s32[]{:S(2)}) async-start(), calls=%async_computation.4 | async-start | bytes 1474560 | tf_op jit(solution)/shard_map/all_gather | solution.py:474
  102.2 164.5 %all-gather.9.cloned.1.call-start = ((), (), s32[]{:S(2)}) async-start(), calls=%async_computation.5 | async-start | bytes 10813440 | tf_op jit(solution)/shard_map/all_gather | solution.py:577
  142.8 291.9 %all-gather.11.cloned.1.call-start = ((), (), s32[]{:S(2)}) async-start(), calls=%async_computation.6 | async-start | bytes 13516800 | tf_op jit(solution)/shard_map/all_gather | solution.py:582
  142.9 41.8 %collective-permute-start.2 = (bf16[480,1600]{1,0:T(8,128)(2,1)}, bf16[480,1600]{1,0:T(8,128)(2,1)}, u32[]{:S(2)}, u32[]{:S(2)}) collective-permute-start(bf16[480,1600]{1,0:T(8,128)(2,1)} %get-tuple-element.493), channel_id=1, source_target_pairs={{0,2},{1,3},{2,0},{3,1},{4,6},{5,7},{6,4},{7,5},{8,10},{9,11},{10,... | collective-permute-start | bytes 4608008 | tf_op jit(solution)/shard_map/ppermute | solution.py:419
  143.5 48.7 %collective-permute-start.4 = (bf16[480,1600]{1,0:T(8,128)(2,1)}, bf16[480,1600]{1,0:T(8,128)(2,1)}, u32[]{:S(2)}, u32[]{:S(2)}) collective-permute-start(bf16[480,1600]{1,0:T(8,128)(2,1)} %get-tuple-element.492), channel_id=1, source_target_pairs={{0,4},{1,5},{2,6},{3,7},{4,0},{5,1},{6,2},{7,3},{8,12},{9,13},{10,... | collective-permute-start | bytes 4608008 | tf_op jit(solution)/shard_map/ppermute | solution.py:419
  144.9 81.8 %collective-permute-start.3 = (bf16[480,1600]{1,0:T(8,128)(2,1)}, bf16[480,1600]{1,0:T(8,128)(2,1)}, u32[]{:S(2)}, u32[]{:S(2)}) collective-permute-start(bf16[480,1600]{1,0:T(8,128)(2,1)} %collective-permute-done), channel_id=1, source_target_pairs={{0,2},{1,3},{2,0},{3,1},{4,6},{5,7},{6,4},{7,5},{8,10},{9,11},{10,... | collective-permute-start | bytes 4608008 | tf_op jit(solution)/shard_map/ppermute | solution.py:419
  145.5 81.3 %collective-permute-start.5 = (bf16[480,1600]{1,0:T(8,128)(2,1)}, bf16[480,1600]{1,0:T(8,128)(2,1)}, u32[]{:S(2)}, u32[]{:S(2)}) collective-permute-start(bf16[480,1600]{1,0:T(8,128)(2,1)} %collective-permute-done.1), channel_id=1, source_target_pairs={{0,4},{1,5},{2,6},{3,7},{4,0},{5,1},{6,2},{7,3},{8,12},{9,13},{10,... | collective-permute-start | bytes 4608008 | tf_op jit(solution)/shard_map/ppermute | solution.py:419
  266.7 1307.8 %reduce-scatter.8.cloned.1.call-start = ((), (), s32[]{:S(2)}) async-start(), calls=%async_computation.9 | async-start | bytes 9584640 | tf_op jit(solution)/shard_map/reduce_scatter | solution.py:720
  292.2 112.8 %collective-permute-start.8 = (bf16[480,1600]{1,0:T(8,128)(2,1)}, bf16[480,1600]{1,0:T(8,128)(2,1)}, u32[]{:S(2)}, u32[]{:S(2)}) collective-permute-start(bf16[480,1600]{1,0:T(8,128)(2,1)} %collective-permute-done), channel_id=1, source_target_pairs={{0,1},{1,0},{2,3},{3,2},{4,5},{5,4},{6,7},{7,6},{8,9},{9,8},{10,11... | collective-permute-start | bytes 4608008 | tf_op jit(solution)/shard_map/ppermute | solution.py:419
  303.8 93.3 %collective-permute-start.7 = (bf16[480,1600]{1,0:T(8,128)(2,1)}, bf16[480,1600]{1,0:T(8,128)(2,1)}, u32[]{:S(2)}, u32[]{:S(2)}) collective-permute-start(bf16[480,1600]{1,0:T(8,128)(2,1)} %collective-permute-done.2), channel_id=1, source_target_pairs={{0,1},{1,0},{2,3},{3,2},{4,5},{5,4},{6,7},{7,6},{8,9},{9,8},{10,11... | collective-permute-start | bytes 4608008 | tf_op jit(solution)/shard_map/ppermute | solution.py:419
  304.1 102.7 %collective-permute-start.12 = (bf16[480,1600]{1,0:T(8,128)(2,1)}, bf16[480,1600]{1,0:T(8,128)(2,1)}, u32[]{:S(2)}, u32[]{:S(2)}) collective-permute-start(bf16[480,1600]{1,0:T(8,128)(2,1)} %collective-permute-done.4), channel_id=1, source_target_pairs={{0,1},{1,0},{2,3},{3,2},{4,5},{5,4},{6,7},{7,6},{8,9},{9,8},{10,11... | collective-permute-start | bytes 4608008 | tf_op jit(solution)/shard_map/ppermute | solution.py:419
  304.3 108.2 %collective-permute-start.9 = (bf16[480,1600]{1,0:T(8,128)(2,1)}, bf16[480,1600]{1,0:T(8,128)(2,1)}, u32[]{:S(2)}, u32[]{:S(2)}) collective-permute-start(bf16[480,1600]{1,0:T(8,128)(2,1)} %collective-permute-done.3), channel_id=1, source_target_pairs={{0,1},{1,0},{2,3},{3,2},{4,5},{5,4},{6,7},{7,6},{8,9},{9,8},{10,11... | collective-permute-start | bytes 4608008 | tf_op jit(solution)/shard_map/ppermute | solution.py:419
  304.6 109.8 %collective-permute-start.13 = (bf16[480,1600]{1,0:T(8,128)(2,1)}, bf16[480,1600]{1,0:T(8,128)(2,1)}, u32[]{:S(2)}, u32[]{:S(2)}) collective-permute-start(bf16[480,1600]{1,0:T(8,128)(2,1)} %collective-permute-done.5), channel_id=1, source_target_pairs={{0,1},{1,0},{2,3},{3,2},{4,5},{5,4},{6,7},{7,6},{8,9},{9,8},{10,11... | collective-permute-start | bytes 4608008 | tf_op jit(solution)/shard_map/ppermute | solution.py:419
  1031.8 545.3 %reduce-scatter.4.cloned.1.call-start = ((), (), s32[]{:S(2)}) async-start(), calls=%async_computation.7 | async-start | bytes 9584640 | tf_op jit(solution)/shard_map/reduce_scatter | solution.py:718
  1064.2 92.1 %collective-permute-start.64 = (bf16[2,2,320,640]{3,2,0,1:T(8,128)(2,1)}, bf16[2,2,320,640]{3,2,0,1:T(8,128)(2,1)}, u32[]{:S(2)}, u32[]{:S(2)}) collective-permute-start(bf16[2,2,320,640]{3,2,0,1:T(8,128)(2,1)} %bitcast.493), channel_id=1, source_target_pairs={{0,1},{1,0},{2,3},{3,2},{4,5},{5,4},{6,7},{7,6},{8,9},{9,8},{10,11... | collective-permute-start | bytes 4915208 | tf_op jit(solution)/shard_map/ppermute | solution.py:419
  1065.5 90.7 %collective-permute-start.62 = (bf16[2,2,320,640]{3,2,1,0:T(8,128)(2,1)}, bf16[2,2,320,640]{3,2,1,0:T(8,128)(2,1)}, u32[]{:S(2)}, u32[]{:S(2)}) collective-permute-start(bf16[2,2,320,640]{3,2,1,0:T(8,128)(2,1)} %dynamic-slice_bitcast_fusion.2), channel_id=1, source_target_pairs={{0,1},{1,0},{2,3},{3,2},{4,5},{5,4},{6,7},{7,6},{8,9},{9,8},{10,11... | collective-permute-start | bytes 4915208 | tf_op jit(solution)/shard_map/ppermute | solution.py:419
  1067.4 88.8 %collective-permute-start.63 = (bf16[2,2,320,640]{3,2,1,0:T(8,128)(2,1)}, bf16[2,2,320,640]{3,2,1,0:T(8,128)(2,1)}, u32[]{:S(2)}, u32[]{:S(2)}) collective-permute-start(bf16[2,2,320,640]{3,2,1,0:T(8,128)(2,1)} %dynamic-slice_bitcast_fusion.1), channel_id=1, source_target_pairs={{0,1},{1,0},{2,3},{3,2},{4,5},{5,4},{6,7},{7,6},{8,9},{9,8},{10,11... | collective-permute-start | bytes 4915208 | tf_op jit(solution)/shard_map/ppermute | solution.py:419
  1068.8 87.5 %collective-permute-start.65 = (bf16[2,2,320,640]{3,2,1,0:T(8,128)(2,1)}, bf16[2,2,320,640]{3,2,1,0:T(8,128)(2,1)}, u32[]{:S(2)}, u32[]{:S(2)}) collective-permute-start(bf16[2,2,320,640]{3,2,1,0:T(8,128)(2,1)} %dynamic-slice_bitcast_fusion), channel_id=1, source_target_pairs={{0,1},{1,0},{2,3},{3,2},{4,5},{5,4},{6,7},{7,6},{8,9},{9,8},{10,11... | collective-permute-start | bytes 4915208 | tf_op jit(solution)/shard_map/ppermute | solution.py:419
  1158.5 55.4 %collective-permute-start.69 = (bf16[2,320,640]{2,1,0:T(8,128)(2,1)S(1)}, bf16[2,320,640]{2,1,0:T(8,128)(2,1)}, u32[]{:S(2)}, u32[]{:S(2)}) collective-permute-start(bf16[2,320,640]{2,1,0:T(8,128)(2,1)S(1)} %dynamic-slice_bitcast_fusion.5), channel_id=1, source_target_pairs={{0,4},{1,5},{2,6},{3,7},{4,0},{5,1},{6,2},{7,3},{8,12},{9,13},{10,... | collective-permute-start | bytes 2457608 | tf_op jit(solution)/shard_map/ppermute | solution.py:419
  1162.5 51.3 %collective-permute-start.68 = (bf16[2,320,640]{2,1,0:T(8,128)(2,1)}, bf16[2,320,640]{2,1,0:T(8,128)(2,1)}, u32[]{:S(2)}, u32[]{:S(2)}) collective-permute-start(bf16[2,320,640]{2,1,0:T(8,128)(2,1)} %dynamic-slice_bitcast_fusion.6), channel_id=1, source_target_pairs={{0,2},{1,3},{2,0},{3,1},{4,6},{5,7},{6,4},{7,5},{8,10},{9,11},{10,... | collective-permute-start | bytes 2457608 | tf_op jit(solution)/shard_map/ppermute | solution.py:419
  1166.5 47.4 %collective-permute-start.67 = (bf16[2,320,640]{2,1,0:T(8,128)(2,1)}, bf16[2,320,640]{2,1,0:T(8,128)(2,1)}, u32[]{:S(2)}, u32[]{:S(2)}) collective-permute-start(bf16[2,320,640]{2,1,0:T(8,128)(2,1)} %dynamic-slice_bitcast_fusion.7), channel_id=1, source_target_pairs={{0,4},{1,5},{2,6},{3,7},{4,0},{5,1},{6,2},{7,3},{8,12},{9,13},{10,... | collective-permute-start | bytes 2457608 | tf_op jit(solution)/shard_map/ppermute | solution.py:419
  1170.1 43.7 %collective-permute-start.66 = (bf16[2,320,640]{2,1,0:T(8,128)(2,1)}, bf16[2,320,640]{2,1,0:T(8,128)(2,1)}, u32[]{:S(2)}, u32[]{:S(2)}) collective-permute-start(bf16[2,320,640]{2,1,0:T(8,128)(2,1)} %dynamic-slice_bitcast_fusion.8), channel_id=1, source_target_pairs={{0,2},{1,3},{2,0},{3,1},{4,6},{5,7},{6,4},{7,5},{8,10},{9,11},{10,... | collective-permute-start | bytes 2457608 | tf_op jit(solution)/shard_map/ppermute | solution.py:419
  1216.3 57.0 %collective-permute-start.73 = (bf16[320,640]{1,0:T(8,128)(2,1)}, bf16[320,640]{1,0:T(8,128)(2,1)S(1)}, u32[]{:S(2)}, u32[]{:S(2)}) collective-permute-start(bf16[320,640]{1,0:T(8,128)(2,1)} %dynamic-slice_bitcast_fusion.17), channel_id=1, source_target_pairs={{0,2},{1,3},{2,0},{3,1},{4,6},{5,7},{6,4},{7,5},{8,10},{9,11},{10,... | collective-permute-start | bytes 1228808 | tf_op jit(solution)/shard_map/ppermute | solution.py:419
  1219.6 53.7 %collective-permute-start.72 = (bf16[320,640]{1,0:T(8,128)(2,1)}, bf16[320,640]{1,0:T(8,128)(2,1)}, u32[]{:S(2)}, u32[]{:S(2)}) collective-permute-start(bf16[320,640]{1,0:T(8,128)(2,1)} %dynamic-slice_bitcast_fusion.18), channel_id=1, source_target_pairs={{0,4},{1,5},{2,6},{3,7},{4,0},{5,1},{6,2},{7,3},{8,12},{9,13},{10,... | collective-permute-start | bytes 1228808 | tf_op jit(solution)/shard_map/ppermute | solution.py:419
  1222.2 51.1 %collective-permute-start.71 = (bf16[320,640]{1,0:T(8,128)(2,1)S(1)}, bf16[320,640]{1,0:T(8,128)(2,1)S(1)}, u32[]{:S(2)}, u32[]{:S(2)}) collective-permute-start(bf16[320,640]{1,0:T(8,128)(2,1)S(1)} %dynamic-slice_bitcast_fusion.19), channel_id=1, source_target_pairs={{0,2},{1,3},{2,0},{3,1},{4,6},{5,7},{6,4},{7,5},{8,10},{9,11},{10,... | collective-permute-start | bytes 1228808 | tf_op jit(solution)/shard_map/ppermute | solution.py:419
  1224.6 48.7 %collective-permute-start.70 = (bf16[320,640]{1,0:T(8,128)(2,1)S(1)}, bf16[320,640]{1,0:T(8,128)(2,1)S(1)}, u32[]{:S(2)}, u32[]{:S(2)}) collective-permute-start(bf16[320,640]{1,0:T(8,128)(2,1)S(1)} %dynamic-slice_bitcast_fusion.20), channel_id=1, source_target_pairs={{0,4},{1,5},{2,6},{3,7},{4,0},{5,1},{6,2},{7,3},{8,12},{9,13},{10,... | collective-permute-start | bytes 1228808 | tf_op jit(solution)/shard_map/ppermute | solution.py:419
  1273.2 51.5 %collective-permute-start.78 = (bf16[2,2,128,1280]{3,2,0,1:T(8,128)(2,1)}, bf16[2,2,128,1280]{3,2,0,1:T(8,128)(2,1)}, u32[]{:S(2)}, u32[]{:S(2)}) collective-permute-start(bf16[2,2,128,1280]{3,2,0,1:T(8,128)(2,1)} %bitcast.495), channel_id=1, source_target_pairs={{0,1},{1,0},{2,3},{3,2},{4,5},{5,4},{6,7},{7,6},{8,9},{9,8},{10,11... | collective-permute-start | bytes 3932168 | tf_op jit(solution)/shard_map/ppermute | solution.py:419
  1283.3 61.1 %collective-permute-start.79 = (bf16[2,2,128,1280]{3,2,1,0:T(8,128)(2,1)}, bf16[2,2,128,1280]{3,2,1,0:T(8,128)(2,1)}, u32[]{:S(2)}, u32[]{:S(2)}) collective-permute-start(bf16[2,2,128,1280]{3,2,1,0:T(8,128)(2,1)} %dynamic-slice_bitcast_fusion.4), channel_id=1, source_target_pairs={{0,1},{1,0},{2,3},{3,2},{4,5},{5,4},{6,7},{7,6},{8,9},{9,8},{10,11... | collective-permute-start | bytes 3932168 | tf_op jit(solution)/shard_map/ppermute | solution.py:419
  1285.9 58.4 %collective-permute-start.80 = (bf16[2,2,128,1280]{3,2,0,1:T(8,128)(2,1)}, bf16[2,2,128,1280]{3,2,0,1:T(8,128)(2,1)}, u32[]{:S(2)}, u32[]{:S(2)}) collective-permute-start(bf16[2,2,128,1280]{3,2,0,1:T(8,128)(2,1)} %bitcast.494), channel_id=1, source_target_pairs={{0,1},{1,0},{2,3},{3,2},{4,5},{5,4},{6,7},{7,6},{8,9},{9,8},{10,11... | collective-permute-start | bytes 3932168 | tf_op jit(solution)/shard_map/ppermute | solution.py:419
  1292.1 52.2 %collective-permute-start.81 = (bf16[2,2,128,1280]{3,2,1,0:T(8,128)(2,1)}, bf16[2,2,128,1280]{3,2,1,0:T(8,128)(2,1)}, u32[]{:S(2)}, u32[]{:S(2)}) collective-permute-start(bf16[2,2,128,1280]{3,2,1,0:T(8,128)(2,1)} %dynamic-slice_bitcast_fusion.3), channel_id=1, source_target_pairs={{0,1},{1,0},{2,3},{3,2},{4,5},{5,4},{6,7},{7,6},{8,9},{9,8},{10,11... | collective-permute-start | bytes 3932168 | tf_op jit(solution)/shard_map/ppermute | solution.py:419
  1341.4 238.4 %reduce-scatter.6.cloned.1.call-start = ((), (), s32[]{:S(2)}) async-start(), calls=%async_computation.8 | async-start | bytes 9584640 | tf_op jit(solution)/shard_map/reduce_scatter | solution.py:719
  (300 other events, 4785.1 us)
Sparse Core Ops, SparseCore 0:
  16.1 70.3 all-gather.4
  102.3 29.0 all-gather.6
  143.0 123.6 all-gather.8
  269.4 96.6 all-gather.10
  1031.9 72.5 reduce-scatter.7
  1341.5 94.3 reduce-scatter.3
  1481.0 80.9 reduce-scatter.5

commit v3 on v2

--- a/solution.py
+++ b/solution.py
@@ -139,20 +139,19 @@
 
 def attend_back_kernel(
     query_rows, tile, weights_ref, query_t_ref, latent_ref, latent_t_ref, rope_ref, cos_ref,
-    sin_ref, bias_ref, mixed_ref, grad_ref, lse_ref,
-    weights_grad_ref, query_grad_ref, latent_grad_ref, rope_grad_ref,
-    query_acc, latent_acc, rope_acc, both_scr,
+    sin_ref, bias_ref, mixed_ref, grad_ref, lse_ref, query_before_ref, latent_before_ref, *rest,
 ):
+    weights_grad_ref, query_acc, latent_acc, both_scr = rest[-4:]
     head = pl.program_id(0)
+    kv_rank = latent_ref.shape[1]
     query_w, latent_w, query_t, keys, both = head_vectors(
         weights_ref, query_t_ref, latent_ref, rope_ref, cos_ref, sin_ref, query_rows
     )
 
     @pl.when(head == 0)
     def _():
-        query_acc[...] = jnp.zeros_like(query_acc)
-        latent_acc[...] = jnp.zeros_like(latent_acc)
-        rope_acc[...] = jnp.zeros_like(rope_acc)
+        query_acc[...] = query_before_ref[...]
+        latent_acc[...] = latent_before_ref[...]
 
     keys_t = keys.T
     query = query_t.T
@@ -176,7 +175,7 @@
         key_back = dot_plain(score_grad, query) * SCALE
         value_back = dot_plain(probs.astype(BF), grad_pad)
         lane = lax.broadcasted_iota(jnp.int32, key_back.shape, 1)
-        rope_acc[rows, :] += key_back
+        latent_acc[rows, kv_rank:] += key_back
         both_scr[rows, :] = jnp.where(lane < NOPE, key_back, value_back).astype(BF)
     query_back_t = query_back_t * SCALE
     half = ROPE // 2
@@ -193,26 +192,21 @@
     ).astype(BF)
     both_back = both_scr[...]
     query_acc[...] += dot_plain(query_w, query_back_t)
-    latent_acc[...] += dot_trans_right(both_back, latent_w)
+    latent_acc[:, :kv_rank] += dot_trans_right(both_back, latent_w)
     query_wg = dot_trans_right(query_t_ref[...], query_back_t)
     latent_wg = dot_plain(latent_t_ref[...], both_back)
     col_total = weights_ref.shape[1]
     weights_grad_ref[0, :, :query_rows, :] = query_wg.astype(BF).reshape(col_total, query_rows, HEAD)
     weights_grad_ref[0, :, query_rows:, :] = latent_wg.astype(BF).reshape(col_total, -1, HEAD)
 
-    @pl.when(head == pl.num_programs(0) - 1)
-    def _():
-        query_grad_ref[...] = query_acc[...]
-        latent_grad_ref[...] = latent_acc[...]
-        rope_grad_ref[...] = rope_acc[...]
-
 
 def whole(shape):
     return pl.BlockSpec(shape, lambda head: (0,) * len(shape))
 
 
 def attend(weights, query_t, latent, rope, cos_t, sin_t, bias_t, query_rows, block):
-    _, col_total, pack_rows, pack_cols = weights.shape
+    _, col_total, _, pack_cols = weights.shape
+    pack_rows = query_rows + latent.shape[1] // col_total
     heads = pack_cols // HEAD
     length, local = bias_t.shape
     tile = math.gcd(length, 256)
@@ -251,9 +245,11 @@
 
 def attend_back(
     weights, query_t, latent, latent_t, rope, cos_t, sin_t, bias_t, mixed_t, grad_t, lse,
-    query_rows, block,
+    query_before, latent_before, weights_before, query_rows, block,
 ):
-    _, col_total, pack_rows, pack_cols = weights.shape
+    row_total, col_total, _, pack_cols = weights.shape
+    more = [] if weights_before is None else [weights_before]
+    pack_rows = query_rows + latent.shape[1] // col_total
     heads = pack_cols // HEAD
     length, local = bias_t.shape
     tile = math.gcd(length, 256)
@@ -272,25 +268,22 @@
             pl.BlockSpec((VDIM, local), lambda head: (head, 0)),
             pl.BlockSpec((VDIM, local), lambda head: (block * heads + head, 0)),
             pl.BlockSpec((1, 1, local), lambda head: (head, 0, 0)),
-        ],
+            whole(query_before.shape),
+            whole(latent_before.shape),
+        ]
+        + [pl.BlockSpec(memory_space=pl.ANY)] * len(more),
         out_specs=[
-            pl.BlockSpec((1, col_total, pack_rows, HEAD), lambda head: (0, 0, 0, head)),
-            whole(query_t.shape),
-            whole(latent.shape),
-            whole(rope.shape),
+            pl.BlockSpec((1, col_total, pack_rows, HEAD), lambda head: (block, 0, 0, head)),
+            whole(query_before.shape),
+            whole(latent_before.shape),
         ],
         out_shape=[
-            jax.ShapeDtypeStruct((1,) + weights.shape[1:], BF),
-            jax.ShapeDtypeStruct(query_t.shape, F32),
-            jax.ShapeDtypeStruct(latent.shape, F32),
-            jax.ShapeDtypeStruct(rope.shape, F32),
-        ],
-        scratch_shapes=[
-            pltpu.VMEM(query_t.shape, F32),
-            pltpu.VMEM(latent.shape, F32),
-            pltpu.VMEM(rope.shape, F32),
-            pltpu.VMEM((length, HEAD), BF),
-        ],
+            jax.ShapeDtypeStruct((row_total, col_total, pack_rows, pack_cols), BF),
+            jax.ShapeDtypeStruct(query_before.shape, F32),
+            jax.ShapeDtypeStruct(latent_before.shape, F32),
+        ],
+        input_output_aliases={13: 0} if more else {},
+        scratch_shapes=[pltpu.VMEM((length, HEAD), BF)],
         compiler_params=pltpu.CompilerParams(
             dimension_semantics=("arbitrary",), vmem_limit_bytes=48 * 1024 * 1024
         ),
@@ -300,7 +293,8 @@
             transcendentals=heads * local * length,
         ),
         name="attend_back",
-    )(weights, query_t, latent, latent_t, rope, cos_t, sin_t, bias_t, mixed_t, grad_t, lse)
+    )(weights, query_t, latent, latent_t, rope, cos_t, sin_t, bias_t, mixed_t, grad_t, lse,
+      query_before, latent_before, *more)
 
 
 def weight_grad_kernel(chunks, *refs):
@@ -336,6 +330,357 @@
     )(*lefts, *rights)
 
 
+MESH = pl.DeviceIdType.MESH
+
+
+def out_grad_kernel(tokens_ref, mixed_ref, out_ref):
+    out_ref[0] = dot_trans_right(tokens_ref[...].T, mixed_ref[...]).astype(BF)
+
+
+def out_weight_grad(tokens, mixed):
+    rows, width = tokens.shape
+    row_total, units, _ = mixed.shape
+    tile = math.gcd(width, 512)
+    return pl.pallas_call(
+        out_grad_kernel,
+        grid=(row_total, width // tile),
+        in_specs=[
+            pl.BlockSpec((rows, tile), lambda block, step: (0, step)),
+            pl.BlockSpec((None, units, rows), lambda block, step: (block, 0, 0)),
+        ],
+        out_specs=pl.BlockSpec((1, tile, units), lambda block, step: (block, step, 0)),
+        out_shape=jax.ShapeDtypeStruct((row_total, width, units), BF),
+        cost_estimate=pl.CostEstimate(
+            flops=2 * rows * width * units * row_total,
+            bytes_accessed=2 * row_total * width * units,
+            transcendentals=0,
+        ),
+        name="out_wg",
+    )(tokens, mixed)
+
+
+def flip(index, bit):
+    return index + bit - 2 * bit * lax.rem(index // bit, 2)
+
+
+def chip_bits(col_total):
+    bits, bit = [], 2
+    while bit < col_total:
+        bits.append(bit)
+        bit *= 2
+    return bits
+
+
+def turn_bit(bits, row, step, row_total):
+    turn = lax.rem(step + (row * len(bits)) // row_total, len(bits))
+    return sum(jnp.where(turn == at, bit, 0) for at, bit in enumerate(bits))
+
+
+def greet(row_total, row_rank, col_rank, bits):
+    barrier = pltpu.get_barrier_semaphore()
+    for bit in [1] + bits:
+        pl.semaphore_signal(
+            barrier, inc=1, device_id=(row_rank, flip(col_rank, bit)), device_id_type=MESH
+        )
+
+    @pl.when(row_rank > 0)
+    def _():
+        pl.semaphore_signal(barrier, inc=1, device_id=(row_rank - 1, col_rank), device_id_type=MESH)
+
+    @pl.when(row_rank < row_total - 1)
+    def _():
+        pl.semaphore_signal(barrier, inc=1, device_id=(row_rank + 1, col_rank), device_id_type=MESH)
+
+    beside = lax.min(row_rank, 1) + lax.min(row_total - 1 - row_rank, 1)
+    pl.semaphore_wait(barrier, 1 + len(bits) + beside)
+
+
+def gather_kernel(
+    row_total, col_total, own_ref, out_ref, own_sem, line_send, line_recv, chip_send, chip_recv,
+    core_send, core_recv,
+):
+    row_rank, col_rank = lax.axis_index("row"), lax.axis_index("col")
+    bits = chip_bits(col_total)
+    masks = 2 ** len(bits)
+    own = pltpu.make_async_copy(own_ref, out_ref.at[row_rank, col_rank], own_sem)
+    own.start()
+    greet(row_total, row_rank, col_rank, bits)
+    own.wait()
+
+    def block_col(row, mask):
+        index = col_rank
+        for step in range(len(bits)):
+            if mask >> step & 1:
+                index = flip(index, turn_bit(bits, row, step, row_total))
+        return index
+
+    def line_copy(way, row):
+        ref = out_ref.at[row, col_rank]
+        return pltpu.make_async_remote_copy(
+            src_ref=ref, dst_ref=ref, send_sem=line_send.at[way, row], recv_sem=line_recv.at[row],
+            device_id=(row_rank + 1 - 2 * way, col_rank), device_id_type=MESH,
+        )
+
+    def chip_copy(row, mask, step):
+        ref = out_ref.at[row, block_col(row, mask)]
+        to = mask + 2**step
+        return pltpu.make_async_remote_copy(
+            src_ref=ref, dst_ref=ref, send_sem=chip_send.at[row, to], recv_sem=chip_recv.at[row, to],
+            device_id=(row_rank, flip(col_rank, turn_bit(bits, row, step, row_total))),
+            device_id_type=MESH,
+        )
+
+    def core_copy(row, mask):
+        ref = out_ref.at[row, block_col(row, mask)]
+        return pltpu.make_async_remote_copy(
+            src_ref=ref, dst_ref=ref, send_sem=core_send.at[row, mask],
+            recv_sem=core_recv.at[row, mask], device_id=(row_rank, flip(col_rank, 1)),
+            device_id_type=MESH,
+        )
+
+    def by_distance(act):
+        for away in range(row_total):
+            for side in (0,) if away == 0 else (-1, 1):
+                row = row_rank + side * away
+
+                @pl.when((row >= 0) & (row < row_total))
+                def _():
+                    act(row, away, side)
+
+    def arrive(row, away, side):
+        if away > 0:
+            line_copy(0, row).wait_recv()
+        if side <= 0:
+
+            @pl.when(row_rank < row_total - 1)
+            def _():
+                line_copy(0, row).start()
+
+        if side >= 0:
+
+            @pl.when(row_rank > 0)
+            def _():
+                line_copy(1, row).start()
+
+        for step in range(len(bits)):
+            chip_copy(row, 0, step).start()
+        core_copy(row, 0).start()
+
+    by_distance(arrive)
+    for mask in range(1, masks):
+        top = mask.bit_length() - 1
+
+        def forward(row, away, side):
+            chip_copy(row, mask - 2**top, top).wait_recv()
+            for step in range(top + 1, len(bits)):
+                chip_copy(row, mask, step).start()
+            core_copy(row, mask).start()
+
+        by_distance(forward)
+    for row in range(row_total):
+        for mask in range(masks):
+            core_copy(row, mask).wait()
+            if mask > 0:
+                top = mask.bit_length() - 1
+                chip_copy(row, mask - 2**top, top).wait_send()
+
+        @pl.when((row <= row_rank) & (row_rank < row_total - 1))
+        def _():
+            line_copy(0, row).wait_send()
+
+        @pl.when((row >= row_rank) & (row_rank > 0))
+        def _():
+            line_copy(1, row).wait_send()
+
+
+def gather_all(values, collective_id, name):
+    row_total, col_total = lax.axis_size("row"), lax.axis_size("col")
+    masks = 2 ** len(chip_bits(col_total))
+    return pl.pallas_call(
+        functools.partial(gather_kernel, row_total, col_total),
+        in_specs=[pl.BlockSpec(memory_space=pl.ANY)],
+        out_specs=pl.BlockSpec(memory_space=pl.ANY),
+        out_shape=jax.ShapeDtypeStruct((row_total, col_total) + values.shape, values.dtype),
+        scratch_shapes=[
+            pltpu.SemaphoreType.DMA,
+            pltpu.SemaphoreType.DMA((2, row_total)),
+            pltpu.SemaphoreType.DMA((row_total,)),
+            pltpu.SemaphoreType.DMA((row_total, masks)),
+            pltpu.SemaphoreType.DMA((row_total, masks)),
+            pltpu.SemaphoreType.DMA((row_total, masks)),
+            pltpu.SemaphoreType.DMA((row_total, masks)),
+        ],
+        compiler_params=pltpu.CompilerParams(
+            collective_id=collective_id, has_side_effects=True
+        ),
+        name=name,
+    )(values)
+
+
+def add_into(total_ref, other_ref):
+    rows = total_ref.shape[0]
+    tile = math.gcd(rows, 32)
+
+    def one(step, carry):
+        here = pl.ds(pl.multiple_of(step * tile, tile), tile)
+        total = total_ref[here, :].astype(F32) + other_ref[here, :].astype(F32)
+        total_ref[here, :] = total.astype(total_ref.dtype)
+        return carry
+
+    lax.fori_loop(0, rows // tile, one, 0)
+
+
+class LineReduce:
+    def __init__(self, row_total, row_rank, col_rank, block, landed, send, recv):
+        self.row_total, self.row_rank, self.col_rank = row_total, row_rank, col_rank
+        self.block, self.landed, self.send, self.recv = block, landed, send, recv
+
+    def copy(self, way, row):
+        return pltpu.make_async_remote_copy(
+            src_ref=self.block(row), dst_ref=self.landed.at[way, row],
+            send_sem=self.send.at[way, row], recv_sem=self.recv.at[way, row],
+            device_id=(self.row_rank + 1 - 2 * way, self.col_rank), device_id_type=MESH,
+        )
+
+    def run(self):
+        last = self.row_total - 1
+        for step in range(last):
+            for way, row in ((0, last - step), (1, step)):
+                sends = self.row_rank < row if way == 0 else self.row_rank > row
+                gets = self.row_rank > 0 if way == 0 else self.row_rank < last
+
+                @pl.when(sends)
+                def _():
+                    @pl.when(gets)
+                    def _():
+                        self.copy(way, row).wait_recv()
+                        add_into(self.block(row), self.landed.at[way, row])
+
+                    self.copy(way, row).start()
+
+        for way, gets in ((0, self.row_rank > 0), (1, self.row_rank < last)):
+
+            @pl.when(gets)
+            def _():
+                self.copy(way, self.row_rank).wait_recv()
+                add_into(self.block(self.row_rank), self.landed.at[way, self.row_rank])
+
+    def finish(self, out_ref):
+        rows = out_ref.shape[0]
+        tile = math.gcd(rows, 32)
+        own = self.block(self.row_rank)
+
+        def one(step, carry):
+            here = pl.ds(pl.multiple_of(step * tile, tile), tile)
+            out_ref[here, :] = own[here, :].astype(out_ref.dtype)
+            return carry
+
+        lax.fori_loop(0, rows // tile, one, 0)
+        for row in range(self.row_total):
+            for way, sends in ((0, self.row_rank < row), (1, self.row_rank > row)):
+
+                @pl.when(sends)
+                def _():
+                    self.copy(way, row).wait_send()
+
+
+def reduce_kernel(
+    row_total, col_total, part_ref, out_ref, sums, chip_buf, line_buf, core_send, core_recv,
+    chip_send, chip_recv, line_send, line_recv,
+):
+    row_rank, col_rank = lax.axis_index("row"), lax.axis_index("col")
+    bits = chip_bits(col_total)
+    count = len(bits)
+    masks = 2**count
+    core = lax.rem(col_rank, 2)
+    greet(row_total, row_rank, col_rank, bits)
+
+    def order(row):
+        turn = (row * count) // row_total
+        return bits[turn:] + bits[:turn]
+
+    def chip_at(row, mask):
+        index = col_rank // 2
+        for step, bit in enumerate(order(row)):
+            if mask >> step & 1:
+                index = flip(index, bit // 2)
+        return index
+
+    def core_copy(row, mask):
+        return pltpu.make_async_remote_copy(
+            src_ref=part_ref.at[row, chip_at(row, mask), 1 - core], dst_ref=sums.at[row, mask],
+            send_sem=core_send.at[row, mask], recv_sem=core_recv.at[row, mask],
+            device_id=(row_rank, flip(col_rank, 1)), device_id_type=MESH,
+        )
+
+    def chip_copy(row, mask, step):
+        return pltpu.make_async_remote_copy(
+            src_ref=sums.at[row, mask], dst_ref=chip_buf.at[row, mask],
+            send_sem=chip_send.at[row, mask], recv_sem=chip_recv.at[row, mask],
+            device_id=(row_rank, flip(col_rank, order(row)[step])), device_id_type=MESH,
+        )
+
+    for mask in range(masks - 1, -1, -1):
+        for row in range(row_total):
+            core_copy(row, mask).start()
+    for mask in range(masks - 1, -1, -1):
+        for row in range(row_total):
+            core_copy(row, mask).wait_recv()
+            add_into(sums.at[row, mask], part_ref.at[row, chip_at(row, mask), core])
+            if mask >= masks // 2:
+                chip_copy(row, mask, count - 1).start()
+    for step in range(count - 1, -1, -1):
+        half = 2**step
+        for mask in range(half - 1, -1, -1):
+            for row in range(row_total):
+                chip_copy(row, mask + half, step).wait_recv()
+                add_into(sums.at[row, mask], chip_buf.at[row, mask + half])
+                if step > 0 and mask >= half // 2:
+                    chip_copy(row, mask, step - 1).start()
+    line = LineReduce(
+        row_total, row_rank, col_rank, lambda row: sums.at[row, 0], line_buf, line_send, line_recv
+    )
+    line.run()
+    line.finish(out_ref)
+    for row in range(row_total):
+        for mask in range(masks):
+            core_copy(row, mask).wait_send()
+            if mask > 0:
+                chip_copy(row, mask, mask.bit_length() - 1).wait_send()
+
+
+def reduce_all(parts, collective_id, name):
+    row_total, col_total, own_rows, lanes = parts.shape
+    rows = -(-own_rows // 16) * 16
+    if rows != own_rows:
+        parts = jnp.pad(parts, ((0, 0), (0, 0), (0, rows - own_rows), (0, 0)))
+    parts = parts.reshape(row_total, col_total // 2, 2, rows, lanes)
+    masks = col_total // 2
+    sem = pltpu.SemaphoreType.DMA
+    vmem = pl.BlockSpec(memory_space=pltpu.VMEM)
+    return pl.pallas_call(
+        functools.partial(reduce_kernel, row_total, col_total),
+        in_specs=[vmem],
+        out_specs=vmem,
+        out_shape=jax.ShapeDtypeStruct((rows, lanes), F32),
+        scratch_shapes=[
+            pltpu.VMEM((row_total, masks, rows, lanes), BF),
+            pltpu.VMEM((row_total, masks, rows, lanes), BF),
+            pltpu.VMEM((2, row_total, rows, lanes), BF),
+            sem((row_total, masks)),
+            sem((row_total, masks)),
+            sem((row_total, masks)),
+            sem((row_total, masks)),
+            sem((2, row_total)),
+            sem((2, row_total)),
+        ],
+        compiler_params=pltpu.CompilerParams(
+            collective_id=collective_id, has_side_effects=True, vmem_limit_bytes=48 * 1024 * 1024
+        ),
+        name=name,
+    )(parts)[:own_rows]
+
+
 together = lax.optimization_barrier
 
 
@@ -350,6 +695,10 @@
             except StopIteration as stop:
                 self.value, self.over = stop.value, True
         return ()
+
+    def advance_into(self):
+        self.state = self.advance()
+        return not self.over
 
     def result(self):
         self.advance()
@@ -400,78 +749,11 @@
     return parts[0].astype(F32) + ways[0].astype(F32) + ways[1].astype(F32)
 
 
-def reduce_row_steps(line):
-    total = lax.axis_size("row")
-    row_rank = lax.axis_index("row")
-    parts = [pick(line, lax.rem(row_rank + total - step, total), 0) for step in range(total)]
-    return (yield from reduce_steps(parts))
-
-
 def product_steps(product):
     total = lax.axis_size("row")
     rows = product.shape[0] // total
     parts = [product[at * rows : (at + 1) * rows] for at in range(total)]
     return (yield from reduce_steps(parts))
-
-
-def swap(values, bit):
-    total = lax.axis_size("col")
-    return lax.ppermute(values, "col", [(i, i ^ bit) for i in range(total)])
-
-
-def pick(values, index, axis):
-    return lax.dynamic_index_in_dim(values, index, axis, keepdims=False)
-
-
-def far_bits():
-    bits, bit = [], 2
-    while bit < lax.axis_size("col"):
-        bits.append(bit)
-        bit *= 2
-    return bits
-
-
-def gather_col_steps(first, second):
-    halves = [[(0, first)], [(0, second)]]
-    orders = [far_bits()[::-1] + [1], far_bits() + [1]]
-    for step in range(len(orders[0])):
-        got = yield tuple(
-            tuple(swap(part, order[step]) for _, part in half)
-            for half, order in zip(halves, orders)
-        )
-        halves = [
-            half + [(away + order[step], part) for (away, _), part in zip(half, parts)]
-            for half, order, parts in zip(halves, orders, got)
-        ]
-    return halves
-
-
-def reduce_col_steps(blocks):
-    col_rank = lax.axis_index("col")
-    bits = far_bits()
-    dims = [bits[::-1] + [1] for _ in blocks]
-    orders = [[1] + (bits if at % 2 == 0 else bits[::-1]) for at in range(len(blocks))]
-    blocks = [block.reshape((2,) * len(dims[0]) + block.shape[1:]) for block in blocks]
-    for step in range(len(dims[0])):
-        keeps, sends = [], []
-        for block, dim, order in zip(blocks, dims, orders):
-            bit = order[step]
-            axis, own = dim.index(bit), lax.rem(col_rank // bit, 2)
-            keeps.append(pick(block, own, axis))
-            sends.append(swap(pick(block, 1 - own, axis), bit))
-            dim.remove(bit)
-        sends = yield tuple(sends)
-        blocks = [add_parts(keep, send) for keep, send in zip(keeps, sends)]
-    return jnp.stack(blocks)
-
-
-def reduce_all_steps(blocks):
-    line = yield from reduce_col_steps(blocks)
-    return (yield from reduce_row_steps(line))
-
-
-def token_rows(values):
-    return lax.all_gather(values, "row", axis=0, tiled=True)
 
 
 def pad_to(values, width):
@@ -523,7 +805,7 @@
         [query_down, latent_down, attn_gain[:, None], mlp_gain[:, None], misc[:, None]], axis=1
     )
     pack_wide = -(-(lat_wide + 3) // 128) * 128
-    down_all = lax.all_gather(pad_to(down_pack, pack_wide), both_axes, axis=0, tiled=True)
+    down_pack = pad_to(down_pack, pack_wide)
 
     query_pack = jnp.pad(
         query_up.reshape(query_rows, heads_here, NOPE + ROPE),
@@ -531,16 +813,19 @@
     ).reshape(query_rows, heads_here * HEAD)
     up_pack = jnp.concatenate([query_pack, latent_up], axis=0)
     pack_rows = up_pack.shape[0]
-    mlp_pack = jnp.concatenate([gate_weight, up_weight, down_weight.T], axis=0)
-    part_rows = gate_weight.shape[0]
-    half_rows = part_rows // 2
-    down_all, mlp_pack = together((down_all, mlp_pack))
-    mlp_w = Task(
-        gather_col_steps(
-            mlp_pack[: part_rows + half_rows], mlp_pack[part_rows + half_rows :]
-        )
-    )
-
+    if up_pack.shape[1] >= pack_wide:
+        head_w = gather_all(
+            jnp.concatenate([up_pack, pad_to(down_pack, up_pack.shape[1])]), 1, "gather_pack"
+        )
+        down_all = head_w[:, :, pack_rows:, :pack_wide]
+    else:
+        head_w = gather_all(up_pack, 1, "gather_up")
+        down_all = gather_all(down_pack, 2, "gather_down")
+    down_all = down_all.reshape(devices * down_rows, pack_wide)
+    down_all, out_here = together((down_all, output_weight.T))
+    out_all = lax.all_gather(out_here, both_axes, axis=0, tiled=True).reshape(
+        row_total, width, heads_here * VDIM
+    )
     attn_g = down_all[:, lat_wide].astype(F32)
     mlp_g = down_all[:, lat_wide + 1].astype(F32)
     misc_all = down_all[:, lat_wide + 2].astype(F32).reshape(devices, down_rows)
@@ -570,56 +855,45 @@
         ],
         axis=1,
     ).astype(BF)
-    latent_all = token_rows(latent_pack)
-    got = mlp_w.advance()
-    latent_all, up_pack, got = together((latent_all, up_pack, got))
-    mlp_w.state = got
-    head_w = lax.all_gather(up_pack, both_axes, axis=0, tiled=True)
-    got = mlp_w.advance()
-    head_w, out_here, got = together((head_w, output_weight.T, got))
-    mlp_w.state = got
-    head_w = head_w.reshape(row_total, col_total, pack_rows, heads_here * HEAD)
-    out_all = lax.all_gather(out_here, both_axes, axis=0, tiled=True).reshape(
-        row_total, width, heads_here * VDIM
-    )
+    latent_give = Task(gather_steps(latent_pack))
+    while latent_give.advance_into():
+        pass
+    latent_all = together(latent_give.value)
     kv_all = latent_all[:, :KV_RANK]
     rope_all = latent_all[:, KV_RANK:]
 
     query_at = offset + jnp.arange(local_rows, dtype=jnp.int32)
     query_seg = lax.dynamic_slice_in_dim(segments, offset, local_rows, 0)
-    key_at = jnp.arange(length, dtype=jnp.int32)
+    begins = [
+        lax.rem(row_rank + row_total - step, row_total) * local_rows for step in range(row_total)
+    ]
+    key_at = jnp.concatenate([begin + jnp.arange(local_rows, dtype=jnp.int32) for begin in begins])
+    key_seg = jnp.concatenate(
+        [lax.dynamic_slice_in_dim(segments, begin, local_rows, 0) for begin in begins]
+    )
     allowed_t = (key_at[:, None] <= query_at[None, :]) & (
-        (segments[:, None] == 0) | (segments[:, None] == query_seg[None, :])
+        (key_seg[:, None] == 0) | (key_seg[:, None] == query_seg[None, :])
     )
     bias_t = jnp.where(allowed_t, 0.0, HIDE).astype(F32)
     query_t = query_nb.T
     cos_t, sin_t = cos_here.T, sin_here.T
+    cut = row_total // 2
     mixed = [
         attend(head_w, query_t, kv_all, rope_all, cos_t, sin_t, bias_t, query_rows, block)
-        for block in range(row_total)
+        for block in range(cut)
     ]
-    while not mlp_w.over:
-        mlp_w.state = mlp_w.advance()
-    gate_full = jnp.zeros((col_total, part_rows, mlp_pack.shape[1]), BF)
-    up_full, down_t = gate_full, gate_full
-    col_rank = lax.axis_index("col")
-
-    def put(array, part, away, row):
-        return lax.dynamic_update_slice(
-            array, part[None], (jnp.bitwise_xor(col_rank, away), row, 0)
-        )
-
-    for (away, one), (away_b, two) in zip(*[sorted(h, key=lambda p: p[0]) for h in mlp_w.value]):
-        gate_full = put(gate_full, one[:part_rows], away, 0)
-        up_full = put(up_full, one[part_rows:], away, 0)
-        up_full = put(up_full, two[: part_rows - half_rows], away_b, half_rows)
-        down_t = put(down_t, two[part_rows - half_rows :], away_b, 0)
+    mixed, out_all, query_t, gate_here, up_here, down_here = together(
+        (mixed, out_all, query_t, gate_weight, up_weight, down_weight.T)
+    )
     gate_full, up_full, down_t = (
-        gate_full.reshape(width, -1), up_full.reshape(width, -1), down_t.reshape(width, -1)
-    )
-    mixed, out_all, gate_full, up_full, down_t = together(
-        (mixed, out_all, gate_full, up_full, down_t)
-    )
+        lax.all_gather(gate_here, "col", axis=0, tiled=True),
+        lax.all_gather(up_here, "col", axis=0, tiled=True),
+        lax.all_gather(down_here, "col", axis=0, tiled=True),
+    )
+    mixed += [
+        attend(head_w, query_t, kv_all, rope_all, cos_t, sin_t, bias_t, query_rows, block)
+        for block in range(cut, row_total)
+    ]
     attn_sum = None
     for block in range(row_total):
         term = dot_dims(mixed[block][0], out_all[block], (0,), (1,))
@@ -634,9 +908,11 @@
     parts = [slice(0, rows), slice(rows, 2 * rows)]
 
     def forward_steps(tokens):
-        gate_act = yield dot_plain(tokens, gate_full)
+        gate_act = yield dot_plain(tokens, gate_full).astype(BF)
+        gate_f = gate_act.astype(F32)
         up_act = dot_plain(tokens, up_full)
-        hidden = yield (gate_act * jax.nn.sigmoid(gate_act) * up_act).astype(BF)
+        hidden = yield (gate_f * jax.nn.sigmoid(gate_f) * up_act).astype(BF)
+        up_act = up_act.astype(BF)
         product = yield dot_trans_right(hidden, down_t).astype(BF)
         return (gate_act, up_act, hidden, product)
 
@@ -648,6 +924,7 @@
         return (out_rows.astype(BF), squared, grad_rows, (RES * grad_rows).astype(BF))
 
     def backward_steps(branch, gate_act, up_act):
+        gate_act, up_act = gate_act.astype(F32), up_act.astype(F32)
         gate_sig = jax.nn.sigmoid(gate_act)
         hidden_grad = dot_plain(branch, down_t)
         gate_grad, up_grad = yield (
@@ -668,7 +945,7 @@
     mlp_b = mlp_in.astype(BF)
     give_0, give_1 = [Task(gather_steps(mlp_b[part])) for part in parts]
     slots(hops, give_0)
-    tokens_0 = give_0.result()
+    tokens_0, gate_full, up_full = together((give_0.result(), gate_full, up_full))
     fore_0 = Task(forward_steps(tokens_0))
     slots(hops, give_1, fore_0)
     tokens_1 = give_1.result()
@@ -693,68 +970,72 @@
     slot(give_1, take_0)
     branch_1 = give_1.result()
     back_1 = Task(backward_steps(branch_1, fore_1[0], fore_1[1]))
-    slots(hops - 1, take_0, back_1)
+    down_work = Task(weight_steps([([branch_0, branch_1], [fore_0[2], fore_1[2]], "down_wg")]))
+    slot(take_0, down_work)
+    slots(hops - 2, take_0, back_1)
     grad_0 = take_0.result()
-    slot(back_1)
-    back_1 = back_1.result()
+    (down_wg,) = down_work.result()
+    while back_1.advance_into():
+        pass
+    back_1 = back_1.value
     take_1 = Task(product_steps(back_1[2]))
     work = Task(
         weight_steps(
             [
-                ([branch_0, branch_1], [fore_0[2], fore_1[2]], "down_wg"),
                 ([tokens_0, tokens_1], [back_0[0], back_1[0]], "gate_wg"),
                 ([tokens_0, tokens_1], [back_0[1], back_1[1]], "up_wg"),
             ]
         )
     )
-    slots(max(hops, 3), take_1, work)
+    slots(max(hops, 2), take_1, work)
     grad_1 = take_1.result()
-    down_wg, gate_wg, up_wg = work.result()
+    gate_wg, up_wg = work.result()
     outputs = jnp.concatenate([judged_0[0], judged_1[0]])
     squared = judged_0[1] + judged_1[1]
     out_grad = jnp.concatenate([judged_0[2], judged_1[2]])
     mlp_in_grad = jnp.concatenate([grad_0, grad_1])
     gate_wg, up_wg, down_wg = (
-        lax.psum_scatter(gate_wg, "col", scatter_dimension=0, tiled=True).astype(F32),
-        lax.psum_scatter(up_wg, "col", scatter_dimension=0, tiled=True).astype(F32),
-        lax.psum_scatter(down_wg, "col", scatter_dimension=0, tiled=True).astype(F32).T,
+        lax.psum_scatter(gate_wg, "col", scatter_dimension=0, tiled=True),
+        lax.psum_scatter(up_wg, "col", scatter_dimension=0, tiled=True),
+        lax.psum_scatter(down_wg, "col", scatter_dimension=0, tiled=True),
     )
     residual_part, mlp_gain_grad = norm_back(mlp_in_grad, mlp_unit, residual, mlp_g)
     residual_grad = out_grad + residual_part
 
     attn_grad_in = (RES * residual_grad).astype(BF)
     grad_t = dot_dims(out_all, attn_grad_in, (1,), (1,)).astype(BF)
-    out_wg = [
-        dot_dims(attn_grad_in, mixed_t, (0,), (1,))
-        .astype(BF)
-        .reshape(col_total, -1, heads_here * VDIM)
-        for mixed_t, _ in mixed
-    ]
     latent_t = kv_all.T
+    out_wg = out_weight_grad(attn_grad_in, jnp.stack([mixed_t for mixed_t, _ in mixed]))
     grad_t, out_wg = together((grad_t.reshape(-1, local_rows), out_wg))
-
-    def back_steps():
-        got = []
-        for block in range(row_total):
-            mixed_t, lse = mixed[block]
-            wg, query_part, kv_part_back, rope_part = yield attend_back(
-                head_w, query_t, kv_all, latent_t, rope_all, cos_t, sin_t, bias_t, mixed_t,
-                grad_t, lse, query_rows, block,
-            )
-            got.append((wg[0], query_part, jnp.concatenate([kv_part_back, rope_part], axis=1)))
-        return got
-
-    steps = len(far_bits()) + 1
-    backs = Task(back_steps())
-    out_reduce = Task(reduce_all_steps(out_wg))
-    slots(row_total, backs, out_reduce)
-    backs = backs.result()
-    query_back_t = sum(query_part for _, query_part, _ in backs)
-    latent_back = sum(part for _, _, part in backs).astype(BF)
-    latent_reduce = Task(reduce_row_steps(latent_back.reshape(row_total, local_rows, -1)))
-    head_reduce = Task(reduce_all_steps([wg for wg, _, _ in backs]))
-    slots(hops, latent_reduce, head_reduce, out_reduce)
-    latent_back = latent_reduce.result()
+    out_wg = lax.psum_scatter(
+        out_wg.reshape(row_total * width, heads_here * VDIM),
+        both_axes, scatter_dimension=0, tiled=True,
+    )
+    query_back_t = jnp.zeros(query_t.shape, F32)
+    latent_back = jnp.zeros(latent_all.shape, F32)
+    head_wg = None
+    for block, (mixed_t, lse) in enumerate(mixed):
+        if block == cut:
+            query_back_t, gate_wg, up_wg, down_wg = together((query_back_t, gate_wg, up_wg, down_wg))
+        head_wg, query_back_t, latent_back = attend_back(
+            head_w, query_t, kv_all, latent_t, rope_all, cos_t, sin_t, bias_t, mixed_t,
+            grad_t, lse, query_back_t, latent_back, head_wg, query_rows, block,
+        )
+    head_wg, out_wg = together((head_wg, out_wg))
+    out_wg = out_wg.astype(F32).T
+    head_wg = lax.psum_scatter(
+        head_wg.reshape(devices * pack_rows, heads_here * HEAD),
+        both_axes, scatter_dimension=0, tiled=True,
+    ).astype(F32)
+    latent_rows = latent_back.astype(BF)
+    latent_reduce = Task(
+        reduce_steps(
+            [latent_rows[at * local_rows : (at + 1) * local_rows] for at in range(row_total)]
+        )
+    )
+    while latent_reduce.advance_into():
+        pass
+    latent_back = latent_reduce.value
     kv_norm_grad = latent_back[:, :KV_RANK]
     rope_grad = latent_back[:, KV_RANK + NOPE : KV_RANK + NOPE + ROPE]
     query_norm_grad = query_back_t.T
@@ -791,10 +1072,7 @@
     small = jnp.where(lane == lat_wide + 1, mlp_gain_grad[:, None], small)
     small = jnp.where(lane == lat_wide + 2, misc_grad, small).astype(BF)
     small = small.reshape(row_total, col_total, down_rows, pack_wide)
-    small_reduce = Task(reduce_all_steps([small[block] for block in range(row_total)]))
-    slots(steps + hops, small_reduce, head_reduce, out_reduce)
-    small, head_wg, out_wg = small_reduce.result(), head_reduce.result(), out_reduce.result()
-    out_wg = out_wg.T
+    small = reduce_all(small, 3, "reduce_down")
     qu_wg = head_wg[:query_rows].reshape(query_rows, heads_here, HEAD)[:, :, : NOPE + ROPE]
     qu_wg = qu_wg.reshape(query_rows, heads_here * (NOPE + ROPE))
     kvu_wg = head_wg[query_rows:]
@@ -810,9 +1088,9 @@
         qu_wg,
         kvu_wg,
         out_wg,
-        gate_wg,
-        up_wg,
-        down_wg,
+        gate_wg.astype(F32),
+        up_wg.astype(F32),
+        down_wg.astype(F32).T,
         small[:, lat_wide],
         misc_sum[:q_part],
         misc_sum[q_part : q_part + kv_part],

time: 1600 us -> 1360 us (0.85)
  Pallas kernels: 295 us -> 507 us
  waiting for transfers between devices: 475 us -> 320 us
  local copies, waits for them, and re-layouts: 200 us -> 57.5 us
  starting transfers between devices: 213 us -> 129 us
  other arithmetic: 181 us -> 116 us
    pallas_call x0 -> x3, Pallas kernels: none -> 210 us  [the longest x1 97.9 us: gather_all(): pl.pallas_call(functools.partial(gather_kernel, row_total, col_total), in...]
    ppermute x50 -> x0, waiting for transfers between devices: 155 us -> none  [swap(): return lax.ppermute(values, 'col', [(i, i ^ bit) for i in range(total)])]
    all_gather x3, waiting for transfers between devices: 103 us -> 0.02 us  [the longest x1 0.02 us: body(): lax.all_gather(down_here, 'col', axis=0, tiled=True)]
    ppermute x12 -> x15, waiting for transfers between devices: 107 us -> 176 us  [gather_steps(): lax.ppermute(ways[1], 'row', [(i, i - 1) for i in range(1, total - step +...]
    dynamic_update_slice x31 -> x0, local copies, waits for them, and re-layouts: 59 us -> none  [put(): lax.dynamic_update_slice(array, part[None], (jnp.bitwise_xor(col_rank, aw...]
    ppermute x24 -> x15, starting transfers between devices: 110 us -> 62.1 us  [reduce_steps(): lax.ppermute(sends[0], 'row', [(i, i + 1) for i in range(step + 1)])]
    convert_element_type x44 -> x10, other arithmetic: 63.7 us -> 17.3 us  [add_parts(): return (left_op.astype(F32) + right_op.astype(F32)).astype(BF)]
    ppermute x50 -> x0, starting transfers between devices: 33.6 us -> none  [swap(): return lax.ppermute(values, 'col', [(i, i ^ bit) for i in range(total)])]
  transfers between devices with their start and end apart: 129 -> 69, of which waited for: 48 -> 31; matrix products, arithmetic and copies ran while one was open for 28% -> 23% of each run, Pallas kernels for 19% -> 30%
where the time goes in v3:
time: 1360 us; the launch traced here: 1350 us
  Pallas kernels  507 us (37%)
  waiting for transfers between devices  320 us (24%)
  matrix products  195 us (14%)
  starting transfers between devices  129 us (9%)
  other arithmetic  116 us (9%)
  local copies, waits for them, and re-layouts  57.5 us (4%)
  between operations  24.2 us (2%)
    ppermute x15, waiting for transfers between devices, gather_steps(): lax.ppermute(ways[1], 'row', [(i, i - 1) for i in range(1, total - step +...  176 us
    pallas_call x4, Pallas kernels, attend_back(): pl.pallas_call(functools.partial(attend_back_kernel, query_rows, tile), g...  174 us
    dot_general x13, matrix products, dot_dims(): lax.dot_general(left_op, right_op, ((left_dims, right_dims), ((), ())), p...  112 us
    pallas_call x1, Pallas kernels, gather_all(): pl.pallas_call(functools.partial(gather_kernel, row_total, col_total), in...  97.9 us
    pallas_call x1, Pallas kernels, reduce_all(): pl.pallas_call(functools.partial(reduce_kernel, row_total, col_total), in...  91.5 us
    dot_general x7, matrix products, dot_plain(): return jnp.dot(left_op, right_op, preferred_element_type=F32)  82.4 us
    pallas_call x4, Pallas kernels, attend(): pl.pallas_call(functools.partial(attend_kernel, query_rows, tile), grid=(...  67 us
    ppermute x15, waiting for transfers between devices, reduce_steps(): lax.ppermute(sends[0], 'row', [(i, i + 1) for i in range(step + 1)])  66.7 us
  transfers between devices with their start and end apart: 69, of which 31 were waited for; matrix products, arithmetic and copies ran while one was open for 23% of the time, Pallas kernels for 30%

profile of v3, /device:TPU:0, one launch (start us, length us, event | category | flops | bytes accessed | tf_op | source)
XLA Modules:
  0.0 1347.7 jit_solution(1269201179343597205)
XLA Ops:
  18.4 97.9 %gather_pack.1.weights_ref = bf16[4,8,208,1280]{3,2,1,0:T(8,128)(2,1)} custom-call(bf16[208,1280]{1,0:T(8,128)(2,1)} %fusion.68.own_ref), custom_call_target="tpu_custom_call" | custom-call | tf_op jit(solution)/shard_map/gather_pack/pallas_call | solution.py:499
  152.2 19.5 %collective-permute-done.1 = bf16[384,384]{0,1:T(8,128)(2,1)S(1)} collective-permute-done((bf16[384,384]{0,1:T(8,128)(2,1)S(1)}, bf16[384,384]{0,1:T(8,128)(2,1)S(1)}, u32[]{:S(2)}, u32[]{:S(2)}) %collective-permute-start.1) | collective-permute-done | bytes 294944 | tf_op jit(solution)/shard_map/ppermute | solution.py:727
  190.7 20.9 %collective-permute-done.3 = bf16[384,384]{0,1:T(8,128)(2,1)} collective-permute-done((bf16[384,384]{0,1:T(8,128)(2,1)}, bf16[384,384]{0,1:T(8,128)(2,1)}, u32[]{:S(2)}, u32[]{:S(2)}) %collective-permute-start.3) | collective-permute-done | bytes 294944 | tf_op jit(solution)/shard_map/ppermute | solution.py:727
  220.7 16.7 %attend.5 = (bf16[640,384]{1,0:T(8,128)(2,1)S(1)}, f32[10,1,384]{2,1,0:T(1,128)S(1)}) custom-call(bf16[4,8,208,1280]{3,2,1,0:T(8,128)(2,1)} %gather_pack.1.weights_ref, bf16[768,384]{1,0:T(8,128)(2,1)S(1)} %fusion.63.query_t_ref, bf16[1536,256]{1,0:T(8,128)(2,1)S(1)} %copy-done.10, bf16[1536,128]{1,0:T(8,128)(2,1)S(1)} %copy-done.19, ...), custom_call_target="tpu_custom_call" | custom-call | flops 16999999488 | bytes 4259840 | tf_op jit(solution)/shard_map/attend/pallas_call | solution.py:213
  238.5 16.9 %attend.4 = (bf16[640,384]{1,0:T(8,128)(2,1)S(1)}, f32[10,1,384]{2,1,0:T(1,128)S(1)}) custom-call(bf16[4,8,208,1280]{3,2,1,0:T(8,128)(2,1)} %gather_pack.1.weights_ref, bf16[768,384]{1,0:T(8,128)(2,1)S(1)} %copy-done.15, bf16[1536,256]{1,0:T(8,128)(2,1)S(1)} %copy-done.10, bf16[1536,128]{1,0:T(8,128)(2,1)S(1)} %copy-done.19, ...), custom_call_target="tpu_custom_call" | custom-call | flops 16999999488 | bytes 4259840 | tf_op jit(solution)/shard_map/attend/pallas_call | solution.py:213
  264.3 16.7 %attend.6 = (bf16[640,384]{1,0:T(8,128)(2,1)S(1)}, f32[10,1,384]{2,1,0:T(1,128)S(1)}) custom-call(bf16[4,8,208,1280]{3,2,1,0:T(8,128)(2,1)} %gather_pack.1.weights_ref, bf16[768,384]{1,0:T(8,128)(2,1)S(1)} %copy-done.16, bf16[1536,256]{1,0:T(8,128)(2,1)S(1)} %copy-done.11, bf16[1536,128]{1,0:T(8,128)(2,1)S(1)} %copy-done.20, ...), custom_call_target="tpu_custom_call" | custom-call | flops 16999999488 | bytes 4259840 | tf_op jit(solution)/shard_map/attend/pallas_call | solution.py:213
  286.2 16.7 %attend.7 = (bf16[640,384]{1,0:T(8,128)(2,1)S(1)}, f32[10,1,384]{2,1,0:T(1,128)S(1)}) custom-call(bf16[4,8,208,1280]{3,2,1,0:T(8,128)(2,1)} %gather_pack.1.weights_ref, bf16[768,384]{1,0:T(8,128)(2,1)S(1)} %copy-done.16, bf16[1536,256]{1,0:T(8,128)(2,1)S(1)} %copy-done.11, bf16[1536,128]{1,0:T(8,128)(2,1)S(1)} %copy-done.20, ...), custom_call_target="tpu_custom_call" | custom-call | flops 16999999488 | bytes 4259840 | tf_op jit(solution)/shard_map/attend/pallas_call | solution.py:213
  312.3 16.4 %collective-permute-done.8 = bf16[192,2560]{1,0:T(8,128)(2,1)S(1)} collective-permute-done((bf16[192,2560]{1,0:T(8,128)(2,1)S(1)}, bf16[192,2560]{1,0:T(8,128)(2,1)S(1)}, u32[]{:S(2)}, u32[]{:S(2)}) %collective-permute-start.8) | collective-permute-done | bytes 983072 | tf_op jit(solution)/shard_map/ppermute | solution.py:726
  339.9 32.6 %collective-permute-done.11 = bf16[192,2560]{1,0:T(8,128)(2,1)} collective-permute-done((bf16[192,2560]{1,0:T(8,128)(2,1)S(1)}, bf16[192,2560]{1,0:T(8,128)(2,1)}, u32[]{:S(2)}, u32[]{:S(2)}) %collective-permute-start.11) | collective-permute-done | bytes 983072 | tf_op jit(solution)/shard_map/ppermute | solution.py:727
  399.4 11.7 convolution_convert_fusion.3
  424.1 15.2 %collective-permute-done.15 = bf16[192,2560]{1,0:T(8,128)(2,1)} collective-permute-done((bf16[192,2560]{1,0:T(8,128)(2,1)}, bf16[192,2560]{1,0:T(8,128)(2,1)}, u32[]{:S(2)}, u32[]{:S(2)}) %collective-permute-start.15) | collective-permute-done | bytes 983072 | tf_op jit(solution)/shard_map/ppermute | solution.py:727
  490.2 14.3 %fusion.21 = (bf16[768,1600]{1,0:T(8,128)(2,1)S(1)}, bf16[768,1600]{1,0:T(8,128)(2,1)}) fusion(bf16[768,1600]{1,0:T(8,128)(2,1)S(1)} %convolution_convert_fusion.2, bf16[2560,1600]{1,0:T(8,128)(2,1)} %all-gather.9.cloned.1.call-done, bf16[192,2560]{1,0:T(8,128)(2,1)S(1)} %add.377, bf16[192,2560]{1,0:T(8,128)(2,1)S(1)} %add.376, ...), kind=kOutput, calls=%fused_computation.35 | convolution fusion | flops 6317015040 | bytes 19496960 | tf_op jit(solution)/shard_map/dot_general | solution.py:29
  574.9 24.6 %collective-permute-done.27 = bf16[192,2560]{1,0:T(8,128)(2,1)S(1)} collective-permute-done((bf16[192,2560]{1,0:T(8,128)(2,1)S(1)}, bf16[192,2560]{1,0:T(8,128)(2,1)S(1)}, u32[]{:S(2)}, u32[]{:S(2)}) %collective-permute-start.27) | collective-permute-done | bytes 983072 | tf_op jit(solution)/shard_map/ppermute | solution.py:727
  604.4 16.3 %collective-permute-done.32 = bf16[192,2560]{1,0:T(8,128)(2,1)S(1)} collective-permute-done((bf16[192,2560]{1,0:T(8,128)(2,1)S(1)}, bf16[192,2560]{1,0:T(8,128)(2,1)S(1)}, u32[]{:S(2)}, u32[]{:S(2)}) %collective-permute-start.32) | collective-permute-done | bytes 983072 | tf_op jit(solution)/shard_map/ppermute | solution.py:746
  635.4 14.7 %fusion.16 = (bf16[768,1600]{1,0:T(8,128)(2,1)S(1)}, bf16[768,1600]{1,0:T(8,128)(2,1)S(1)}) fusion(bf16[768,1600]{1,0:T(8,128)(2,1)} %copy-done.125, bf16[768,1600]{1,0:T(8,128)(2,1)} %get-tuple-element.338, bf16[2560,1600]{1,0:T(8,128)(2,1)} %all-gather.11.cloned.1.call-done, bf16[192,2560]{1,0:T(8,128)(2,1)} %add.395, bf16[192,2560]{1,0:T(8,128)(2,1)S(1)} %add.394, ...), kind=kOutput, calls=%fused_computation.30 | convolution fusion | flops 6325616640 | bytes 21954560 | tf_op jit(solution)/shard_map/dot_general | solution.py:29
  680.1 11.7 fusion.92
  703.3 18.0 %collective-permute-done.39 = bf16[192,2560]{1,0:T(8,128)(2,1)} collective-permute-done((bf16[192,2560]{1,0:T(8,128)(2,1)}, bf16[192,2560]{1,0:T(8,128)(2,1)}, u32[]{:S(2)}, u32[]{:S(2)}) %collective-permute-start.39) | collective-permute-done | bytes 983072 | tf_op jit(solution)/shard_map/ppermute | solution.py:727
  731.1 14.0 %collective-permute-done.42 = bf16[192,2560]{1,0:T(8,128)(2,1)S(1)} collective-permute-done((bf16[192,2560]{1,0:T(8,128)(2,1)S(1)}, bf16[192,2560]{1,0:T(8,128)(2,1)S(1)}, u32[]{:S(2)}, u32[]{:S(2)}) %collective-permute-start.42) | collective-permute-done | bytes 983072 | tf_op jit(solution)/shard_map/ppermute | solution.py:746
  760.9 18.6 %down_wg.1 = bf16[2560,1600]{1,0:T(8,128)(2,1)} custom-call(bf16[768,2560]{1,0:T(8,128)(2,1)} %pad_maximum_fusion.2.refs_0_, bf16[768,2560]{1,0:T(8,128)(2,1)} %pad_maximum_fusion.3.refs_1_, bf16[768,1600]{1,0:T(8,128)(2,1)S(1)} %copy-done.37, bf16[768,1600]{1,0:T(8,128)(2,1)S(1)} %get-tuple-element.158.refs_3_), custom_call_target="tpu_custom_call" | custom-call | flops 12582912000 | bytes 16056320 | tf_op jit(solution)/shard_map/down_wg/pallas_call | solution.py:314
  791.9 15.0 %fusion.26 = (bf16[768,1600]{1,0:T(8,128)(2,1)S(1)}, bf16[768,1600]{1,0:T(8,128)(2,1)S(1)}) fusion(bf16[768,1600]{1,0:T(8,128)(2,1)S(1)} %copy-done.127, bf16[768,1600]{1,0:T(8,128)(2,1)} %get-tuple-element.340, bf16[2560,1600]{1,0:T(8,128)(2,1)} %all-gather.11.cloned.1.call-done, bf16[192,2560]{1,0:T(8,128)(2,1)S(1)} %copy-done.75, ...), kind=kOutput, calls=%fused_computation.40 | convolution fusion | flops 6325616640 | bytes 21954560 | tf_op jit(solution)/shard_map/dot_general | solution.py:29
  807.0 12.5 fusion.94
  820.9 12.1 add_convert_fusion
  842.6 18.6 %gate_wg.1 = bf16[2560,1600]{1,0:T(8,128)(2,1)} custom-call(bf16[768,2560]{1,0:T(8,128)(2,1)} %pad_maximum_fusion.refs_0_, bf16[768,2560]{1,0:T(8,128)(2,1)} %pad_maximum_fusion.1.refs_1_, bf16[768,1600]{1,0:T(8,128)(2,1)S(1)} %copy-done.33, bf16[768,1600]{1,0:T(8,128)(2,1)S(1)} %get-tuple-element.190.refs_3_), custom_call_target="tpu_custom_call" | custom-call | flops 12582912000 | bytes 16056320 | tf_op jit(solution)/shard_map/gate_wg/pallas_call | solution.py:314
  871.0 18.7 %up_wg.1 = bf16[2560,1600]{1,0:T(8,128)(2,1)} custom-call(bf16[768,2560]{1,0:T(8,128)(2,1)} %pad_maximum_fusion.refs_0_, bf16[768,2560]{1,0:T(8,128)(2,1)} %pad_maximum_fusion.1.refs_1_, bf16[768,1600]{1,0:T(8,128)(2,1)S(1)} %get-tuple-element.178.refs_2_, bf16[768,1600]{1,0:T(8,128)(2,1)S(1)} %copy-done.35), custom_call_target="tpu_custom_call" | custom-call | flops 12582912000 | bytes 16056320 | tf_op jit(solution)/shard_map/up_wg/pallas_call | solution.py:314
  921.5 20.2 %out_wg.1 = bf16[4,2560,640]{2,1,0:T(8,128)(2,1)} custom-call(bf16[384,2560]{1,0:T(8,128)(2,1)} %get-tuple-element.271.tokens_ref, bf16[4,640,384]{2,1,0:T(8,128)(2,1)} %pad_maximum_fusion.6.mixed_ref), custom_call_target="tpu_custom_call" | custom-call | flops 5033164800 | bytes 13107200 | tf_op jit(solution)/shard_map/out_wg/pallas_call | solution.py:344
  941.7 13.0 fusion.56
  958.0 44.0 %attend_back.4 = (bf16[4,8,128,1280]{3,2,1,0:T(8,128)(2,1)}, f32[768,384]{1,0:T(8,128)S(1)}, f32[1536,384]{1,0:T(8,128)}) custom-call(bf16[4,8,208,1280]{3,2,1,0:T(8,128)(2,1)} %gather_pack.1.weights_ref, bf16[768,384]{1,0:T(8,128)(2,1)S(1)} %copy-done.17, bf16[1536,256]{1,0:T(8,128)(2,1)S(1)} %copy-done.12, bf16[256,1536]{1,0:T(8,128)(2,1)S(1)} %copy-done.13, ...), custom_call_target="tpu_custom_call" | custom-call | flops 41999998976 | bytes 8519680 | tf_op jit(solution)/shard_map/attend_back/pallas_call | solution.py:256
  1002.1 43.3 %attend_back.5 = (bf16[4,8,128,1280]{3,2,1,0:T(8,128)(2,1)}, f32[768,384]{1,0:T(8,128)S(1)}, f32[1536,384]{1,0:T(8,128)}) custom-call(bf16[4,8,208,1280]{3,2,1,0:T(8,128)(2,1)} %gather_pack.1.weights_ref, bf16[768,384]{1,0:T(8,128)(2,1)S(1)} %copy-done.17, bf16[1536,256]{1,0:T(8,128)(2,1)S(1)} %copy-done.12, ...), custom_call_target="tpu_custom_call", output_to_operand_aliasing={{0}: (13, {})} | custom-call | flops 41999998976 | bytes 8519680 | tf_op jit(solution)/shard_map/attend_back/pallas_call | solution.py:256
  1048.7 43.3 %attend_back.6 = (bf16[4,8,128,1280]{3,2,1,0:T(8,128)(2,1)}, f32[768,384]{1,0:T(8,128)S(1)}, f32[1536,384]{1,0:T(8,128)}) custom-call(bf16[4,8,208,1280]{3,2,1,0:T(8,128)(2,1)} %gather_pack.1.weights_ref, bf16[768,384]{1,0:T(8,128)(2,1)S(1)} %copy-done.18, bf16[1536,256]{1,0:T(8,128)(2,1)S(1)} %copy-done.12, ...), custom_call_target="tpu_custom_call", output_to_operand_aliasing={{0}: (13, {})} | custom-call | flops 41999998976 | bytes 8519680 | tf_op jit(solution)/shard_map/attend_back/pallas_call | solution.py:256
  1091.9 43.4 %attend_back.7 = (bf16[4,8,128,1280]{3,2,1,0:T(8,128)(2,1)}, f32[768,384]{1,0:T(8,128)S(1)}, f32[1536,384]{1,0:T(8,128)}) custom-call(bf16[4,8,208,1280]{3,2,1,0:T(8,128)(2,1)} %gather_pack.1.weights_ref, bf16[768,384]{1,0:T(8,128)(2,1)S(1)} %copy-done.18, bf16[1536,256]{1,0:T(8,128)(2,1)S(1)} %copy-done.12, ...), custom_call_target="tpu_custom_call", output_to_operand_aliasing={{0}: (13, {})} | custom-call | flops 41999998976 | bytes 8519680 | tf_op jit(solution)/shard_map/attend_back/pallas_call | solution.py:256
  1135.4 31.9 %reduce-scatter.12.cloned.1.call-done = bf16[320,640]{1,0:T(8,128)(2,1)} async-done(((bf16[10240,640]{1,0:T(8,128)(2,1)}), bf16[320,640]{1,0:T(8,128)(2,1)}) %reduce-scatter.12.cloned.1.call-update) | async-done | bytes 409616 | tf_op jit(solution)/shard_map/reduce_scatter | solution.py:1010
  1232.0 91.5 %reduce_down.1 = f32[80,1152]{1,0:T(8,128)S(1)} custom-call(bf16[4,4,2,80,1152]{4,3,2,1,0:T(8,128)(2,1)} %bitcast.117), custom_call_target="tpu_custom_call" | custom-call | tf_op jit(solution)/shard_map/reduce_down/pallas_call | solution.py:661
  (546 shorter events, 502.7 us)
Async XLA Ops:
  7.2 248.2 %all-gather.5.cloned.1.call-start = ((), (), s32[]{:S(2)}) async-start(), calls=%async_computation.5 | async-start | bytes 13516800 | tf_op jit(solution)/shard_map/all_gather | solution.py:826
  122.1 277.2 %all-gather.7.cloned.1.call-start = ((), (), s32[]{:S(2)}) async-start(), calls=%async_computation.6 | async-start | bytes 9584640 | tf_op jit(solution)/shard_map/all_gather | solution.py:889
  145.4 26.3 %collective-permute-start.1 = (bf16[384,384]{0,1:T(8,128)(2,1)S(1)}, bf16[384,384]{0,1:T(8,128)(2,1)S(1)}, u32[]{:S(2)}, u32[]{:S(2)}) collective-permute-start(bf16[384,384]{0,1:T(8,128)(2,1)S(1)} %constant_dynamic-update-slice_fusion), channel_id=1, source_target_pairs={{8,0},{16,8},{24,16},{9,1},{17,9},{25,17},{10,2},{18,10},{26,18},{... | collective-permute-start | bytes 884744 | tf_op jit(solution)/shard_map/ppermute | solution.py:727
  146.7 26.3 %collective-permute-start = (bf16[384,384]{0,1:T(8,128)(2,1)S(1)}, bf16[384,384]{0,1:T(8,128)(2,1)S(1)}, u32[]{:S(2)}, u32[]{:S(2)}) collective-permute-start(bf16[384,384]{0,1:T(8,128)(2,1)S(1)} %constant_dynamic-update-slice_fusion), channel_id=1, source_target_pairs={{0,8},{8,16},{16,24},{1,9},{9,17},{17,25},{2,10},{10,18},{18,26},{... | collective-permute-start | bytes 884744 | tf_op jit(solution)/shard_map/ppermute | solution.py:726
  184.8 26.8 %collective-permute-start.3 = (bf16[384,384]{0,1:T(8,128)(2,1)}, bf16[384,384]{0,1:T(8,128)(2,1)}, u32[]{:S(2)}, u32[]{:S(2)}) collective-permute-start(bf16[384,384]{0,1:T(8,128)(2,1)} %collective-permute-done.2), channel_id=1, source_target_pairs={{8,0},{9,1},{10,2},{11,3},{12,4},{13,5},{14,6},{15,7}} | collective-permute-start | bytes 884744 | tf_op jit(solution)/shard_map/ppermute | solution.py:727
  186.1 26.6 %collective-permute-start.5 = (bf16[384,384]{0,1:T(8,128)(2,1)}, bf16[384,384]{0,1:T(8,128)(2,1)}, u32[]{:S(2)}, u32[]{:S(2)}) collective-permute-start(bf16[384,384]{0,1:T(8,128)(2,1)} %collective-permute-done.4), channel_id=1, source_target_pairs={{16,24},{17,25},{18,26},{19,27},{20,28},{21,29},{22,30},{23,31}} | collective-permute-start | bytes 884744 | tf_op jit(solution)/shard_map/ppermute | solution.py:726
  255.4 143.9 %all-gather.9.cloned.1.call-start = ((), (), s32[]{:S(2)}) async-start(), calls=%async_computation.7 | async-start | bytes 9584640 | tf_op jit(solution)/shard_map/all_gather | solution.py:890
  256.2 187.7 %all-gather.11.cloned.1.call-start = ((), (), s32[]{:S(2)}) async-start(), calls=%async_computation.8 | async-start | bytes 9584640 | tf_op jit(solution)/shard_map/all_gather | solution.py:891
  256.7 789.6 %reduce-scatter.10.cloned.1.call-start = ((), (), s32[]{:S(2)}) async-start(), calls=%async_computation.11 | async-start | bytes 9584640 | tf_op jit(solution)/shard_map/reduce_scatter | solution.py:1000
  311.0 25.9 %collective-permute-start.9 = (bf16[192,2560]{1,0:T(8,128)(2,1)S(1)}, bf16[192,2560]{1,0:T(8,128)(2,1)S(1)}, u32[]{:S(2)}, u32[]{:S(2)}) collective-permute-start(bf16[192,2560]{1,0:T(8,128)(2,1)S(1)} %get-tuple-element.308), channel_id=1, source_target_pairs={{8,0},{16,8},{24,16},{9,1},{17,9},{25,17},{10,2},{18,10},{26,18},{... | collective-permute-start | bytes 2949128 | tf_op jit(solution)/shard_map/ppermute | solution.py:727
  338.6 33.9 %collective-permute-start.11 = (bf16[192,2560]{1,0:T(8,128)(2,1)S(1)}, bf16[192,2560]{1,0:T(8,128)(2,1)}, u32[]{:S(2)}, u32[]{:S(2)}) collective-permute-start(bf16[192,2560]{1,0:T(8,128)(2,1)S(1)} %collective-permute-done.9), channel_id=1, source_target_pairs={{8,0},{16,8},{9,1},{17,9},{10,2},{18,10},{11,3},{19,11},{12,4},{20... | collective-permute-start | bytes 2949128 | tf_op jit(solution)/shard_map/ppermute | solution.py:727
  378.1 33.1 %collective-permute-start.6 = (bf16[192,2560]{1,0:T(8,128)(2,1)S(1)}, bf16[192,2560]{1,0:T(8,128)(2,1)S(1)}, u32[]{:S(2)}, u32[]{:S(2)}) collective-permute-start(bf16[192,2560]{1,0:T(8,128)(2,1)S(1)} %get-tuple-element.309), channel_id=1, source_target_pairs={{0,8},{8,16},{16,24},{1,9},{9,17},{17,25},{2,10},{10,18},{18,26},{... | collective-permute-start | bytes 2949128 | tf_op jit(solution)/shard_map/ppermute | solution.py:726
  383.7 28.8 %collective-permute-start.7 = (bf16[192,2560]{1,0:T(8,128)(2,1)S(1)}, bf16[192,2560]{1,0:T(8,128)(2,1)}, u32[]{:S(2)}, u32[]{:S(2)}) collective-permute-start(bf16[192,2560]{1,0:T(8,128)(2,1)S(1)} %get-tuple-element.309), channel_id=1, source_target_pairs={{8,0},{16,8},{24,16},{9,1},{17,9},{25,17},{10,2},{18,10},{26,18},{... | collective-permute-start | bytes 2949128 | tf_op jit(solution)/shard_map/ppermute | solution.py:727
  414.1 25.2 %collective-permute-start.15 = (bf16[192,2560]{1,0:T(8,128)(2,1)}, bf16[192,2560]{1,0:T(8,128)(2,1)}, u32[]{:S(2)}, u32[]{:S(2)}) collective-permute-start(bf16[192,2560]{1,0:T(8,128)(2,1)} %collective-permute-done.7), channel_id=1, source_target_pairs={{8,0},{16,8},{9,1},{17,9},{10,2},{18,10},{11,3},{19,11},{12,4},{20... | collective-permute-start | bytes 2949128 | tf_op jit(solution)/shard_map/ppermute | solution.py:727
  460.9 23.7 %collective-permute-start.18 = (bf16[192,2560]{1,0:T(8,128)(2,1)S(1)}, bf16[192,2560]{1,0:T(8,128)(2,1)S(1)}, u32[]{:S(2)}, u32[]{:S(2)}) collective-permute-start(bf16[192,2560]{1,0:T(8,128)(2,1)S(1)} %get-tuple-element.306), channel_id=1, source_target_pairs={{0,8},{1,9},{2,10},{3,11},{4,12},{5,13},{6,14},{7,15}} | collective-permute-start | bytes 2949128 | tf_op jit(solution)/shard_map/ppermute | solution.py:746
  485.0 24.4 %collective-permute-start.20 = (bf16[192,2560]{1,0:T(8,128)(2,1)S(1)}, bf16[192,2560]{1,0:T(8,128)(2,1)S(1)}, u32[]{:S(2)}, u32[]{:S(2)}) collective-permute-start(bf16[192,2560]{1,0:T(8,128)(2,1)S(1)} %get-tuple-element.304), channel_id=1, source_target_pairs={{0,8},{8,16},{1,9},{9,17},{2,10},{10,18},{3,11},{11,19},{4,12},{12... | collective-permute-start | bytes 2949128 | tf_op jit(solution)/shard_map/ppermute | solution.py:746
  509.8 29.1 %collective-permute-start.22 = (bf16[192,2560]{1,0:T(8,128)(2,1)S(1)}, bf16[192,2560]{1,0:T(8,128)(2,1)S(1)}, u32[]{:S(2)}, u32[]{:S(2)}) collective-permute-start(bf16[192,2560]{1,0:T(8,128)(2,1)S(1)} %get-tuple-element.302), channel_id=1, source_target_pairs={{0,8},{8,16},{16,24},{1,9},{9,17},{17,25},{2,10},{10,18},{18,26},{... | collective-permute-start | bytes 2949128 | tf_op jit(solution)/shard_map/ppermute | solution.py:746
  519.9 24.3 %collective-permute-start.23 = (bf16[192,2560]{1,0:T(8,128)(2,1)S(1)}, bf16[192,2560]{1,0:T(8,128)(2,1)S(1)}, u32[]{:S(2)}, u32[]{:S(2)}) collective-permute-start(bf16[192,2560]{1,0:T(8,128)(2,1)S(1)} %get-tuple-element.301), channel_id=1, source_target_pairs={{8,0},{16,8},{24,16},{9,1},{17,9},{25,17},{10,2},{18,10},{26,18},{... | collective-permute-start | bytes 2949128 | tf_op jit(solution)/shard_map/ppermute | solution.py:747
  552.0 22.8 %collective-permute-start.28 = (bf16[192,2560]{1,0:T(8,128)(2,1)S(1)}, bf16[192,2560]{1,0:T(8,128)(2,1)S(1)}, u32[]{:S(2)}, u32[]{:S(2)}) collective-permute-start(bf16[192,2560]{1,0:T(8,128)(2,1)S(1)} %get-tuple-element.300), channel_id=1, source_target_pairs={{0,8},{1,9},{2,10},{3,11},{4,12},{5,13},{6,14},{7,15}} | collective-permute-start | bytes 2949128 | tf_op jit(solution)/shard_map/ppermute | solution.py:746
  573.5 25.9 %collective-permute-start.27 = (bf16[192,2560]{1,0:T(8,128)(2,1)S(1)}, bf16[192,2560]{1,0:T(8,128)(2,1)S(1)}, u32[]{:S(2)}, u32[]{:S(2)}) collective-permute-start(bf16[192,2560]{1,0:T(8,128)(2,1)S(1)} %collective-permute-done.25), channel_id=1, source_target_pairs={{8,0},{16,8},{9,1},{17,9},{10,2},{18,10},{11,3},{19,11},{12,4},{20... | collective-permute-start | bytes 2949128 | tf_op jit(solution)/shard_map/ppermute | solution.py:727
  602.8 24.6 %collective-permute-start.31 = (bf16[192,2560]{1,0:T(8,128)(2,1)S(1)}, bf16[192,2560]{1,0:T(8,128)(2,1)S(1)}, u32[]{:S(2)}, u32[]{:S(2)}) collective-permute-start(bf16[192,2560]{1,0:T(8,128)(2,1)S(1)} %collective-permute-done.27), channel_id=1, source_target_pairs={{8,0},{9,1},{10,2},{11,3},{12,4},{13,5},{14,6},{15,7}} | collective-permute-start | bytes 2949128 | tf_op jit(solution)/shard_map/ppermute | solution.py:727
  634.1 24.4 %collective-permute-start.35 = (bf16[192,2560]{1,0:T(8,128)(2,1)}, bf16[192,2560]{1,0:T(8,128)(2,1)}, u32[]{:S(2)}, u32[]{:S(2)}) collective-permute-start(bf16[192,2560]{1,0:T(8,128)(2,1)} %get-tuple-element.295), channel_id=1, source_target_pairs={{8,0},{16,8},{24,16},{9,1},{17,9},{25,17},{10,2},{18,10},{26,18},{... | collective-permute-start | bytes 2949128 | tf_op jit(solution)/shard_map/ppermute | solution.py:747
  664.4 27.4 %collective-permute-start.36 = (bf16[192,2560]{1,0:T(8,128)(2,1)S(1)}, bf16[192,2560]{1,0:T(8,128)(2,1)}, u32[]{:S(2)}, u32[]{:S(2)}) collective-permute-start(bf16[192,2560]{1,0:T(8,128)(2,1)S(1)} %get-tuple-element.273), channel_id=1, source_target_pairs={{0,8},{8,16},{16,24},{1,9},{9,17},{17,25},{2,10},{10,18},{18,26},{... | collective-permute-start | bytes 2949128 | tf_op jit(solution)/shard_map/ppermute | solution.py:726
  666.8 25.0 %collective-permute-start.37 = (bf16[192,2560]{1,0:T(8,128)(2,1)S(1)}, bf16[192,2560]{1,0:T(8,128)(2,1)}, u32[]{:S(2)}, u32[]{:S(2)}) collective-permute-start(bf16[192,2560]{1,0:T(8,128)(2,1)S(1)} %get-tuple-element.273), channel_id=1, source_target_pairs={{8,0},{16,8},{24,16},{9,1},{17,9},{25,17},{10,2},{18,10},{26,18},{... | collective-permute-start | bytes 2949128 | tf_op jit(solution)/shard_map/ppermute | solution.py:727
  693.4 27.9 %collective-permute-start.39 = (bf16[192,2560]{1,0:T(8,128)(2,1)}, bf16[192,2560]{1,0:T(8,128)(2,1)}, u32[]{:S(2)}, u32[]{:S(2)}) collective-permute-start(bf16[192,2560]{1,0:T(8,128)(2,1)} %collective-permute-done.37), channel_id=1, source_target_pairs={{8,0},{16,8},{9,1},{17,9},{10,2},{18,10},{11,3},{19,11},{12,4},{20... | collective-permute-start | bytes 2949128 | tf_op jit(solution)/shard_map/ppermute | solution.py:727
  751.7 27.8 %collective-permute-start.44 = (bf16[192,2560]{1,0:T(8,128)(2,1)}, bf16[192,2560]{1,0:T(8,128)(2,1)}, u32[]{:S(2)}, u32[]{:S(2)}) collective-permute-start(bf16[192,2560]{1,0:T(8,128)(2,1)} %get-tuple-element.292), channel_id=1, source_target_pairs={{0,8},{8,16},{1,9},{9,17},{2,10},{10,18},{3,11},{11,19},{4,12},{12... | collective-permute-start | bytes 2949128 | tf_op jit(solution)/shard_map/ppermute | solution.py:746
  779.5 266.9 %reduce-scatter.6.cloned.1.call-start = ((), (), s32[]{:S(2)}) async-start(), calls=%async_computation.9 | async-start | bytes 9584640 | tf_op jit(solution)/shard_map/reduce_scatter | solution.py:998
  836.5 24.9 %collective-permute-start.48 = (bf16[192,2560]{1,0:T(8,128)(2,1)}, bf16[192,2560]{1,0:T(8,128)(2,1)S(1)}, u32[]{:S(2)}, u32[]{:S(2)}) collective-permute-start(bf16[192,2560]{1,0:T(8,128)(2,1)} %get-tuple-element.288), channel_id=1, source_target_pairs={{0,8},{1,9},{2,10},{3,11},{4,12},{5,13},{6,14},{7,15}} | collective-permute-start | bytes 2949128 | tf_op jit(solution)/shard_map/ppermute | solution.py:746
  861.3 185.0 %reduce-scatter.8.cloned.1.call-start = ((), (), s32[]{:S(2)}) async-start(), calls=%async_computation.10 | async-start | bytes 9584640 | tf_op jit(solution)/shard_map/reduce_scatter | solution.py:999
  864.8 24.9 %collective-permute-start.50 = (bf16[192,2560]{1,0:T(8,128)(2,1)}, bf16[192,2560]{1,0:T(8,128)(2,1)S(1)}, u32[]{:S(2)}, u32[]{:S(2)}) collective-permute-start(bf16[192,2560]{1,0:T(8,128)(2,1)} %get-tuple-element.286), channel_id=1, source_target_pairs={{0,8},{8,16},{1,9},{9,17},{2,10},{10,18},{3,11},{11,19},{4,12},{12... | collective-permute-start | bytes 2949128 | tf_op jit(solution)/shard_map/ppermute | solution.py:746
  890.7 276.6 %reduce-scatter.12.cloned.1.call-start = ((), (), s32[]{:S(2)}) async-start(), calls=%async_computation.12 | async-start | bytes 13516800 | tf_op jit(solution)/shard_map/reduce_scatter | solution.py:1010
  954.8 382.0 %reduce-scatter.14.cloned.1.call-start = ((), (), s32[]{:S(2)}) async-start(), calls=%async_computation.13 | async-start | bytes 10813440 | tf_op jit(solution)/shard_map/reduce_scatter | solution.py:1026
  (165 other events, 3195.3 us)
Sparse Core Ops, SparseCore 0:
  122.3 104.0 all-gather.4
  255.5 60.9 all-gather.6
  318.4 54.9 all-gather.8
  375.2 54.9 all-gather.10
  779.6 69.9 reduce-scatter.9
  861.5 70.1 reduce-scatter.5
  935.2 72.0 reduce-scatter.7
  1009.6 157.6 reduce-scatter.11
  1169.7 167.0 reduce-scatter.13

commit v4 on v3

--- a/solution.py
+++ b/solution.py
@@ -13,6 +13,7 @@
 VDIM = 64
 KV_RANK = 256
 CONTS = 4
+CONT_LEN = 256
 HEAD = 128
 
 EPS = 1e-05
@@ -83,138 +84,153 @@
 
 def head_weights(weights_ref, query_rows):
     block = weights_ref[0]
-    col_total = block.shape[0]
-    query_w = block[:, :query_rows, :].reshape(col_total * query_rows, HEAD)
-    latent_w = block[:, query_rows:, :].reshape(-1, HEAD)
+    col_total, _, lanes = block.shape
+    query_w = block[:, :query_rows, :].reshape(col_total * query_rows, lanes)
+    latent_w = block[:, query_rows:, :].reshape(-1, lanes)
     return (query_w, latent_w)
 
 
-def head_vectors(weights_ref, query_t_ref, latent_ref, rope_ref, cos_ref, sin_ref, query_rows):
-    query_w, latent_w = head_weights(weights_ref, query_rows)
+def head_queries(query_w, query_t_ref, cos_ref, sin_ref):
     half = ROPE // 2
     proj_t = dot_plain(query_w.T, query_t_ref[...])
-    first, second = proj_t[NOPE : NOPE + half], proj_t[NOPE + half : NOPE + ROPE]
     cosine, sine = cos_ref[...], sin_ref[...]
-    query_t = jnp.concatenate(
-        [
-            proj_t[:NOPE],
-            first * cosine - second * sine,
-            second * cosine + first * sine,
-            proj_t[NOPE + ROPE :],
-        ],
-        axis=0,
-    ).astype(BF)
-    both = dot_plain(latent_ref[...], latent_w).astype(BF)
+    queries = []
+    for begin in range(0, proj_t.shape[0], HEAD):
+        head_t = proj_t[begin : begin + HEAD]
+        first, second = head_t[NOPE : NOPE + half], head_t[NOPE + half : NOPE + ROPE]
+        queries.append(
+            jnp.concatenate(
+                [
+                    head_t[:NOPE],
+                    first * cosine - second * sine,
+                    second * cosine + first * sine,
+                    head_t[NOPE + ROPE :],
+                ],
+                axis=0,
+            ).astype(BF)
+        )
+    return queries
+
+
+def head_tile(both, rope_rows, index):
+    both = both[:, index * HEAD : (index + 1) * HEAD]
     lane = lax.broadcasted_iota(jnp.int32, both.shape, 1)
-    keys = jnp.where(lane < NOPE, both, rope_ref[...])
-    return (query_w, latent_w, query_t, keys, both)
+    return (jnp.where(lane < NOPE, both, rope_rows), both)
 
 
 def attend_kernel(
     query_rows, tile, weights_ref, query_t_ref, latent_ref, rope_ref, cos_ref, sin_ref, bias_ref,
     mixed_ref, lse_ref, scores_ref,
 ):
-    _, _, query_t, keys, both = head_vectors(
-        weights_ref, query_t_ref, latent_ref, rope_ref, cos_ref, sin_ref, query_rows
-    )
-    values_t = both.T[NOPE:]
-    length = keys.shape[0]
-    top = None
-    for begin in range(0, length, tile):
-        part = dot_plain(keys[begin : begin + tile], query_t) * (SCALE * LOG2E)
-        part = part + bias_ref[begin : begin + tile, :]
-        scores_ref[begin : begin + tile, :] = part
-        tile_top = jnp.max(part, axis=0, keepdims=True)
-        top = tile_top if top is None else jnp.maximum(top, tile_top)
-    total, out_t = None, None
-    for begin in range(0, length, tile):
-        expo = jnp.exp2(scores_ref[begin : begin + tile, :] - top)
-        tile_sum = jnp.sum(expo, axis=0, keepdims=True)
-        term = dot_plain(values_t[:, begin : begin + tile], expo.astype(BF))
-        total = tile_sum if total is None else total + tile_sum
-        out_t = term if out_t is None else out_t + term
-    mixed_ref[...] = (out_t / total).astype(BF)
-    lse_ref[0] = top + jnp.log2(total)
+    query_w, latent_w = head_weights(weights_ref, query_rows)
+    queries = head_queries(query_w, query_t_ref, cos_ref, sin_ref)
+    projected = dot_plain(latent_ref[...], latent_w).astype(BF)
+    length = projected.shape[0]
+    for index, query_t in enumerate(queries):
+        keys, both = head_tile(projected, rope_ref[...], index)
+        values_t = both.T[NOPE:]
+        top = None
+        for begin in range(0, length, tile):
+            rows = slice(begin, begin + tile)
+            part = dot_plain(keys[rows], query_t) * (SCALE * LOG2E) + bias_ref[rows, :]
+            scores_ref[index, rows, :] = part
+            tile_top = jnp.max(part, axis=0, keepdims=True)
+            top = tile_top if top is None else jnp.maximum(top, tile_top)
+        total, out_t = None, None
+        for begin in range(0, length, tile):
+            rows = slice(begin, begin + tile)
+            expo = jnp.exp2(scores_ref[index, rows, :] - top)
+            tile_sum = jnp.sum(expo, axis=0, keepdims=True)
+            term = dot_plain(values_t[:, rows], expo.astype(BF))
+            total = tile_sum if total is None else total + tile_sum
+            out_t = term if out_t is None else out_t + term
+        mixed_ref[index * VDIM : (index + 1) * VDIM, :] = (out_t / total).astype(BF)
+        lse_ref[index] = top + jnp.log2(total)
 
 
 def attend_back_kernel(
-    query_rows, tile, weights_ref, query_t_ref, latent_ref, latent_t_ref, rope_ref, cos_ref,
-    sin_ref, bias_ref, mixed_ref, grad_ref, lse_ref, query_before_ref, latent_before_ref, *rest,
+    query_rows, tile, weights_ref, query_t_ref, latent_ref, latent_t_ref, rope_ref,
+    cos_ref, sin_ref, bias_ref, mixed_ref, grad_ref, lse_ref, query_before_ref, latent_before_ref,
+    *rest,
 ):
     weights_grad_ref, query_acc, latent_acc, both_scr = rest[-4:]
-    head = pl.program_id(0)
     kv_rank = latent_ref.shape[1]
-    query_w, latent_w, query_t, keys, both = head_vectors(
-        weights_ref, query_t_ref, latent_ref, rope_ref, cos_ref, sin_ref, query_rows
-    )
-
-    @pl.when(head == 0)
+    query_w, latent_w = head_weights(weights_ref, query_rows)
+    queries = head_queries(query_w, query_t_ref, cos_ref, sin_ref)
+    projected = dot_plain(latent_ref[...], latent_w).astype(BF)
+    length = projected.shape[0]
+
+    @pl.when(pl.program_id(0) == 0)
     def _():
         query_acc[...] = query_before_ref[...]
         latent_acc[...] = latent_before_ref[...]
 
-    keys_t = keys.T
-    query = query_t.T
-    grad_t = grad_ref[...]
-    delta = jnp.sum(
-        grad_t.astype(F32) * mixed_ref[...].astype(F32), axis=0, keepdims=True
-    )
-    grad_pad_t = jnp.concatenate([jnp.zeros_like(grad_t), grad_t], axis=0)
-    grad_pad = grad_pad_t.T
-    lse = lse_ref[0]
-    length = keys.shape[0]
-    query_back_t = None
-    for begin in range(0, length, tile):
-        rows = slice(begin, begin + tile)
-        scores = dot_plain(keys[rows], query_t) * (SCALE * LOG2E)
-        probs = jnp.exp2(scores + bias_ref[rows, :] - lse)
-        prob_grad = dot_plain(both[rows], grad_pad_t)
-        score_grad = (probs * (prob_grad - delta)).astype(BF)
-        term = dot_plain(keys_t[:, rows], score_grad)
-        query_back_t = term if query_back_t is None else query_back_t + term
-        key_back = dot_plain(score_grad, query) * SCALE
-        value_back = dot_plain(probs.astype(BF), grad_pad)
-        lane = lax.broadcasted_iota(jnp.int32, key_back.shape, 1)
-        latent_acc[rows, kv_rank:] += key_back
-        both_scr[rows, :] = jnp.where(lane < NOPE, key_back, value_back).astype(BF)
-    query_back_t = query_back_t * SCALE
     half = ROPE // 2
-    first, second = query_back_t[NOPE : NOPE + half], query_back_t[NOPE + half : NOPE + ROPE]
     cosine, sine = cos_ref[...], sin_ref[...]
-    query_back_t = jnp.concatenate(
-        [
-            query_back_t[:NOPE],
+    backs = []
+    for index, query_t in enumerate(queries):
+        part = slice(index * VDIM, (index + 1) * VDIM)
+        lanes = slice(index * HEAD, (index + 1) * HEAD)
+        keys, both = head_tile(projected, rope_ref[...], index)
+        keys_t, query = keys.T, query_t.T
+        grad_t = grad_ref[part, :]
+        delta = jnp.sum(
+            grad_t.astype(F32) * mixed_ref[part, :].astype(F32), axis=0, keepdims=True
+        )
+        grad_pad_t = jnp.concatenate([jnp.zeros_like(grad_t), grad_t], axis=0)
+        grad_pad = grad_pad_t.T
+        lse = lse_ref[index]
+        back_t = None
+        for begin in range(0, length, tile):
+            rows = slice(begin, begin + tile)
+            scores = dot_plain(keys[rows], query_t) * (SCALE * LOG2E)
+            probs = jnp.exp2(scores + bias_ref[rows, :] - lse)
+            prob_grad = dot_plain(both[rows], grad_pad_t)
+            score_grad = (probs * (prob_grad - delta)).astype(BF)
+            term = dot_plain(keys_t[:, rows], score_grad)
+            back_t = term if back_t is None else back_t + term
+            key_back = dot_plain(score_grad, query) * SCALE
+            value_back = dot_plain(probs.astype(BF), grad_pad)
+            latent_acc[rows, kv_rank:] += key_back
+            lane = lax.broadcasted_iota(jnp.int32, key_back.shape, 1)
+            both_scr[rows, lanes] = jnp.where(lane < NOPE, key_back, value_back).astype(BF)
+        back_t = back_t * SCALE
+        first, second = back_t[NOPE : NOPE + half], back_t[NOPE + half : NOPE + ROPE]
+        backs += [
+            back_t[:NOPE],
             first * cosine + second * sine,
             second * cosine - first * sine,
-            jnp.zeros_like(query_back_t[NOPE + ROPE :]),
-        ],
-        axis=0,
-    ).astype(BF)
+            jnp.zeros_like(back_t[NOPE + ROPE :]),
+        ]
     both_back = both_scr[...]
+    latent_acc[:, :kv_rank] += dot_trans_right(both_back, latent_w)
+    query_back_t = jnp.concatenate(backs, axis=0).astype(BF)
     query_acc[...] += dot_plain(query_w, query_back_t)
-    latent_acc[:, :kv_rank] += dot_trans_right(both_back, latent_w)
-    query_wg = dot_trans_right(query_t_ref[...], query_back_t)
-    latent_wg = dot_plain(latent_t_ref[...], both_back)
-    col_total = weights_ref.shape[1]
-    weights_grad_ref[0, :, :query_rows, :] = query_wg.astype(BF).reshape(col_total, query_rows, HEAD)
-    weights_grad_ref[0, :, query_rows:, :] = latent_wg.astype(BF).reshape(col_total, -1, HEAD)
+    query_wg = dot_trans_right(query_t_ref[...], query_back_t).astype(BF)
+    latent_wg = dot_plain(latent_t_ref[...], both_back).astype(BF)
+    col_total, lanes = weights_ref.shape[1], weights_ref.shape[3]
+    weights_grad_ref[:, 0, :query_rows, :] = query_wg.reshape(col_total, query_rows, lanes)
+    weights_grad_ref[:, 0, query_rows:, :] = latent_wg.reshape(col_total, -1, lanes)
 
 
 def whole(shape):
-    return pl.BlockSpec(shape, lambda head: (0,) * len(shape))
+    return pl.BlockSpec(shape, lambda step: (0,) * len(shape))
 
 
 def attend(weights, query_t, latent, rope, cos_t, sin_t, bias_t, query_rows, block):
     _, col_total, _, pack_cols = weights.shape
     pack_rows = query_rows + latent.shape[1] // col_total
     heads = pack_cols // HEAD
+    group = math.gcd(heads, 2)
     length, local = bias_t.shape
     tile = math.gcd(length, 256)
     return pl.pallas_call(
         functools.partial(attend_kernel, query_rows, tile),
-        grid=(heads,),
+        grid=(heads // group,),
         in_specs=[
-            pl.BlockSpec((1, col_total, pack_rows, HEAD), lambda head: (block, 0, 0, head)),
+            pl.BlockSpec(
+                (1, col_total, pack_rows, group * HEAD), lambda step: (block, 0, 0, step)
+            ),
             whole(query_t.shape),
             whole(latent.shape),
             whole(rope.shape),
@@ -223,19 +239,21 @@
             whole(bias_t.shape),
         ],
         out_specs=[
-            pl.BlockSpec((VDIM, local), lambda head: (head, 0)),
-            pl.BlockSpec((1, 1, local), lambda head: (head, 0, 0)),
+            pl.BlockSpec((group * VDIM, local), lambda step: (step, 0)),
+            pl.BlockSpec((group, 1, local), lambda step: (step, 0, 0)),
         ],
         out_shape=[
             jax.ShapeDtypeStruct((heads * VDIM, local), BF),
             jax.ShapeDtypeStruct((heads, 1, local), F32),
         ],
-        scratch_shapes=[pltpu.VMEM((length, local), F32)],
+        scratch_shapes=[
+            pltpu.VMEM((group, length, local), F32),
+        ],
         compiler_params=pltpu.CompilerParams(
             dimension_semantics=("arbitrary",), vmem_limit_bytes=48 * 1024 * 1024
         ),
         cost_estimate=pl.CostEstimate(
-            flops=heads * 1_700_000_000,
+            flops=heads * 1_200_000_000,
             bytes_accessed=weights[0].size * 2,
             transcendentals=heads * local * length,
         ),
@@ -251,13 +269,17 @@
     more = [] if weights_before is None else [weights_before]
     pack_rows = query_rows + latent.shape[1] // col_total
     heads = pack_cols // HEAD
+    group = math.gcd(heads, 2)
+    steps = heads // group
     length, local = bias_t.shape
     tile = math.gcd(length, 256)
     return pl.pallas_call(
         functools.partial(attend_back_kernel, query_rows, tile),
-        grid=(heads,),
+        grid=(steps,),
         in_specs=[
-            pl.BlockSpec((1, col_total, pack_rows, HEAD), lambda head: (block, 0, 0, head)),
+            pl.BlockSpec(
+                (1, col_total, pack_rows, group * HEAD), lambda step: (block, 0, 0, step)
+            ),
             whole(query_t.shape),
             whole(latent.shape),
             whole(latent_t.shape),
@@ -265,30 +287,34 @@
             whole(cos_t.shape),
             whole(sin_t.shape),
             whole(bias_t.shape),
-            pl.BlockSpec((VDIM, local), lambda head: (head, 0)),
-            pl.BlockSpec((VDIM, local), lambda head: (block * heads + head, 0)),
-            pl.BlockSpec((1, 1, local), lambda head: (head, 0, 0)),
+            pl.BlockSpec((group * VDIM, local), lambda step: (step, 0)),
+            pl.BlockSpec((group * VDIM, local), lambda step: (block * steps + step, 0)),
+            pl.BlockSpec((group, 1, local), lambda step: (step, 0, 0)),
             whole(query_before.shape),
             whole(latent_before.shape),
         ]
         + [pl.BlockSpec(memory_space=pl.ANY)] * len(more),
         out_specs=[
-            pl.BlockSpec((1, col_total, pack_rows, HEAD), lambda head: (block, 0, 0, head)),
+            pl.BlockSpec(
+                (col_total, 1, pack_rows, group * HEAD), lambda step: (0, block, 0, step)
+            ),
             whole(query_before.shape),
             whole(latent_before.shape),
         ],
         out_shape=[
-            jax.ShapeDtypeStruct((row_total, col_total, pack_rows, pack_cols), BF),
+            jax.ShapeDtypeStruct((col_total, row_total, pack_rows, pack_cols), BF),
             jax.ShapeDtypeStruct(query_before.shape, F32),
             jax.ShapeDtypeStruct(latent_before.shape, F32),
         ],
         input_output_aliases={13: 0} if more else {},
-        scratch_shapes=[pltpu.VMEM((length, HEAD), BF)],
+        scratch_shapes=[
+            pltpu.VMEM((length, group * HEAD), BF),
+        ],
         compiler_params=pltpu.CompilerParams(
             dimension_semantics=("arbitrary",), vmem_limit_bytes=48 * 1024 * 1024
         ),
         cost_estimate=pl.CostEstimate(
-            flops=heads * 4_200_000_000,
+            flops=heads * 2_500_000_000,
             bytes_accessed=weights[0].size * 4,
             transcendentals=heads * local * length,
         ),
@@ -334,25 +360,25 @@
 
 
 def out_grad_kernel(tokens_ref, mixed_ref, out_ref):
-    out_ref[0] = dot_trans_right(tokens_ref[...].T, mixed_ref[...]).astype(BF)
+    out_ref[...] = dot_trans_right(tokens_ref[...].T, mixed_ref[...]).astype(BF)
 
 
 def out_weight_grad(tokens, mixed):
     rows, width = tokens.shape
-    row_total, units, _ = mixed.shape
-    tile = math.gcd(width, 512)
+    units = mixed.shape[0]
+    tile = math.gcd(width, 256)
     return pl.pallas_call(
         out_grad_kernel,
-        grid=(row_total, width // tile),
+        grid=(width // tile,),
         in_specs=[
-            pl.BlockSpec((rows, tile), lambda block, step: (0, step)),
-            pl.BlockSpec((None, units, rows), lambda block, step: (block, 0, 0)),
-        ],
-        out_specs=pl.BlockSpec((1, tile, units), lambda block, step: (block, step, 0)),
-        out_shape=jax.ShapeDtypeStruct((row_total, width, units), BF),
+            pl.BlockSpec((rows, tile), lambda step: (0, step)),
+            pl.BlockSpec((units, rows), lambda step: (0, 0)),
+        ],
+        out_specs=pl.BlockSpec((tile, units), lambda step: (step, 0)),
+        out_shape=jax.ShapeDtypeStruct((width, units), BF),
         cost_estimate=pl.CostEstimate(
-            flops=2 * rows * width * units * row_total,
-            bytes_accessed=2 * row_total * width * units,
+            flops=2 * rows * width * units,
+            bytes_accessed=2 * width * units,
             transcendentals=0,
         ),
         name="out_wg",
@@ -396,16 +422,22 @@
 
 
 def gather_kernel(
-    row_total, col_total, own_ref, out_ref, own_sem, line_send, line_recv, chip_send, chip_recv,
-    core_send, core_recv,
+    row_total, col_total, arrays, *refs,
 ):
+    own_refs, out_refs = refs[:arrays], refs[arrays : 2 * arrays]
+    own_sem, line_send, line_recv, chip_send, chip_recv, core_send, core_recv = refs[2 * arrays :]
     row_rank, col_rank = lax.axis_index("row"), lax.axis_index("col")
     bits = chip_bits(col_total)
     masks = 2 ** len(bits)
-    own = pltpu.make_async_copy(own_ref, out_ref.at[row_rank, col_rank], own_sem)
-    own.start()
+    owns = [
+        pltpu.make_async_copy(own_ref, out_ref.at[row_rank, col_rank], own_sem.at[at])
+        for at, (own_ref, out_ref) in enumerate(zip(own_refs, out_refs))
+    ]
+    for own in owns:
+        own.start()
     greet(row_total, row_rank, col_rank, bits)
-    own.wait()
+    for own in owns:
+        own.wait()
 
     def block_col(row, mask):
         index = col_rank
@@ -414,27 +446,29 @@
                 index = flip(index, turn_bit(bits, row, step, row_total))
         return index
 
-    def line_copy(way, row):
-        ref = out_ref.at[row, col_rank]
+    def line_copy(at, way, row):
+        ref = out_refs[at].at[row, col_rank]
         return pltpu.make_async_remote_copy(
-            src_ref=ref, dst_ref=ref, send_sem=line_send.at[way, row], recv_sem=line_recv.at[row],
+            src_ref=ref, dst_ref=ref, send_sem=line_send.at[at, way, row],
+            recv_sem=line_recv.at[at, row],
             device_id=(row_rank + 1 - 2 * way, col_rank), device_id_type=MESH,
         )
 
-    def chip_copy(row, mask, step):
-        ref = out_ref.at[row, block_col(row, mask)]
+    def chip_copy(at, row, mask, step):
+        ref = out_refs[at].at[row, block_col(row, mask)]
         to = mask + 2**step
         return pltpu.make_async_remote_copy(
-            src_ref=ref, dst_ref=ref, send_sem=chip_send.at[row, to], recv_sem=chip_recv.at[row, to],
+            src_ref=ref, dst_ref=ref, send_sem=chip_send.at[at, row, to],
+            recv_sem=chip_recv.at[at, row, to],
             device_id=(row_rank, flip(col_rank, turn_bit(bits, row, step, row_total))),
             device_id_type=MESH,
         )
 
-    def core_copy(row, mask):
-        ref = out_ref.at[row, block_col(row, mask)]
+    def core_copy(at, row, mask):
+        ref = out_refs[at].at[row, block_col(row, mask)]
         return pltpu.make_async_remote_copy(
-            src_ref=ref, dst_ref=ref, send_sem=core_send.at[row, mask],
-            recv_sem=core_recv.at[row, mask], device_id=(row_rank, flip(col_rank, 1)),
+            src_ref=ref, dst_ref=ref, send_sem=core_send.at[at, row, mask],
+            recv_sem=core_recv.at[at, row, mask], device_id=(row_rank, flip(col_rank, 1)),
             device_id_type=MESH,
         )
 
@@ -448,73 +482,82 @@
                     act(row, away, side)
 
     def arrive(row, away, side):
-        if away > 0:
-            line_copy(0, row).wait_recv()
-        if side <= 0:
-
-            @pl.when(row_rank < row_total - 1)
-            def _():
-                line_copy(0, row).start()
-
-        if side >= 0:
-
-            @pl.when(row_rank > 0)
-            def _():
-                line_copy(1, row).start()
-
-        for step in range(len(bits)):
-            chip_copy(row, 0, step).start()
-        core_copy(row, 0).start()
+        for at in range(arrays):
+            if away > 0:
+                line_copy(at, 0, row).wait_recv()
+            if side <= 0:
+
+                @pl.when(row_rank < row_total - 1)
+                def _():
+                    line_copy(at, 0, row).start()
+
+            if side >= 0:
+
+                @pl.when(row_rank > 0)
+                def _():
+                    line_copy(at, 1, row).start()
+
+            for step in range(len(bits)):
+                chip_copy(at, row, 0, step).start()
+            core_copy(at, row, 0).start()
 
     by_distance(arrive)
     for mask in range(1, masks):
         top = mask.bit_length() - 1
 
         def forward(row, away, side):
-            chip_copy(row, mask - 2**top, top).wait_recv()
-            for step in range(top + 1, len(bits)):
-                chip_copy(row, mask, step).start()
-            core_copy(row, mask).start()
+            for at in range(arrays):
+                chip_copy(at, row, mask - 2**top, top).wait_recv()
+                for step in range(top + 1, len(bits)):
+                    chip_copy(at, row, mask, step).start()
+                core_copy(at, row, mask).start()
 
         by_distance(forward)
-    for row in range(row_total):
-        for mask in range(masks):
-            core_copy(row, mask).wait()
-            if mask > 0:
-                top = mask.bit_length() - 1
-                chip_copy(row, mask - 2**top, top).wait_send()
-
-        @pl.when((row <= row_rank) & (row_rank < row_total - 1))
-        def _():
-            line_copy(0, row).wait_send()
-
-        @pl.when((row >= row_rank) & (row_rank > 0))
-        def _():
-            line_copy(1, row).wait_send()
+    for at in range(arrays):
+        for row in range(row_total):
+            for mask in range(masks):
+                core_copy(at, row, mask).wait()
+                if mask > 0:
+                    top = mask.bit_length() - 1
+                    chip_copy(at, row, mask - 2**top, top).wait_send()
+
+            @pl.when((row <= row_rank) & (row_rank < row_total - 1))
+            def _():
+                line_copy(at, 0, row).wait_send()
+
+            @pl.when((row >= row_rank) & (row_rank > 0))
+            def _():
+                line_copy(at, 1, row).wait_send()
 
 
 def gather_all(values, collective_id, name):
     row_total, col_total = lax.axis_size("row"), lax.axis_size("col")
     masks = 2 ** len(chip_bits(col_total))
+    arrays = len(values)
+    sem = pltpu.SemaphoreType.DMA
+    anywhere = pl.BlockSpec(memory_space=pl.ANY)
     return pl.pallas_call(
-        functools.partial(gather_kernel, row_total, col_total),
-        in_specs=[pl.BlockSpec(memory_space=pl.ANY)],
-        out_specs=pl.BlockSpec(memory_space=pl.ANY),
-        out_shape=jax.ShapeDtypeStruct((row_total, col_total) + values.shape, values.dtype),
+        functools.partial(gather_kernel, row_total, col_total, arrays),
+        in_specs=[anywhere] * arrays,
+        out_specs=[anywhere] * arrays,
+        out_shape=[
+            jax.ShapeDtypeStruct((row_total, col_total) + array.shape, array.dtype)
+            for array in values
+        ],
         scratch_shapes=[
-            pltpu.SemaphoreType.DMA,
-            pltpu.SemaphoreType.DMA((2, row_total)),
-            pltpu.SemaphoreType.DMA((row_total,)),
-            pltpu.SemaphoreType.DMA((row_total, masks)),
-            pltpu.SemaphoreType.DMA((row_total, masks)),
-            pltpu.SemaphoreType.DMA((row_total, masks)),
-            pltpu.SemaphoreType.DMA((row_total, masks)),
+            sem((arrays,)),
+            sem((arrays, 2, row_total)),
+            sem((arrays, row_total)),
+            sem((arrays, row_total, masks)),
+            sem((arrays, row_total, masks)),
+            sem((arrays, row_total, masks)),
+            sem((arrays, row_total, masks)),
         ],
         compiler_params=pltpu.CompilerParams(
             collective_id=collective_id, has_side_effects=True
         ),
         name=name,
-    )(values)
+    )(*values)
 
 
 def add_into(total_ref, other_ref):
@@ -565,6 +608,17 @@
                 self.copy(way, self.row_rank).wait_recv()
                 add_into(self.block(self.row_rank), self.landed.at[way, self.row_rank])
 
+    def load(self, from_ref, row):
+        rows = from_ref.shape[1]
+        tile = math.gcd(rows, 32)
+
+        def one(step, carry):
+            here = pl.ds(pl.multiple_of(step * tile, tile), tile)
+            self.block(row)[here, :] = from_ref[row, here, :]
+            return carry
+
+        lax.fori_loop(0, rows // tile, one, 0)
+
     def finish(self, out_ref):
         rows = out_ref.shape[0]
         tile = math.gcd(rows, 32)
@@ -584,10 +638,10 @@
                     self.copy(way, row).wait_send()
 
 
-def reduce_kernel(
-    row_total, col_total, part_ref, out_ref, sums, chip_buf, line_buf, core_send, core_recv,
-    chip_send, chip_recv, line_send, line_recv,
-):
+def reduce_kernel(row_total, col_total, part_ref, side_ref, out_ref, side_out_ref, *scratch):
+    sums, chip_buf, line_buf, side_sums, side_buf = scratch[:5]
+    core_send, core_recv, chip_send, chip_recv = scratch[5:9]
+    line_send, line_recv, side_send, side_recv = scratch[9:]
     row_rank, col_rank = lax.axis_index("row"), lax.axis_index("col")
     bits = chip_bits(col_total)
     count = len(bits)
@@ -629,6 +683,12 @@
             add_into(sums.at[row, mask], part_ref.at[row, chip_at(row, mask), core])
             if mask >= masks // 2:
                 chip_copy(row, mask, count - 1).start()
+    side = LineReduce(
+        row_total, row_rank, col_rank, lambda row: side_sums.at[row], side_buf, side_send, side_recv
+    )
+    for row in range(row_total):
+        side.load(side_ref, row)
+    side.run()
     for step in range(count - 1, -1, -1):
         half = 2**step
         for mask in range(half - 1, -1, -1):
@@ -642,6 +702,7 @@
     )
     line.run()
     line.finish(out_ref)
+    side.finish(side_out_ref)
     for row in range(row_total):
         for mask in range(masks):
             core_copy(row, mask).wait_send()
@@ -649,36 +710,50 @@
                 chip_copy(row, mask, mask.bit_length() - 1).wait_send()
 
 
-def reduce_all(parts, collective_id, name):
+def whole_tiles(values):
+    rows = values.shape[-2]
+    more = -rows % 16
+    return jnp.pad(values, ((0, 0),) * (values.ndim - 2) + ((0, more), (0, 0))) if more else values
+
+
+def reduce_all(parts, side, collective_id, name):
     row_total, col_total, own_rows, lanes = parts.shape
-    rows = -(-own_rows // 16) * 16
-    if rows != own_rows:
-        parts = jnp.pad(parts, ((0, 0), (0, 0), (0, rows - own_rows), (0, 0)))
+    own_side = side.shape[1]
+    parts, side = whole_tiles(parts), whole_tiles(side)
+    rows = parts.shape[2]
     parts = parts.reshape(row_total, col_total // 2, 2, rows, lanes)
     masks = col_total // 2
     sem = pltpu.SemaphoreType.DMA
     vmem = pl.BlockSpec(memory_space=pltpu.VMEM)
-    return pl.pallas_call(
+    out, side_out = pl.pallas_call(
         functools.partial(reduce_kernel, row_total, col_total),
-        in_specs=[vmem],
-        out_specs=vmem,
-        out_shape=jax.ShapeDtypeStruct((rows, lanes), F32),
+        in_specs=[vmem, vmem],
+        out_specs=[vmem, vmem],
+        out_shape=[
+            jax.ShapeDtypeStruct((rows, lanes), F32),
+            jax.ShapeDtypeStruct(side.shape[1:], F32),
+        ],
         scratch_shapes=[
             pltpu.VMEM((row_total, masks, rows, lanes), BF),
             pltpu.VMEM((row_total, masks, rows, lanes), BF),
             pltpu.VMEM((2, row_total, rows, lanes), BF),
+            pltpu.VMEM(side.shape, BF),
+            pltpu.VMEM((2,) + side.shape, BF),
             sem((row_total, masks)),
             sem((row_total, masks)),
             sem((row_total, masks)),
             sem((row_total, masks)),
             sem((2, row_total)),
             sem((2, row_total)),
+            sem((2, row_total)),
+            sem((2, row_total)),
         ],
         compiler_params=pltpu.CompilerParams(
             collective_id=collective_id, has_side_effects=True, vmem_limit_bytes=48 * 1024 * 1024
         ),
         name=name,
-    )(parts)[:own_rows]
+    )(parts, side)
+    return (out[:own_rows], side_out[:own_side])
 
 
 together = lax.optimization_barrier
@@ -813,24 +888,17 @@
     ).reshape(query_rows, heads_here * HEAD)
     up_pack = jnp.concatenate([query_pack, latent_up], axis=0)
     pack_rows = up_pack.shape[0]
-    if up_pack.shape[1] >= pack_wide:
-        head_w = gather_all(
-            jnp.concatenate([up_pack, pad_to(down_pack, up_pack.shape[1])]), 1, "gather_pack"
-        )
-        down_all = head_w[:, :, pack_rows:, :pack_wide]
-    else:
-        head_w = gather_all(up_pack, 1, "gather_up")
-        down_all = gather_all(down_pack, 2, "gather_down")
+    down_all, head_w = gather_all([down_pack, up_pack], 1, "gather_pack")
     down_all = down_all.reshape(devices * down_rows, pack_wide)
-    down_all, out_here = together((down_all, output_weight.T))
-    out_all = lax.all_gather(out_here, both_axes, axis=0, tiled=True).reshape(
-        row_total, width, heads_here * VDIM
-    )
     attn_g = down_all[:, lat_wide].astype(F32)
     mlp_g = down_all[:, lat_wide + 1].astype(F32)
     misc_all = down_all[:, lat_wide + 2].astype(F32).reshape(devices, down_rows)
     query_g = misc_all[:, :q_part].reshape(-1)
     latent_g = misc_all[:, q_part : q_part + kv_part].reshape(-1)
+    query_g, out_here = together((query_g, output_weight.T))
+    out_all = lax.all_gather(out_here, both_axes, axis=0, tiled=True).reshape(
+        row_total, width, heads_here * VDIM
+    )
     counts = jnp.sum(misc_all[:, q_part + kv_part : q_part + kv_part + 2], axis=0)
     valid_total = counts[0] * 256.0 + counts[1]
 
@@ -859,18 +927,43 @@
     while latent_give.advance_into():
         pass
     latent_all = together(latent_give.value)
-    kv_all = latent_all[:, :KV_RANK]
-    rope_all = latent_all[:, KV_RANK:]
-
+    blocks = latent_all.reshape(row_total, local_rows, -1)
+    froms = [lax.rem(row_rank + row_total - step, row_total) for step in range(row_total)]
+    latent_all = jnp.concatenate(
+        [lax.dynamic_index_in_dim(blocks, at, 0, keepdims=False) for at in froms]
+    )
+
+    kept = 0
+    for block in range(row_total):
+        begin = block * local_rows
+        ahead = [CONTS - at for at in range(1, CONTS + 1) if begin < length - (CONTS - at) * CONT_LEN]
+        passed = CONTS - 1 - max(ahead)
+        kept = max(kept, begin + local_rows - passed * CONT_LEN)
+    kept = min(length, -(-kept // 256) * 256)
     query_at = offset + jnp.arange(local_rows, dtype=jnp.int32)
     query_seg = lax.dynamic_slice_in_dim(segments, offset, local_rows, 0)
-    begins = [
-        lax.rem(row_rank + row_total - step, row_total) * local_rows for step in range(row_total)
-    ]
-    key_at = jnp.concatenate([begin + jnp.arange(local_rows, dtype=jnp.int32) for begin in begins])
-    key_seg = jnp.concatenate(
-        [lax.dynamic_slice_in_dim(segments, begin, local_rows, 0) for begin in begins]
-    )
+    prompt = jnp.sum((segments == 0).astype(jnp.int32))
+    shift = jnp.maximum(jnp.sum((segments < query_seg[0]).astype(jnp.int32)) - prompt, 0)
+
+    def keep(values):
+        far = jnp.pad(values, ((0, kept),) + ((0, 0),) * (values.ndim - 1))
+        far = lax.dynamic_slice_in_dim(far, shift, kept, 0)
+        near = jnp.arange(kept, dtype=jnp.int32) < prompt
+        return jnp.where(near.reshape((kept,) + (1,) * (values.ndim - 1)), values[:kept], far)
+
+    def spread(values):
+        places = jnp.arange(length, dtype=jnp.int32)[:, None]
+        near = jnp.pad(values, ((0, length - kept), (0, 0)))
+        far = jnp.pad(values, ((length, length - kept), (0, 0)))
+        far = lax.dynamic_slice_in_dim(far, length - shift, length, 0)
+        return jnp.where(places < prompt, near, jnp.where(places < prompt + shift, 0.0, far))
+
+    kept_all = keep(latent_all)
+    kv_all = kept_all[:, :KV_RANK]
+    rope_all = kept_all[:, KV_RANK:]
+    key_at = jnp.arange(kept, dtype=jnp.int32)
+    key_at = jnp.where(key_at < prompt, key_at, key_at + shift)
+    key_seg = keep(segments)
     allowed_t = (key_at[:, None] <= query_at[None, :]) & (
         (key_seg[:, None] == 0) | (key_seg[:, None] == query_seg[None, :])
     )
@@ -1005,14 +1098,11 @@
     attn_grad_in = (RES * residual_grad).astype(BF)
     grad_t = dot_dims(out_all, attn_grad_in, (1,), (1,)).astype(BF)
     latent_t = kv_all.T
-    out_wg = out_weight_grad(attn_grad_in, jnp.stack([mixed_t for mixed_t, _ in mixed]))
+    out_wg = out_weight_grad(attn_grad_in, jnp.concatenate([mixed_t for mixed_t, _ in mixed]))
     grad_t, out_wg = together((grad_t.reshape(-1, local_rows), out_wg))
-    out_wg = lax.psum_scatter(
-        out_wg.reshape(row_total * width, heads_here * VDIM),
-        both_axes, scatter_dimension=0, tiled=True,
-    )
+    out_wg = lax.psum_scatter(out_wg, "col", scatter_dimension=0, tiled=True)
     query_back_t = jnp.zeros(query_t.shape, F32)
-    latent_back = jnp.zeros(latent_all.shape, F32)
+    latent_back = jnp.zeros(kept_all.shape, F32)
     head_wg = None
     for block, (mixed_t, lse) in enumerate(mixed):
         if block == cut:
@@ -1021,16 +1111,14 @@
             head_w, query_t, kv_all, latent_t, rope_all, cos_t, sin_t, bias_t, mixed_t,
             grad_t, lse, query_back_t, latent_back, head_wg, query_rows, block,
         )
-    head_wg, out_wg = together((head_wg, out_wg))
-    out_wg = out_wg.astype(F32).T
     head_wg = lax.psum_scatter(
-        head_wg.reshape(devices * pack_rows, heads_here * HEAD),
-        both_axes, scatter_dimension=0, tiled=True,
-    ).astype(F32)
-    latent_rows = latent_back.astype(BF)
+        head_wg.reshape(devices * pack_rows, heads_here * HEAD), "col",
+        scatter_dimension=0, tiled=True,
+    ).reshape(row_total, pack_rows, heads_here * HEAD)
+    latent_rows = spread(latent_back).astype(BF).reshape(blocks.shape)
     latent_reduce = Task(
         reduce_steps(
-            [latent_rows[at * local_rows : (at + 1) * local_rows] for at in range(row_total)]
+            [lax.dynamic_index_in_dim(latent_rows, at, 0, keepdims=False) for at in froms]
         )
     )
     while latent_reduce.advance_into():
@@ -1072,7 +1160,18 @@
     small = jnp.where(lane == lat_wide + 1, mlp_gain_grad[:, None], small)
     small = jnp.where(lane == lat_wide + 2, misc_grad, small).astype(BF)
     small = small.reshape(row_total, col_total, down_rows, pack_wide)
-    small = reduce_all(small, 3, "reduce_down")
+    units = heads_here * VDIM
+    out_wg = jnp.stack(
+        [out_wg[:, at * units : (at + 1) * units] for at in range(row_total)]
+    )
+    small, out_wg = reduce_all(small, out_wg, 3, "reduce_down")
+    out_wg = out_wg.T
+    small, head_wg = together((small, head_wg))
+    head_reduce = Task(
+        reduce_steps([lax.dynamic_index_in_dim(head_wg, at, 0, keepdims=False) for at in froms])
+    )
+    slots(hops, head_reduce)
+    head_wg = head_reduce.result()
     qu_wg = head_wg[:query_rows].reshape(query_rows, heads_here, HEAD)[:, :, : NOPE + ROPE]
     qu_wg = qu_wg.reshape(query_rows, heads_here * (NOPE + ROPE))
     kvu_wg = head_wg[query_rows:]

time: 1360 us -> 1210 us (0.89)
  Pallas kernels: 507 us -> 394 us
  waiting for transfers between devices: 320 us -> 243 us
  starting transfers between devices: 129 us -> 149 us
    pallas_call x4, Pallas kernels: 174 us -> 105 us  [attend_back(): pl.pallas_call(functools.partial(attend_back_kernel, query_rows, tile), g...]
    ppermute x15, waiting for transfers between devices: 176 us -> 123 us  [gather_steps(): lax.ppermute(ways[1], 'row', [(i, i - 1) for i in range(1, total - step +...]
    reduce_scatter x1, waiting for transfers between devices: 31.9 us -> 0.01 us  [body(): out_wg = lax.psum_scatter(out_wg, 'col', scatter_dimension=0, tiled=True)]
    pallas_call x4, Pallas kernels: 67 us -> 43.8 us  [attend(): pl.pallas_call(functools.partial(attend_kernel, query_rows, tile), grid=(...]
    dynamic_slice x0 -> x9, local copies, waits for them, and re-layouts: none -> 17.6 us  [the longest x5 15.3 us: body(): lax.dynamic_index_in_dim(blocks, at, 0, keepdims=False)]
    pallas_call x2, Pallas kernels: 118 us -> 104 us  [the longest x1 90.9 us: gather_all(): pl.pallas_call(functools.partial(gather_kernel, row_total, col_total, arr...]
    ppermute x15 -> x18, starting transfers between devices: 62.1 us -> 73.8 us  [reduce_steps(): lax.ppermute(sends[0], 'row', [(i, i + 1) for i in range(step + 1)])]
    ppermute x15 -> x18, waiting for transfers between devices: 66.7 us -> 57.1 us  [reduce_steps(): lax.ppermute(sends[0], 'row', [(i, i + 1) for i in range(step + 1)])]
  transfers between devices with their start and end apart: 69 -> 75, of which waited for: 31 -> 32; matrix products, arithmetic and copies ran while one was open for 23% -> 27% of each run, Pallas kernels for 30% -> 25%
where the time goes in v4:
time: 1210 us; the launch traced here: 1200 us
  Pallas kernels  394 us (33%)
  waiting for transfers between devices  243 us (20%)
  matrix products  194 us (16%)
  starting transfers between devices  149 us (12%)
  other arithmetic  124 us (10%)
  local copies, waits for them, and re-layouts  65.7 us (5%)
  between operations  26.1 us (2%)
    ppermute x15, waiting for transfers between devices, gather_steps(): lax.ppermute(ways[1], 'row', [(i, i - 1) for i in range(1, total - step +...  123 us
    dot_general x13, matrix products, dot_dims(): lax.dot_general(left_op, right_op, ((left_dims, right_dims), ((), ())), p...  110 us
    pallas_call x4, Pallas kernels, attend_back(): pl.pallas_call(functools.partial(attend_back_kernel, query_rows, tile), g...  105 us
    pallas_call x1, Pallas kernels, gather_all(): pl.pallas_call(functools.partial(gather_kernel, row_total, col_total, arr...  90.9 us
    pallas_call x1, Pallas kernels, reduce_all(): pl.pallas_call(functools.partial(reduce_kernel, row_total, col_total), in...  84.8 us
    dot_general x7, matrix products, dot_plain(): return jnp.dot(left_op, right_op, preferred_element_type=F32)  83.3 us
    ppermute x18, starting transfers between devices, reduce_steps(): lax.ppermute(sends[0], 'row', [(i, i + 1) for i in range(step + 1)])  73.8 us
    ppermute x18, waiting for transfers between devices, reduce_steps(): lax.ppermute(sends[0], 'row', [(i, i + 1) for i in range(step + 1)])  57.1 us
  transfers between devices with their start and end apart: 75, of which 32 were waited for; matrix products, arithmetic and copies ran while one was open for 27% of the time, Pallas kernels for 25%

profile of v4, /device:TPU:0, one launch (start us, length us, event | category | flops | bytes accessed | tf_op | source)
XLA Modules:
  0.0 1195.1 jit_solution(18255449583432260603)
XLA Ops:
  18.6 90.9 %gather_pack.1 = (bf16[4,8,80,1152]{3,2,1,0:T(8,128)(2,1)}, bf16[4,8,128,1280]{3,2,1,0:T(8,128)(2,1)}) custom-call(bf16[80,1152]{1,0:T(8,128)(2,1)} %pad.34.refs_0_, bf16[128,1280]{1,0:T(8,128)(2,1)} %pad_maximum_fusion.11.refs_1_), custom_call_target="tpu_custom_call" | custom-call | tf_op jit(solution)/shard_map/gather_pack/pallas_call | solution.py:539
  143.9 14.2 %collective-permute-done.2 = bf16[384,384]{0,1:T(8,128)(2,1)} collective-permute-done((bf16[384,384]{0,1:T(8,128)(2,1)S(1)}, bf16[384,384]{0,1:T(8,128)(2,1)}, u32[]{:S(2)}, u32[]{:S(2)}) %collective-permute-start.2) | collective-permute-done | bytes 294944 | tf_op jit(solution)/shard_map/ppermute | solution.py:802
  163.8 11.5 collective-permute-done.3
  203.0 11.0 attend.5
  214.0 11.0 attend.4
  235.6 10.9 attend.6
  251.0 10.9 attend.7
  270.8 19.3 %collective-permute-done.8 = bf16[192,2560]{1,0:T(8,128)(2,1)S(1)} collective-permute-done((bf16[192,2560]{1,0:T(8,128)(2,1)S(1)}, bf16[192,2560]{1,0:T(8,128)(2,1)S(1)}, u32[]{:S(2)}, u32[]{:S(2)}) %collective-permute-start.8) | collective-permute-done | bytes 983072 | tf_op jit(solution)/shard_map/ppermute | solution.py:801
  299.1 25.6 %collective-permute-done.11 = bf16[192,2560]{1,0:T(8,128)(2,1)} collective-permute-done((bf16[192,2560]{1,0:T(8,128)(2,1)S(1)}, bf16[192,2560]{1,0:T(8,128)(2,1)}, u32[]{:S(2)}, u32[]{:S(2)}) %collective-permute-start.11) | collective-permute-done | bytes 983072 | tf_op jit(solution)/shard_map/ppermute | solution.py:802
  339.5 13.7 %collective-permute-done.13 = bf16[192,2560]{1,0:T(8,128)(2,1)} collective-permute-done((bf16[192,2560]{1,0:T(8,128)(2,1)}, bf16[192,2560]{1,0:T(8,128)(2,1)}, u32[]{:S(2)}, u32[]{:S(2)}) %collective-permute-start.13) | collective-permute-done | bytes 983072 | tf_op jit(solution)/shard_map/ppermute | solution.py:802
  358.5 11.6 convolution_convert_fusion.3
  382.0 10.6 collective-permute-done.15
  420.4 10.8 convolution_convert_fusion.2
  442.1 14.2 %fusion.21 = (bf16[768,1600]{1,0:T(8,128)(2,1)S(1)}, bf16[768,1600]{1,0:T(8,128)(2,1)}) fusion(bf16[768,1600]{1,0:T(8,128)(2,1)S(1)} %convolution_convert_fusion.2, bf16[2560,1600]{1,0:T(8,128)(2,1)} %all-gather.9.cloned.1.call-done, bf16[192,2560]{1,0:T(8,128)(2,1)S(1)} %add.400, bf16[192,2560]{1,0:T(8,128)(2,1)S(1)} %copy-done.39, ...), kind=kOutput, calls=%fused_computation.35 | convolution fusion | flops 6317015040 | bytes 19496960 | tf_op jit(solution)/shard_map/dot_general | solution.py:30
  457.4 12.6 %collective-permute-start.22 = (bf16[192,2560]{1,0:T(8,128)(2,1)S(1)}, bf16[192,2560]{1,0:T(8,128)(2,1)S(1)}, u32[]{:S(2)}, u32[]{:S(2)}) collective-permute-start(bf16[192,2560]{1,0:T(8,128)(2,1)S(1)} %get-tuple-element.326), channel_id=1, source_target_pairs={{0,8},{8,16},{16,24},{1,9},{9,17},{17,25},{2,10},{10,18},{18,26},{... | collective-permute-start | bytes 2949128 | tf_op jit(solution)/shard_map/ppermute | solution.py:821
  506.5 14.9 %collective-permute-done.24 = bf16[192,2560]{1,0:T(8,128)(2,1)S(1)} collective-permute-done((bf16[192,2560]{1,0:T(8,128)(2,1)S(1)}, bf16[192,2560]{1,0:T(8,128)(2,1)S(1)}, u32[]{:S(2)}, u32[]{:S(2)}) %collective-permute-start.24) | collective-permute-done | bytes 983072 | tf_op jit(solution)/shard_map/ppermute | solution.py:801
  524.0 14.9 %collective-permute-done.28 = bf16[192,2560]{1,0:T(8,128)(2,1)S(1)} collective-permute-done((bf16[192,2560]{1,0:T(8,128)(2,1)S(1)}, bf16[192,2560]{1,0:T(8,128)(2,1)S(1)}, u32[]{:S(2)}, u32[]{:S(2)}) %collective-permute-start.28) | collective-permute-done | bytes 983072 | tf_op jit(solution)/shard_map/ppermute | solution.py:821
  576.1 14.8 %fusion.16 = (bf16[768,1600]{1,0:T(8,128)(2,1)S(1)}, bf16[768,1600]{1,0:T(8,128)(2,1)S(1)}) fusion(bf16[768,1600]{1,0:T(8,128)(2,1)} %copy-done.91, bf16[768,1600]{1,0:T(8,128)(2,1)} %get-tuple-element.370, bf16[2560,1600]{1,0:T(8,128)(2,1)} %all-gather.11.cloned.1.call-done, bf16[192,2560]{1,0:T(8,128)(2,1)} %add.418, bf16[192,2560]{1,0:T(8,128)(2,1)S(1)} %add.417, ...), kind=kOutput, calls=%fused_computation.30 | convolution fusion | flops 6325616640 | bytes 21954560 | tf_op jit(solution)/shard_map/dot_general | solution.py:30
  605.0 11.7 fusion.104
  683.8 18.9 %down_wg.1 = bf16[2560,1600]{1,0:T(8,128)(2,1)} custom-call(bf16[768,2560]{1,0:T(8,128)(2,1)} %pad_maximum_fusion.2.refs_0_, bf16[768,2560]{1,0:T(8,128)(2,1)} %pad_maximum_fusion.3.refs_1_, bf16[768,1600]{1,0:T(8,128)(2,1)S(1)} %copy-done.20, bf16[768,1600]{1,0:T(8,128)(2,1)S(1)} %get-tuple-element.170.refs_3_), custom_call_target="tpu_custom_call" | custom-call | flops 12582912000 | bytes 16056320 | tf_op jit(solution)/shard_map/down_wg/pallas_call | solution.py:340
  712.6 16.5 %fusion.26 = (bf16[768,1600]{1,0:T(8,128)(2,1)S(1)}, bf16[768,1600]{1,0:T(8,128)(2,1)S(1)}) fusion(bf16[768,1600]{1,0:T(8,128)(2,1)} %copy-done.92, bf16[768,1600]{1,0:T(8,128)(2,1)} %get-tuple-element.372, bf16[2560,1600]{1,0:T(8,128)(2,1)} %all-gather.11.cloned.1.call-done, bf16[192,2560]{1,0:T(8,128)(2,1)S(1)} %copy-done.54, ...), kind=kOutput, calls=%fused_computation.40 | convolution fusion | flops 6325616640 | bytes 21954560 | tf_op jit(solution)/shard_map/dot_general | solution.py:30
  730.5 11.7 fusion.105
  743.6 12.1 %add_convert_fusion = bf16[768,2560]{1,0:T(8,128)(2,1)S(1)} fusion(f32[768,2560]{1,0:T(8,128)} %fusion.105, bf16[768,1600]{1,0:T(8,128)(2,1)S(1)} %get-tuple-element.202.refs_3_, bf16[2560,1600]{1,0:T(8,128)(2,1)} %all-gather.7.cloned.1.call-done), kind=kOutput, calls=%fused_computation.12 | convolution fusion | flops 6295388160 | bytes 22446080 | tf_op jit(solution)/shard_map/dot_general | solution.py:34
  766.1 18.8 %gate_wg.1 = bf16[2560,1600]{1,0:T(8,128)(2,1)} custom-call(bf16[768,2560]{1,0:T(8,128)(2,1)} %pad_maximum_fusion.refs_0_, bf16[768,2560]{1,0:T(8,128)(2,1)} %pad_maximum_fusion.1.refs_1_, bf16[768,1600]{1,0:T(8,128)(2,1)S(1)} %copy-done.16, bf16[768,1600]{1,0:T(8,128)(2,1)S(1)} %get-tuple-element.202.refs_3_), custom_call_target="tpu_custom_call" | custom-call | flops 12582912000 | bytes 16056320 | tf_op jit(solution)/shard_map/gate_wg/pallas_call | solution.py:340
  793.0 18.6 %up_wg.1 = bf16[2560,1600]{1,0:T(8,128)(2,1)} custom-call(bf16[768,2560]{1,0:T(8,128)(2,1)} %pad_maximum_fusion.refs_0_, bf16[768,2560]{1,0:T(8,128)(2,1)} %pad_maximum_fusion.1.refs_1_, bf16[768,1600]{1,0:T(8,128)(2,1)S(1)} %get-tuple-element.190.refs_2_, bf16[768,1600]{1,0:T(8,128)(2,1)S(1)} %copy-done.18), custom_call_target="tpu_custom_call" | custom-call | flops 12582912000 | bytes 16056320 | tf_op jit(solution)/shard_map/up_wg/pallas_call | solution.py:340
  840.1 13.0 %out_wg.1 = bf16[2560,2560]{1,0:T(8,128)(2,1)} custom-call(bf16[384,2560]{1,0:T(8,128)(2,1)} %get-tuple-element.288.tokens_ref, bf16[2560,384]{1,0:T(8,128)(2,1)} %pad_maximum_fusion.6.mixed_ref), custom_call_target="tpu_custom_call" | custom-call | flops 5033164800 | bytes 13107200 | tf_op jit(solution)/shard_map/out_wg/pallas_call | solution.py:370
  853.2 11.7 fusion.59
  870.7 26.7 %attend_back.4 = (bf16[8,4,128,1280]{3,2,1,0:T(8,128)(2,1)}, f32[768,384]{1,0:T(8,128)S(1)}, f32[1024,384]{1,0:T(8,128)}) custom-call(bf16[4,8,128,1280]{3,2,1,0:T(8,128)(2,1)} %get-tuple-element.130.weights_ref, bf16[768,384]{1,0:T(8,128)(2,1)S(1)} %fusion.76.query_t_ref, bf16[1024,256]{1,0:T(8,128)(2,1)S(1)} %copy-done.11, ...), custom_call_target="tpu_custom_call" | custom-call | flops 24999999488 | bytes 5242880 | tf_op jit(solution)/shard_map/attend_back/pallas_call | solution.py:276
  897.4 26.1 %attend_back.5 = (bf16[8,4,128,1280]{3,2,1,0:T(8,128)(2,1)}, f32[768,384]{1,0:T(8,128)S(1)}, f32[1024,384]{1,0:T(8,128)}) custom-call(bf16[4,8,128,1280]{3,2,1,0:T(8,128)(2,1)} %get-tuple-element.130.weights_ref, bf16[768,384]{1,0:T(8,128)(2,1)S(1)} %fusion.76.query_t_ref, bf16[1024,256]{1,0:T(8,128)(2,1)S(1)} %copy-done.11, ...), custom_call_target="tpu_custom_call", output_to_operand_aliasing={{0}: (13, {})} | custom-call | flops 24999999488 | bytes 5242880 | tf_op jit(solution)/shard_map/attend_back/pallas_call | solution.py:276
  936.3 26.2 %attend_back.6 = (bf16[8,4,128,1280]{3,2,1,0:T(8,128)(2,1)}, f32[768,384]{1,0:T(8,128)S(1)}, f32[1024,384]{1,0:T(8,128)}) custom-call(bf16[4,8,128,1280]{3,2,1,0:T(8,128)(2,1)} %get-tuple-element.130.weights_ref, bf16[768,384]{1,0:T(8,128)(2,1)S(1)} %fusion.76.query_t_ref, bf16[1024,256]{1,0:T(8,128)(2,1)S(1)} %copy-done.12, ...), custom_call_target="tpu_custom_call", output_to_operand_aliasing={{0}: (13, {})} | custom-call | flops 24999999488 | bytes 5242880 | tf_op jit(solution)/shard_map/attend_back/pallas_call | solution.py:276
  962.5 26.0 %attend_back.7 = (bf16[8,4,128,1280]{3,2,1,0:T(8,128)(2,1)}, f32[768,384]{1,0:T(8,128)S(1)}, f32[1024,384]{1,0:T(8,128)}) custom-call(bf16[4,8,128,1280]{3,2,1,0:T(8,128)(2,1)} %get-tuple-element.130.weights_ref, bf16[768,384]{1,0:T(8,128)(2,1)S(1)} %fusion.76.query_t_ref, bf16[1024,256]{1,0:T(8,128)(2,1)S(1)} %copy-done.12, ...), custom_call_target="tpu_custom_call", output_to_operand_aliasing={{0}: (13, {})} | custom-call | flops 24999999488 | bytes 5242880 | tf_op jit(solution)/shard_map/attend_back/pallas_call | solution.py:276
  1060.6 84.8 %reduce_down.1 = (f32[80,1152]{1,0:T(8,128)S(1)}, f32[320,640]{1,0:T(8,128)S(1)}) custom-call(bf16[4,4,2,80,1152]{4,3,2,1,0:T(8,128)(2,1)} %bitcast.143, bf16[4,320,640]{2,1,0:T(8,128)(2,1)S(1)} %pad_maximum_fusion.7.side_ref), custom_call_target="tpu_custom_call" | custom-call | tf_op jit(solution)/shard_map/reduce_down/pallas_call | solution.py:728
  (519 shorter events, 522.5 us)
Async XLA Ops:
  7.2 217.8 %all-gather.5.cloned.1.call-start = ((), (), s32[]{:S(2)}) async-start(), calls=%async_computation.5 | async-start | bytes 13516800 | tf_op jit(solution)/shard_map/all_gather | solution.py:899
  113.1 245.3 %all-gather.7.cloned.1.call-start = ((), (), s32[]{:S(2)}) async-start(), calls=%async_computation.6 | async-start | bytes 9584640 | tf_op jit(solution)/shard_map/all_gather | solution.py:982
  225.0 133.4 %all-gather.9.cloned.1.call-start = ((), (), s32[]{:S(2)}) async-start(), calls=%async_computation.7 | async-start | bytes 9584640 | tf_op jit(solution)/shard_map/all_gather | solution.py:983
  225.8 172.5 %all-gather.11.cloned.1.call-start = ((), (), s32[]{:S(2)}) async-start(), calls=%async_computation.8 | async-start | bytes 9584640 | tf_op jit(solution)/shard_map/all_gather | solution.py:984
  226.3 698.2 %reduce-scatter.10.cloned.1.call-start = ((), (), s32[]{:S(2)}) async-start(), calls=%async_computation.11 | async-start | bytes 9584640 | tf_op jit(solution)/shard_map/reduce_scatter | solution.py:1093
  268.1 21.9 %collective-permute-start.8 = (bf16[192,2560]{1,0:T(8,128)(2,1)S(1)}, bf16[192,2560]{1,0:T(8,128)(2,1)S(1)}, u32[]{:S(2)}, u32[]{:S(2)}) collective-permute-start(bf16[192,2560]{1,0:T(8,128)(2,1)S(1)} %get-tuple-element.332), channel_id=1, source_target_pairs={{0,8},{8,16},{16,24},{1,9},{9,17},{17,25},{2,10},{10,18},{18,26},{... | collective-permute-start | bytes 2949128 | tf_op jit(solution)/shard_map/ppermute | solution.py:801
  269.5 26.7 %collective-permute-start.9 = (bf16[192,2560]{1,0:T(8,128)(2,1)S(1)}, bf16[192,2560]{1,0:T(8,128)(2,1)S(1)}, u32[]{:S(2)}, u32[]{:S(2)}) collective-permute-start(bf16[192,2560]{1,0:T(8,128)(2,1)S(1)} %get-tuple-element.332), channel_id=1, source_target_pairs={{8,0},{16,8},{24,16},{9,1},{17,9},{25,17},{10,2},{18,10},{26,18},{... | collective-permute-start | bytes 2949128 | tf_op jit(solution)/shard_map/ppermute | solution.py:802
  297.8 26.9 %collective-permute-start.11 = (bf16[192,2560]{1,0:T(8,128)(2,1)S(1)}, bf16[192,2560]{1,0:T(8,128)(2,1)}, u32[]{:S(2)}, u32[]{:S(2)}) collective-permute-start(bf16[192,2560]{1,0:T(8,128)(2,1)S(1)} %collective-permute-done.9), channel_id=1, source_target_pairs={{8,0},{16,8},{9,1},{17,9},{10,2},{18,10},{11,3},{19,11},{12,4},{20... | collective-permute-start | bytes 2949128 | tf_op jit(solution)/shard_map/ppermute | solution.py:802
  326.3 26.9 %collective-permute-start.13 = (bf16[192,2560]{1,0:T(8,128)(2,1)}, bf16[192,2560]{1,0:T(8,128)(2,1)}, u32[]{:S(2)}, u32[]{:S(2)}) collective-permute-start(bf16[192,2560]{1,0:T(8,128)(2,1)} %collective-permute-done.11), channel_id=1, source_target_pairs={{8,0},{9,1},{10,2},{11,3},{12,4},{13,5},{14,6},{15,7}} | collective-permute-start | bytes 2949128 | tf_op jit(solution)/shard_map/ppermute | solution.py:802
  329.7 40.4 %collective-permute-start.6 = (bf16[192,2560]{1,0:T(8,128)(2,1)S(1)}, bf16[192,2560]{1,0:T(8,128)(2,1)}, u32[]{:S(2)}, u32[]{:S(2)}) collective-permute-start(bf16[192,2560]{1,0:T(8,128)(2,1)S(1)} %get-tuple-element.333), channel_id=1, source_target_pairs={{0,8},{8,16},{16,24},{1,9},{9,17},{17,25},{2,10},{10,18},{18,26},{... | collective-permute-start | bytes 2949128 | tf_op jit(solution)/shard_map/ppermute | solution.py:801
  336.3 33.8 %collective-permute-start.7 = (bf16[192,2560]{1,0:T(8,128)(2,1)S(1)}, bf16[192,2560]{1,0:T(8,128)(2,1)}, u32[]{:S(2)}, u32[]{:S(2)}) collective-permute-start(bf16[192,2560]{1,0:T(8,128)(2,1)S(1)} %get-tuple-element.333), channel_id=1, source_target_pairs={{8,0},{16,8},{24,16},{9,1},{17,9},{25,17},{10,2},{18,10},{26,18},{... | collective-permute-start | bytes 2949128 | tf_op jit(solution)/shard_map/ppermute | solution.py:802
  372.0 20.6 %collective-permute-start.15 = (bf16[192,2560]{1,0:T(8,128)(2,1)}, bf16[192,2560]{1,0:T(8,128)(2,1)}, u32[]{:S(2)}, u32[]{:S(2)}) collective-permute-start(bf16[192,2560]{1,0:T(8,128)(2,1)} %collective-permute-done.7), channel_id=1, source_target_pairs={{8,0},{16,8},{9,1},{17,9},{10,2},{18,10},{11,3},{19,11},{12,4},{20... | collective-permute-start | bytes 2949128 | tf_op jit(solution)/shard_map/ppermute | solution.py:802
  457.4 32.0 %collective-permute-start.22 = (bf16[192,2560]{1,0:T(8,128)(2,1)S(1)}, bf16[192,2560]{1,0:T(8,128)(2,1)S(1)}, u32[]{:S(2)}, u32[]{:S(2)}) collective-permute-start(bf16[192,2560]{1,0:T(8,128)(2,1)S(1)} %get-tuple-element.326), channel_id=1, source_target_pairs={{0,8},{8,16},{16,24},{1,9},{9,17},{17,25},{2,10},{10,18},{18,26},{... | collective-permute-start | bytes 2949128 | tf_op jit(solution)/shard_map/ppermute | solution.py:821
  470.0 23.8 %collective-permute-start.23 = (bf16[192,2560]{1,0:T(8,128)(2,1)S(1)}, bf16[192,2560]{1,0:T(8,128)(2,1)S(1)}, u32[]{:S(2)}, u32[]{:S(2)}) collective-permute-start(bf16[192,2560]{1,0:T(8,128)(2,1)S(1)} %get-tuple-element.325), channel_id=1, source_target_pairs={{8,0},{16,8},{24,16},{9,1},{17,9},{25,17},{10,2},{18,10},{26,18},{... | collective-permute-start | bytes 2949128 | tf_op jit(solution)/shard_map/ppermute | solution.py:822
  497.1 24.3 %collective-permute-start.24 = (bf16[192,2560]{1,0:T(8,128)(2,1)S(1)}, bf16[192,2560]{1,0:T(8,128)(2,1)S(1)}, u32[]{:S(2)}, u32[]{:S(2)}) collective-permute-start(bf16[192,2560]{1,0:T(8,128)(2,1)S(1)} %get-tuple-element.294), channel_id=1, source_target_pairs={{0,8},{8,16},{16,24},{1,9},{9,17},{17,25},{2,10},{10,18},{18,26},{... | collective-permute-start | bytes 2949128 | tf_op jit(solution)/shard_map/ppermute | solution.py:801
  499.3 22.6 %collective-permute-start.25 = (bf16[192,2560]{1,0:T(8,128)(2,1)S(1)}, bf16[192,2560]{1,0:T(8,128)(2,1)S(1)}, u32[]{:S(2)}, u32[]{:S(2)}) collective-permute-start(bf16[192,2560]{1,0:T(8,128)(2,1)S(1)} %get-tuple-element.294), channel_id=1, source_target_pairs={{8,0},{16,8},{24,16},{9,1},{17,9},{25,17},{10,2},{18,10},{26,18},{... | collective-permute-start | bytes 2949128 | tf_op jit(solution)/shard_map/ppermute | solution.py:802
  501.2 37.6 %collective-permute-start.28 = (bf16[192,2560]{1,0:T(8,128)(2,1)S(1)}, bf16[192,2560]{1,0:T(8,128)(2,1)S(1)}, u32[]{:S(2)}, u32[]{:S(2)}) collective-permute-start(bf16[192,2560]{1,0:T(8,128)(2,1)S(1)} %get-tuple-element.324), channel_id=1, source_target_pairs={{0,8},{1,9},{2,10},{3,11},{4,12},{5,13},{6,14},{7,15}} | collective-permute-start | bytes 2949128 | tf_op jit(solution)/shard_map/ppermute | solution.py:821
  505.8 33.0 %collective-permute-start.29 = (bf16[192,2560]{1,0:T(8,128)(2,1)S(1)}, bf16[192,2560]{1,0:T(8,128)(2,1)S(1)}, u32[]{:S(2)}, u32[]{:S(2)}) collective-permute-start(bf16[192,2560]{1,0:T(8,128)(2,1)S(1)} %get-tuple-element.323), channel_id=1, source_target_pairs={{24,16},{25,17},{26,18},{27,19},{28,20},{29,21},{30,22},{31,23}} | collective-permute-start | bytes 2949128 | tf_op jit(solution)/shard_map/ppermute | solution.py:822
  522.7 21.9 %collective-permute-start.27 = (bf16[192,2560]{1,0:T(8,128)(2,1)S(1)}, bf16[192,2560]{1,0:T(8,128)(2,1)S(1)}, u32[]{:S(2)}, u32[]{:S(2)}) collective-permute-start(bf16[192,2560]{1,0:T(8,128)(2,1)S(1)} %collective-permute-done.25), channel_id=1, source_target_pairs={{8,0},{16,8},{9,1},{17,9},{10,2},{18,10},{11,3},{19,11},{12,4},{20... | collective-permute-start | bytes 2949128 | tf_op jit(solution)/shard_map/ppermute | solution.py:802
  599.0 27.3 %collective-permute-start.36 = (bf16[192,2560]{1,0:T(8,128)(2,1)S(1)}, bf16[192,2560]{1,0:T(8,128)(2,1)}, u32[]{:S(2)}, u32[]{:S(2)}) collective-permute-start(bf16[192,2560]{1,0:T(8,128)(2,1)S(1)} %get-tuple-element.290), channel_id=1, source_target_pairs={{0,8},{8,16},{16,24},{1,9},{9,17},{17,25},{2,10},{10,18},{18,26},{... | collective-permute-start | bytes 2949128 | tf_op jit(solution)/shard_map/ppermute | solution.py:801
  603.5 22.8 %collective-permute-start.37 = (bf16[192,2560]{1,0:T(8,128)(2,1)S(1)}, bf16[192,2560]{1,0:T(8,128)(2,1)}, u32[]{:S(2)}, u32[]{:S(2)}) collective-permute-start(bf16[192,2560]{1,0:T(8,128)(2,1)S(1)} %get-tuple-element.290), channel_id=1, source_target_pairs={{8,0},{16,8},{24,16},{9,1},{17,9},{25,17},{10,2},{18,10},{26,18},{... | collective-permute-start | bytes 2949128 | tf_op jit(solution)/shard_map/ppermute | solution.py:802
  627.9 20.0 %collective-permute-start.39 = (bf16[192,2560]{1,0:T(8,128)(2,1)}, bf16[192,2560]{1,0:T(8,128)(2,1)}, u32[]{:S(2)}, u32[]{:S(2)}) collective-permute-start(bf16[192,2560]{1,0:T(8,128)(2,1)} %collective-permute-done.37), channel_id=1, source_target_pairs={{8,0},{16,8},{9,1},{17,9},{10,2},{18,10},{11,3},{19,11},{12,4},{20... | collective-permute-start | bytes 2949128 | tf_op jit(solution)/shard_map/ppermute | solution.py:802
  677.4 25.2 %collective-permute-start.44 = (bf16[192,2560]{1,0:T(8,128)(2,1)}, bf16[192,2560]{1,0:T(8,128)(2,1)}, u32[]{:S(2)}, u32[]{:S(2)}) collective-permute-start(bf16[192,2560]{1,0:T(8,128)(2,1)} %get-tuple-element.316), channel_id=1, source_target_pairs={{0,8},{8,16},{1,9},{9,17},{2,10},{10,18},{3,11},{11,19},{4,12},{12... | collective-permute-start | bytes 2949128 | tf_op jit(solution)/shard_map/ppermute | solution.py:821
  679.9 22.7 %collective-permute-start.45 = (bf16[192,2560]{1,0:T(8,128)(2,1)}, bf16[192,2560]{1,0:T(8,128)(2,1)}, u32[]{:S(2)}, u32[]{:S(2)}) collective-permute-start(bf16[192,2560]{1,0:T(8,128)(2,1)} %get-tuple-element.315), channel_id=1, source_target_pairs={{16,8},{24,16},{17,9},{25,17},{18,10},{26,18},{19,11},{27,19},{20,... | collective-permute-start | bytes 2949128 | tf_op jit(solution)/shard_map/ppermute | solution.py:822
  702.7 221.9 %reduce-scatter.6.cloned.1.call-start = ((), (), s32[]{:S(2)}) async-start(), calls=%async_computation.9 | async-start | bytes 9584640 | tf_op jit(solution)/shard_map/reduce_scatter | solution.py:1091
  759.0 25.9 %collective-permute-start.48 = (bf16[192,2560]{1,0:T(8,128)(2,1)}, bf16[192,2560]{1,0:T(8,128)(2,1)}, u32[]{:S(2)}, u32[]{:S(2)}) collective-permute-start(bf16[192,2560]{1,0:T(8,128)(2,1)} %get-tuple-element.312), channel_id=1, source_target_pairs={{0,8},{1,9},{2,10},{3,11},{4,12},{5,13},{6,14},{7,15}} | collective-permute-start | bytes 2949128 | tf_op jit(solution)/shard_map/ppermute | solution.py:821
  764.5 20.5 %collective-permute-start.49 = (bf16[192,2560]{1,0:T(8,128)(2,1)}, bf16[192,2560]{1,0:T(8,128)(2,1)}, u32[]{:S(2)}, u32[]{:S(2)}) collective-permute-start(bf16[192,2560]{1,0:T(8,128)(2,1)} %get-tuple-element.311), channel_id=1, source_target_pairs={{24,16},{25,17},{26,18},{27,19},{28,20},{29,21},{30,22},{31,23}} | collective-permute-start | bytes 2949128 | tf_op jit(solution)/shard_map/ppermute | solution.py:822
  785.0 149.0 %reduce-scatter.8.cloned.1.call-start = ((), (), s32[]{:S(2)}) async-start(), calls=%async_computation.10 | async-start | bytes 9584640 | tf_op jit(solution)/shard_map/reduce_scatter | solution.py:1092
  788.7 22.8 %collective-permute-start.50 = (bf16[192,2560]{1,0:T(8,128)(2,1)}, bf16[192,2560]{1,0:T(8,128)(2,1)}, u32[]{:S(2)}, u32[]{:S(2)}) collective-permute-start(bf16[192,2560]{1,0:T(8,128)(2,1)} %get-tuple-element.310), channel_id=1, source_target_pairs={{0,8},{8,16},{1,9},{9,17},{2,10},{10,18},{3,11},{11,19},{4,12},{12... | collective-permute-start | bytes 2949128 | tf_op jit(solution)/shard_map/ppermute | solution.py:821
  791.4 20.2 %collective-permute-start.51 = (bf16[192,2560]{1,0:T(8,128)(2,1)}, bf16[192,2560]{1,0:T(8,128)(2,1)}, u32[]{:S(2)}, u32[]{:S(2)}) collective-permute-start(bf16[192,2560]{1,0:T(8,128)(2,1)} %get-tuple-element.309), channel_id=1, source_target_pairs={{16,8},{24,16},{17,9},{25,17},{18,10},{26,18},{19,11},{27,19},{20,... | collective-permute-start | bytes 2949128 | tf_op jit(solution)/shard_map/ppermute | solution.py:822
  811.6 247.2 %reduce-scatter.12.cloned.1.call-start = ((), (), s32[]{:S(2)}) async-start(), calls=%async_computation.12 | async-start | bytes 14745600 | tf_op jit(solution)/shard_map/reduce_scatter | solution.py:1103
  864.9 280.5 %reduce-scatter.14.cloned.1.call-start = ((), (), s32[]{:S(2)}) async-start(), calls=%async_computation.13 | async-start | bytes 11796480 | tf_op jit(solution)/shard_map/reduce_scatter | solution.py:1114
  (139 other events, 2286.8 us)
Sparse Core Ops, SparseCore 0:
  113.2 107.8 all-gather.4
  225.2 58.4 all-gather.6
  285.5 54.9 all-gather.8
  342.2 54.9 all-gather.10
  702.8 71.0 reduce-scatter.9
  785.1 73.2 reduce-scatter.5
  861.9 72.0 reduce-scatter.7
  937.5 95.1 reduce-scatter.11
  1036.2 104.9 reduce-scatter.13

commit v5 on v4

--- a/solution.py
+++ b/solution.py
@@ -436,8 +436,6 @@
     for own in owns:
         own.start()
     greet(row_total, row_rank, col_rank, bits)
-    for own in owns:
-        own.wait()
 
     def block_col(row, mask):
         index = col_rank
@@ -446,28 +444,28 @@
                 index = flip(index, turn_bit(bits, row, step, row_total))
         return index
 
-    def line_copy(at, way, row):
+    def line_copy(at, way, row, own=False):
         ref = out_refs[at].at[row, col_rank]
         return pltpu.make_async_remote_copy(
-            src_ref=ref, dst_ref=ref, send_sem=line_send.at[at, way, row],
+            src_ref=own_refs[at] if own else ref, dst_ref=ref, send_sem=line_send.at[at, way, row],
             recv_sem=line_recv.at[at, row],
             device_id=(row_rank + 1 - 2 * way, col_rank), device_id_type=MESH,
         )
 
-    def chip_copy(at, row, mask, step):
+    def chip_copy(at, row, mask, step, own=False):
         ref = out_refs[at].at[row, block_col(row, mask)]
         to = mask + 2**step
         return pltpu.make_async_remote_copy(
-            src_ref=ref, dst_ref=ref, send_sem=chip_send.at[at, row, to],
+            src_ref=own_refs[at] if own else ref, dst_ref=ref, send_sem=chip_send.at[at, row, to],
             recv_sem=chip_recv.at[at, row, to],
             device_id=(row_rank, flip(col_rank, turn_bit(bits, row, step, row_total))),
             device_id_type=MESH,
         )
 
-    def core_copy(at, row, mask):
+    def core_copy(at, row, mask, own=False):
         ref = out_refs[at].at[row, block_col(row, mask)]
         return pltpu.make_async_remote_copy(
-            src_ref=ref, dst_ref=ref, send_sem=core_send.at[at, row, mask],
+            src_ref=own_refs[at] if own else ref, dst_ref=ref, send_sem=core_send.at[at, row, mask],
             recv_sem=core_recv.at[at, row, mask], device_id=(row_rank, flip(col_rank, 1)),
             device_id_type=MESH,
         )
@@ -489,17 +487,17 @@
 
                 @pl.when(row_rank < row_total - 1)
                 def _():
-                    line_copy(at, 0, row).start()
+                    line_copy(at, 0, row, away == 0).start()
 
             if side >= 0:
 
                 @pl.when(row_rank > 0)
                 def _():
-                    line_copy(at, 1, row).start()
+                    line_copy(at, 1, row, away == 0).start()
 
             for step in range(len(bits)):
-                chip_copy(at, row, 0, step).start()
-            core_copy(at, row, 0).start()
+                chip_copy(at, row, 0, step, away == 0).start()
+            core_copy(at, row, 0, away == 0).start()
 
     by_distance(arrive)
     for mask in range(1, masks):
@@ -513,6 +511,8 @@
                 core_copy(at, row, mask).start()
 
         by_distance(forward)
+    for own in owns:
+        own.wait()
     for at in range(arrays):
         for row in range(row_total):
             for mask in range(masks):
@@ -926,12 +926,15 @@
     latent_give = Task(gather_steps(latent_pack))
     while latent_give.advance_into():
         pass
-    latent_all = together(latent_give.value)
-    blocks = latent_all.reshape(row_total, local_rows, -1)
+    latent_blocks, gate_here, up_here, down_here = together(
+        (latent_give.value, gate_weight, up_weight, down_weight.T)
+    )
+    gate_full, up_full, down_t = (
+        lax.all_gather(gate_here, "col", axis=0, tiled=True),
+        lax.all_gather(up_here, "col", axis=0, tiled=True),
+        lax.all_gather(down_here, "col", axis=0, tiled=True),
+    )
     froms = [lax.rem(row_rank + row_total - step, row_total) for step in range(row_total)]
-    latent_all = jnp.concatenate(
-        [lax.dynamic_index_in_dim(blocks, at, 0, keepdims=False) for at in froms]
-    )
 
     kept = 0
     for block in range(row_total):
@@ -946,8 +949,7 @@
     shift = jnp.maximum(jnp.sum((segments < query_seg[0]).astype(jnp.int32)) - prompt, 0)
 
     def keep(values):
-        far = jnp.pad(values, ((0, kept),) + ((0, 0),) * (values.ndim - 1))
-        far = lax.dynamic_slice_in_dim(far, shift, kept, 0)
+        far = lax.dynamic_slice_in_dim(values, shift, kept, 0)
         near = jnp.arange(kept, dtype=jnp.int32) < prompt
         return jnp.where(near.reshape((kept,) + (1,) * (values.ndim - 1)), values[:kept], far)
 
@@ -958,12 +960,18 @@
         far = lax.dynamic_slice_in_dim(far, length - shift, length, 0)
         return jnp.where(places < prompt, near, jnp.where(places < prompt + shift, 0.0, far))
 
+    latent_all = jnp.zeros((length + kept, latent_pack.shape[1]), BF)
+    for step, at in enumerate(froms):
+        latent_all = lax.dynamic_update_slice_in_dim(
+            latent_all, latent_blocks[step * local_rows : (step + 1) * local_rows],
+            at * local_rows, 0,
+        )
     kept_all = keep(latent_all)
     kv_all = kept_all[:, :KV_RANK]
     rope_all = kept_all[:, KV_RANK:]
     key_at = jnp.arange(kept, dtype=jnp.int32)
     key_at = jnp.where(key_at < prompt, key_at, key_at + shift)
-    key_seg = keep(segments)
+    key_seg = keep(jnp.pad(segments, (0, kept)))
     allowed_t = (key_at[:, None] <= query_at[None, :]) & (
         (key_seg[:, None] == 0) | (key_seg[:, None] == query_seg[None, :])
     )
@@ -975,14 +983,7 @@
         attend(head_w, query_t, kv_all, rope_all, cos_t, sin_t, bias_t, query_rows, block)
         for block in range(cut)
     ]
-    mixed, out_all, query_t, gate_here, up_here, down_here = together(
-        (mixed, out_all, query_t, gate_weight, up_weight, down_weight.T)
-    )
-    gate_full, up_full, down_t = (
-        lax.all_gather(gate_here, "col", axis=0, tiled=True),
-        lax.all_gather(up_here, "col", axis=0, tiled=True),
-        lax.all_gather(down_here, "col", axis=0, tiled=True),
-    )
+    mixed, out_all, query_t = together((mixed, out_all, query_t))
     mixed += [
         attend(head_w, query_t, kv_all, rope_all, cos_t, sin_t, bias_t, query_rows, block)
         for block in range(cut, row_total)
@@ -1115,7 +1116,7 @@
         head_wg.reshape(devices * pack_rows, heads_here * HEAD), "col",
         scatter_dimension=0, tiled=True,
     ).reshape(row_total, pack_rows, heads_here * HEAD)
-    latent_rows = spread(latent_back).astype(BF).reshape(blocks.shape)
+    latent_rows = spread(latent_back).astype(BF).reshape(row_total, local_rows, -1)
     latent_reduce = Task(
         reduce_steps(
             [lax.dynamic_index_in_dim(latent_rows, at, 0, keepdims=False) for at in froms]

time: 1210 us -> 1210 us (level)
  waiting for transfers between devices: 243 us -> 275 us
  Pallas kernels: 394 us -> 377 us
  local copies, waits for them, and re-layouts: 65.7 us -> 51.4 us
    pallas_call x1, Pallas kernels: 90.9 us -> 75.6 us  [gather_all(): pl.pallas_call(functools.partial(gather_kernel, row_total, col_total, arr...]
    dynamic_slice x5 -> x0, local copies, waits for them, and re-layouts: 15.3 us -> none  [body(): lax.dynamic_index_in_dim(blocks, at, 0, keepdims=False)]
    ppermute x15, waiting for transfers between devices: 123 us -> 138 us  [gather_steps(): lax.ppermute(ways[1], 'row', [(i, i - 1) for i in range(1, total - step +...]
  transfers between devices with their start and end apart: 75 -> 75, of which waited for: 32 -> 33; matrix products, arithmetic and copies ran while one was open for 27% -> 25% of each run, Pallas kernels for 25% -> 25%
where the time goes in v5:
time: 1210 us; the launch traced here: 1200 us
  Pallas kernels  377 us (31%)
  waiting for transfers between devices  275 us (23%)
  matrix products  194 us (16%)
  starting transfers between devices  156 us (13%)
  other arithmetic  116 us (10%)
  local copies, waits for them, and re-layouts  51.4 us (4%)
  between operations  26.3 us (2%)
    ppermute x15, waiting for transfers between devices, gather_steps(): lax.ppermute(ways[1], 'row', [(i, i - 1) for i in range(1, total - step +...  138 us
    dot_general x13, matrix products, dot_dims(): lax.dot_general(left_op, right_op, ((left_dims, right_dims), ((), ())), p...  111 us
    pallas_call x4, Pallas kernels, attend_back(): pl.pallas_call(functools.partial(attend_back_kernel, query_rows, tile), g...  105 us
    pallas_call x1, Pallas kernels, reduce_all(): pl.pallas_call(functools.partial(reduce_kernel, row_total, col_total), in...  82.9 us
    dot_general x7, matrix products, dot_plain(): return jnp.dot(left_op, right_op, preferred_element_type=F32)  82.9 us
    ppermute x18, starting transfers between devices, reduce_steps(): lax.ppermute(sends[0], 'row', [(i, i + 1) for i in range(step + 1)])  78.3 us
    pallas_call x1, Pallas kernels, gather_all(): pl.pallas_call(functools.partial(gather_kernel, row_total, col_total, arr...  75.6 us
    ppermute x18, waiting for transfers between devices, reduce_steps(): lax.ppermute(sends[0], 'row', [(i, i + 1) for i in range(step + 1)])  64.5 us
  transfers between devices with their start and end apart: 75, of which 33 were waited for; matrix products, arithmetic and copies ran while one was open for 25% of the time, Pallas kernels for 25%

profile of v5, /device:TPU:0, one launch (start us, length us, event | category | flops | bytes accessed | tf_op | source)
XLA Modules:
  0.0 1195.8 jit_solution(16810379363673451189)
XLA Ops:
  18.6 75.6 %gather_pack.1 = (bf16[4,8,80,1152]{3,2,1,0:T(8,128)(2,1)}, bf16[4,8,128,1280]{3,2,1,0:T(8,128)(2,1)}) custom-call(bf16[80,1152]{1,0:T(8,128)(2,1)} %pad.30.refs_0_, bf16[128,1280]{1,0:T(8,128)(2,1)} %pad_maximum_fusion.9.refs_1_), custom_call_target="tpu_custom_call" | custom-call | tf_op jit(solution)/shard_map/gather_pack/pallas_call | solution.py:539
  115.4 11.1 collective-permute-done.1
  128.5 15.4 %collective-permute-done.2 = bf16[384,384]{0,1:T(8,128)(2,1)S(1)} collective-permute-done((bf16[384,384]{0,1:T(8,128)(2,1)S(1)}, bf16[384,384]{0,1:T(8,128)(2,1)S(1)}, u32[]{:S(2)}, u32[]{:S(2)}) %collective-permute-start.2) | collective-permute-done | bytes 294944 | tf_op jit(solution)/shard_map/ppermute | solution.py:802
  146.0 14.9 %collective-permute-done.3 = bf16[384,384]{0,1:T(8,128)(2,1)S(1)} collective-permute-done((bf16[384,384]{0,1:T(8,128)(2,1)S(1)}, bf16[384,384]{0,1:T(8,128)(2,1)S(1)}, u32[]{:S(2)}, u32[]{:S(2)}) %collective-permute-start.3) | collective-permute-done | bytes 294944 | tf_op jit(solution)/shard_map/ppermute | solution.py:802
  185.7 11.0 attend.4
  229.3 11.4 attend.7
  250.9 20.0 %collective-permute-done.8 = bf16[192,2560]{1,0:T(8,128)(2,1)S(1)} collective-permute-done((bf16[192,2560]{1,0:T(8,128)(2,1)S(1)}, bf16[192,2560]{1,0:T(8,128)(2,1)S(1)}, u32[]{:S(2)}, u32[]{:S(2)}) %collective-permute-start.8) | collective-permute-done | bytes 983072 | tf_op jit(solution)/shard_map/ppermute | solution.py:801
  278.0 24.5 %collective-permute-done.11 = bf16[192,2560]{1,0:T(8,128)(2,1)} collective-permute-done((bf16[192,2560]{1,0:T(8,128)(2,1)S(1)}, bf16[192,2560]{1,0:T(8,128)(2,1)}, u32[]{:S(2)}, u32[]{:S(2)}) %collective-permute-start.11) | collective-permute-done | bytes 983072 | tf_op jit(solution)/shard_map/ppermute | solution.py:802
  317.1 13.9 %collective-permute-done.13 = bf16[192,2560]{1,0:T(8,128)(2,1)} collective-permute-done((bf16[192,2560]{1,0:T(8,128)(2,1)}, bf16[192,2560]{1,0:T(8,128)(2,1)}, u32[]{:S(2)}, u32[]{:S(2)}) %collective-permute-start.13) | collective-permute-done | bytes 983072 | tf_op jit(solution)/shard_map/ppermute | solution.py:802
  336.3 11.6 convolution_convert_fusion.3
  360.9 13.2 %collective-permute-done.15 = bf16[192,2560]{1,0:T(8,128)(2,1)} collective-permute-done((bf16[192,2560]{1,0:T(8,128)(2,1)}, bf16[192,2560]{1,0:T(8,128)(2,1)}, u32[]{:S(2)}, u32[]{:S(2)}) %collective-permute-start.15) | collective-permute-done | bytes 983072 | tf_op jit(solution)/shard_map/ppermute | solution.py:802
  426.2 14.2 %fusion.21 = (bf16[768,1600]{1,0:T(8,128)(2,1)S(1)}, bf16[768,1600]{1,0:T(8,128)(2,1)}) fusion(bf16[768,1600]{1,0:T(8,128)(2,1)S(1)} %convolution_convert_fusion.2, bf16[2560,1600]{1,0:T(8,128)(2,1)} %all-gather.9.cloned.1.call-done, bf16[192,2560]{1,0:T(8,128)(2,1)S(1)} %add.406, bf16[192,2560]{1,0:T(8,128)(2,1)S(1)} %copy-done.40, ...), kind=kOutput, calls=%fused_computation.35 | convolution fusion | flops 6317015040 | bytes 19496960 | tf_op jit(solution)/shard_map/dot_general | solution.py:30
  479.0 15.3 %collective-permute-done.24 = bf16[192,2560]{1,0:T(8,128)(2,1)S(1)} collective-permute-done((bf16[192,2560]{1,0:T(8,128)(2,1)S(1)}, bf16[192,2560]{1,0:T(8,128)(2,1)S(1)}, u32[]{:S(2)}, u32[]{:S(2)}) %collective-permute-start.24) | collective-permute-done | bytes 983072 | tf_op jit(solution)/shard_map/ppermute | solution.py:801
  496.4 14.0 %collective-permute-done.28 = bf16[192,2560]{1,0:T(8,128)(2,1)S(1)} collective-permute-done((bf16[192,2560]{1,0:T(8,128)(2,1)S(1)}, bf16[192,2560]{1,0:T(8,128)(2,1)S(1)}, u32[]{:S(2)}, u32[]{:S(2)}) %collective-permute-start.28) | collective-permute-done | bytes 983072 | tf_op jit(solution)/shard_map/ppermute | solution.py:821
  528.9 12.8 %collective-permute-done.32 = bf16[192,2560]{1,0:T(8,128)(2,1)S(1)} collective-permute-done((bf16[192,2560]{1,0:T(8,128)(2,1)S(1)}, bf16[192,2560]{1,0:T(8,128)(2,1)S(1)}, u32[]{:S(2)}, u32[]{:S(2)}) %collective-permute-start.32) | collective-permute-done | bytes 983072 | tf_op jit(solution)/shard_map/ppermute | solution.py:821
  556.4 15.2 %fusion.16 = (bf16[768,1600]{1,0:T(8,128)(2,1)S(1)}, bf16[768,1600]{1,0:T(8,128)(2,1)S(1)}) fusion(bf16[768,1600]{1,0:T(8,128)(2,1)} %copy-done.92, bf16[768,1600]{1,0:T(8,128)(2,1)} %get-tuple-element.372, bf16[2560,1600]{1,0:T(8,128)(2,1)} %all-gather.11.cloned.1.call-done, bf16[192,2560]{1,0:T(8,128)(2,1)} %add.424, bf16[192,2560]{1,0:T(8,128)(2,1)S(1)} %add.423, ...), kind=kOutput, calls=%fused_computation.30 | convolution fusion | flops 6325616640 | bytes 21954560 | tf_op jit(solution)/shard_map/dot_general | solution.py:30
  593.8 11.7 fusion.97
  626.9 15.0 %collective-permute-done.39 = bf16[192,2560]{1,0:T(8,128)(2,1)} collective-permute-done((bf16[192,2560]{1,0:T(8,128)(2,1)}, bf16[192,2560]{1,0:T(8,128)(2,1)}, u32[]{:S(2)}, u32[]{:S(2)}) %collective-permute-start.39) | collective-permute-done | bytes 983072 | tf_op jit(solution)/shard_map/ppermute | solution.py:802
  651.6 14.5 %collective-permute-done.42 = bf16[192,2560]{1,0:T(8,128)(2,1)S(1)} collective-permute-done((bf16[192,2560]{1,0:T(8,128)(2,1)S(1)}, bf16[192,2560]{1,0:T(8,128)(2,1)S(1)}, u32[]{:S(2)}, u32[]{:S(2)}) %collective-permute-start.42) | collective-permute-done | bytes 983072 | tf_op jit(solution)/shard_map/ppermute | solution.py:821
  681.8 18.9 %down_wg.1 = bf16[2560,1600]{1,0:T(8,128)(2,1)} custom-call(bf16[768,2560]{1,0:T(8,128)(2,1)} %pad_maximum_fusion.2.refs_0_, bf16[768,2560]{1,0:T(8,128)(2,1)} %pad_maximum_fusion.3.refs_1_, bf16[768,1600]{1,0:T(8,128)(2,1)S(1)} %copy-done.20, bf16[768,1600]{1,0:T(8,128)(2,1)S(1)} %get-tuple-element.172.refs_3_), custom_call_target="tpu_custom_call" | custom-call | flops 12582912000 | bytes 16056320 | tf_op jit(solution)/shard_map/down_wg/pallas_call | solution.py:340
  714.2 15.7 %fusion.26 = (bf16[768,1600]{1,0:T(8,128)(2,1)S(1)}, bf16[768,1600]{1,0:T(8,128)(2,1)S(1)}) fusion(bf16[768,1600]{1,0:T(8,128)(2,1)} %copy-done.93, bf16[768,1600]{1,0:T(8,128)(2,1)} %get-tuple-element.374, bf16[2560,1600]{1,0:T(8,128)(2,1)} %all-gather.11.cloned.1.call-done, bf16[192,2560]{1,0:T(8,128)(2,1)S(1)} %copy-done.55, ...), kind=kOutput, calls=%fused_computation.40 | convolution fusion | flops 6325616640 | bytes 21954560 | tf_op jit(solution)/shard_map/dot_general | solution.py:30
  731.1 12.0 fusion.98
  744.5 12.1 %add_convert_fusion = bf16[768,2560]{1,0:T(8,128)(2,1)S(1)} fusion(f32[768,2560]{1,0:T(8,128)} %fusion.98, bf16[768,1600]{1,0:T(8,128)(2,1)S(1)} %get-tuple-element.204.refs_3_, bf16[2560,1600]{1,0:T(8,128)(2,1)} %all-gather.7.cloned.1.call-done), kind=kOutput, calls=%fused_computation.12 | convolution fusion | flops 6295388160 | bytes 22446080 | tf_op jit(solution)/shard_map/dot_general | solution.py:34
  766.7 18.9 %gate_wg.1 = bf16[2560,1600]{1,0:T(8,128)(2,1)} custom-call(bf16[768,2560]{1,0:T(8,128)(2,1)} %pad_maximum_fusion.refs_0_, bf16[768,2560]{1,0:T(8,128)(2,1)} %pad_maximum_fusion.1.refs_1_, bf16[768,1600]{1,0:T(8,128)(2,1)S(1)} %copy-done.16, bf16[768,1600]{1,0:T(8,128)(2,1)S(1)} %get-tuple-element.204.refs_3_), custom_call_target="tpu_custom_call" | custom-call | flops 12582912000 | bytes 16056320 | tf_op jit(solution)/shard_map/gate_wg/pallas_call | solution.py:340
  795.2 18.7 %up_wg.1 = bf16[2560,1600]{1,0:T(8,128)(2,1)} custom-call(bf16[768,2560]{1,0:T(8,128)(2,1)} %pad_maximum_fusion.refs_0_, bf16[768,2560]{1,0:T(8,128)(2,1)} %pad_maximum_fusion.1.refs_1_, bf16[768,1600]{1,0:T(8,128)(2,1)S(1)} %get-tuple-element.192.refs_2_, bf16[768,1600]{1,0:T(8,128)(2,1)S(1)} %copy-done.18), custom_call_target="tpu_custom_call" | custom-call | flops 12582912000 | bytes 16056320 | tf_op jit(solution)/shard_map/up_wg/pallas_call | solution.py:340
  842.7 13.0 %out_wg.1 = bf16[2560,2560]{1,0:T(8,128)(2,1)} custom-call(bf16[384,2560]{1,0:T(8,128)(2,1)} %get-tuple-element.290.tokens_ref, bf16[2560,384]{1,0:T(8,128)(2,1)} %pad_maximum_fusion.6.mixed_ref), custom_call_target="tpu_custom_call" | custom-call | flops 5033164800 | bytes 13107200 | tf_op jit(solution)/shard_map/out_wg/pallas_call | solution.py:370
  855.7 11.7 fusion.59
  873.4 26.7 %attend_back.4 = (bf16[8,4,128,1280]{3,2,1,0:T(8,128)(2,1)}, f32[768,384]{1,0:T(8,128)S(1)}, f32[1024,384]{1,0:T(8,128)}) custom-call(bf16[4,8,128,1280]{3,2,1,0:T(8,128)(2,1)} %get-tuple-element.131.weights_ref, bf16[768,384]{1,0:T(8,128)(2,1)S(1)} %fusion.68.query_t_ref, bf16[1024,256]{1,0:T(8,128)(2,1)S(1)} %copy-done.11, ...), custom_call_target="tpu_custom_call" | custom-call | flops 24999999488 | bytes 5242880 | tf_op jit(solution)/shard_map/attend_back/pallas_call | solution.py:276
  900.1 26.3 %attend_back.5 = (bf16[8,4,128,1280]{3,2,1,0:T(8,128)(2,1)}, f32[768,384]{1,0:T(8,128)S(1)}, f32[1024,384]{1,0:T(8,128)}) custom-call(bf16[4,8,128,1280]{3,2,1,0:T(8,128)(2,1)} %get-tuple-element.131.weights_ref, bf16[768,384]{1,0:T(8,128)(2,1)S(1)} %fusion.68.query_t_ref, bf16[1024,256]{1,0:T(8,128)(2,1)S(1)} %copy-done.11, ...), custom_call_target="tpu_custom_call", output_to_operand_aliasing={{0}: (13, {})} | custom-call | flops 24999999488 | bytes 5242880 | tf_op jit(solution)/shard_map/attend_back/pallas_call | solution.py:276
  934.7 26.2 %attend_back.6 = (bf16[8,4,128,1280]{3,2,1,0:T(8,128)(2,1)}, f32[768,384]{1,0:T(8,128)S(1)}, f32[1024,384]{1,0:T(8,128)}) custom-call(bf16[4,8,128,1280]{3,2,1,0:T(8,128)(2,1)} %get-tuple-element.131.weights_ref, bf16[768,384]{1,0:T(8,128)(2,1)S(1)} %fusion.68.query_t_ref, bf16[1024,256]{1,0:T(8,128)(2,1)S(1)} %copy-done.12, ...), custom_call_target="tpu_custom_call", output_to_operand_aliasing={{0}: (13, {})} | custom-call | flops 24999999488 | bytes 5242880 | tf_op jit(solution)/shard_map/attend_back/pallas_call | solution.py:276
  961.0 26.1 %attend_back.7 = (bf16[8,4,128,1280]{3,2,1,0:T(8,128)(2,1)}, f32[768,384]{1,0:T(8,128)S(1)}, f32[1024,384]{1,0:T(8,128)}) custom-call(bf16[4,8,128,1280]{3,2,1,0:T(8,128)(2,1)} %get-tuple-element.131.weights_ref, bf16[768,384]{1,0:T(8,128)(2,1)S(1)} %fusion.68.query_t_ref, bf16[1024,256]{1,0:T(8,128)(2,1)S(1)} %copy-done.12, ...), custom_call_target="tpu_custom_call", output_to_operand_aliasing={{0}: (13, {})} | custom-call | flops 24999999488 | bytes 5242880 | tf_op jit(solution)/shard_map/attend_back/pallas_call | solution.py:276
  1059.1 82.9 %reduce_down.1 = (f32[80,1152]{1,0:T(8,128)S(1)}, f32[320,640]{1,0:T(8,128)S(1)}) custom-call(bf16[4,4,2,80,1152]{4,3,2,1,0:T(8,128)(2,1)} %bitcast.137, bf16[4,320,640]{2,1,0:T(8,128)(2,1)S(1)} %pad_maximum_fusion.7.side_ref), custom_call_target="tpu_custom_call" | custom-call | tf_op jit(solution)/shard_map/reduce_down/pallas_call | solution.py:728
  (525 shorter events, 524.9 us)
Async XLA Ops:
  7.2 199.3 %all-gather.5.cloned.1.call-start = ((), (), s32[]{:S(2)}) async-start(), calls=%async_computation.5 | async-start | bytes 13516800 | tf_op jit(solution)/shard_map/all_gather | solution.py:899
  98.8 237.4 %all-gather.7.cloned.1.call-start = ((), (), s32[]{:S(2)}) async-start(), calls=%async_computation.6 | async-start | bytes 9584640 | tf_op jit(solution)/shard_map/all_gather | solution.py:933
  162.2 174.1 %all-gather.9.cloned.1.call-start = ((), (), s32[]{:S(2)}) async-start(), calls=%async_computation.7 | async-start | bytes 9584640 | tf_op jit(solution)/shard_map/all_gather | solution.py:934
  162.9 216.7 %all-gather.11.cloned.1.call-start = ((), (), s32[]{:S(2)}) async-start(), calls=%async_computation.8 | async-start | bytes 9584640 | tf_op jit(solution)/shard_map/all_gather | solution.py:935
  173.8 753.6 %reduce-scatter.10.cloned.1.call-start = ((), (), s32[]{:S(2)}) async-start(), calls=%async_computation.11 | async-start | bytes 9584640 | tf_op jit(solution)/shard_map/reduce_scatter | solution.py:1094
  246.8 24.1 %collective-permute-start.8 = (bf16[192,2560]{1,0:T(8,128)(2,1)S(1)}, bf16[192,2560]{1,0:T(8,128)(2,1)S(1)}, u32[]{:S(2)}, u32[]{:S(2)}) collective-permute-start(bf16[192,2560]{1,0:T(8,128)(2,1)S(1)} %get-tuple-element.334), channel_id=1, source_target_pairs={{0,8},{8,16},{16,24},{1,9},{9,17},{17,25},{2,10},{10,18},{18,26},{... | collective-permute-start | bytes 2949128 | tf_op jit(solution)/shard_map/ppermute | solution.py:801
  249.6 25.5 %collective-permute-start.9 = (bf16[192,2560]{1,0:T(8,128)(2,1)S(1)}, bf16[192,2560]{1,0:T(8,128)(2,1)S(1)}, u32[]{:S(2)}, u32[]{:S(2)}) collective-permute-start(bf16[192,2560]{1,0:T(8,128)(2,1)S(1)} %get-tuple-element.334), channel_id=1, source_target_pairs={{8,0},{16,8},{24,16},{9,1},{17,9},{25,17},{10,2},{18,10},{26,18},{... | collective-permute-start | bytes 2949128 | tf_op jit(solution)/shard_map/ppermute | solution.py:802
  276.7 25.8 %collective-permute-start.11 = (bf16[192,2560]{1,0:T(8,128)(2,1)S(1)}, bf16[192,2560]{1,0:T(8,128)(2,1)}, u32[]{:S(2)}, u32[]{:S(2)}) collective-permute-start(bf16[192,2560]{1,0:T(8,128)(2,1)S(1)} %collective-permute-done.9), channel_id=1, source_target_pairs={{8,0},{16,8},{9,1},{17,9},{10,2},{18,10},{11,3},{19,11},{12,4},{20... | collective-permute-start | bytes 2949128 | tf_op jit(solution)/shard_map/ppermute | solution.py:802
  304.1 26.9 %collective-permute-start.13 = (bf16[192,2560]{1,0:T(8,128)(2,1)}, bf16[192,2560]{1,0:T(8,128)(2,1)}, u32[]{:S(2)}, u32[]{:S(2)}) collective-permute-start(bf16[192,2560]{1,0:T(8,128)(2,1)} %collective-permute-done.11), channel_id=1, source_target_pairs={{8,0},{9,1},{10,2},{11,3},{12,4},{13,5},{14,6},{15,7}} | collective-permute-start | bytes 2949128 | tf_op jit(solution)/shard_map/ppermute | solution.py:802
  307.5 40.4 %collective-permute-start.6 = (bf16[192,2560]{1,0:T(8,128)(2,1)S(1)}, bf16[192,2560]{1,0:T(8,128)(2,1)}, u32[]{:S(2)}, u32[]{:S(2)}) collective-permute-start(bf16[192,2560]{1,0:T(8,128)(2,1)S(1)} %get-tuple-element.335), channel_id=1, source_target_pairs={{0,8},{8,16},{16,24},{1,9},{9,17},{17,25},{2,10},{10,18},{18,26},{... | collective-permute-start | bytes 2949128 | tf_op jit(solution)/shard_map/ppermute | solution.py:801
  314.1 35.2 %collective-permute-start.7 = (bf16[192,2560]{1,0:T(8,128)(2,1)S(1)}, bf16[192,2560]{1,0:T(8,128)(2,1)}, u32[]{:S(2)}, u32[]{:S(2)}) collective-permute-start(bf16[192,2560]{1,0:T(8,128)(2,1)S(1)} %get-tuple-element.335), channel_id=1, source_target_pairs={{8,0},{16,8},{24,16},{9,1},{17,9},{25,17},{10,2},{18,10},{26,18},{... | collective-permute-start | bytes 2949128 | tf_op jit(solution)/shard_map/ppermute | solution.py:802
  350.9 23.2 %collective-permute-start.15 = (bf16[192,2560]{1,0:T(8,128)(2,1)}, bf16[192,2560]{1,0:T(8,128)(2,1)}, u32[]{:S(2)}, u32[]{:S(2)}) collective-permute-start(bf16[192,2560]{1,0:T(8,128)(2,1)} %collective-permute-done.7), channel_id=1, source_target_pairs={{8,0},{16,8},{9,1},{17,9},{10,2},{18,10},{11,3},{19,11},{12,4},{20... | collective-permute-start | bytes 2949128 | tf_op jit(solution)/shard_map/ppermute | solution.py:802
  375.7 22.3 %collective-permute-start.17 = (bf16[192,2560]{1,0:T(8,128)(2,1)}, bf16[192,2560]{1,0:T(8,128)(2,1)}, u32[]{:S(2)}, u32[]{:S(2)}) collective-permute-start(bf16[192,2560]{1,0:T(8,128)(2,1)} %collective-permute-done.15), channel_id=1, source_target_pairs={{8,0},{9,1},{10,2},{11,3},{12,4},{13,5},{14,6},{15,7}} | collective-permute-start | bytes 2949128 | tf_op jit(solution)/shard_map/ppermute | solution.py:802
  470.1 24.3 %collective-permute-start.24 = (bf16[192,2560]{1,0:T(8,128)(2,1)S(1)}, bf16[192,2560]{1,0:T(8,128)(2,1)S(1)}, u32[]{:S(2)}, u32[]{:S(2)}) collective-permute-start(bf16[192,2560]{1,0:T(8,128)(2,1)S(1)} %get-tuple-element.296), channel_id=1, source_target_pairs={{0,8},{8,16},{16,24},{1,9},{9,17},{17,25},{2,10},{10,18},{18,26},{... | collective-permute-start | bytes 2949128 | tf_op jit(solution)/shard_map/ppermute | solution.py:801
  472.2 22.1 %collective-permute-start.25 = (bf16[192,2560]{1,0:T(8,128)(2,1)S(1)}, bf16[192,2560]{1,0:T(8,128)(2,1)S(1)}, u32[]{:S(2)}, u32[]{:S(2)}) collective-permute-start(bf16[192,2560]{1,0:T(8,128)(2,1)S(1)} %get-tuple-element.296), channel_id=1, source_target_pairs={{8,0},{16,8},{24,16},{9,1},{17,9},{25,17},{10,2},{18,10},{26,18},{... | collective-permute-start | bytes 2949128 | tf_op jit(solution)/shard_map/ppermute | solution.py:802
  473.7 36.7 %collective-permute-start.28 = (bf16[192,2560]{1,0:T(8,128)(2,1)S(1)}, bf16[192,2560]{1,0:T(8,128)(2,1)S(1)}, u32[]{:S(2)}, u32[]{:S(2)}) collective-permute-start(bf16[192,2560]{1,0:T(8,128)(2,1)S(1)} %get-tuple-element.326), channel_id=1, source_target_pairs={{0,8},{1,9},{2,10},{3,11},{4,12},{5,13},{6,14},{7,15}} | collective-permute-start | bytes 2949128 | tf_op jit(solution)/shard_map/ppermute | solution.py:821
  478.3 32.1 %collective-permute-start.29 = (bf16[192,2560]{1,0:T(8,128)(2,1)S(1)}, bf16[192,2560]{1,0:T(8,128)(2,1)S(1)}, u32[]{:S(2)}, u32[]{:S(2)}) collective-permute-start(bf16[192,2560]{1,0:T(8,128)(2,1)S(1)} %get-tuple-element.325), channel_id=1, source_target_pairs={{24,16},{25,17},{26,18},{27,19},{28,20},{29,21},{30,22},{31,23}} | collective-permute-start | bytes 2949128 | tf_op jit(solution)/shard_map/ppermute | solution.py:822
  495.1 24.3 %collective-permute-start.27 = (bf16[192,2560]{1,0:T(8,128)(2,1)S(1)}, bf16[192,2560]{1,0:T(8,128)(2,1)S(1)}, u32[]{:S(2)}, u32[]{:S(2)}) collective-permute-start(bf16[192,2560]{1,0:T(8,128)(2,1)S(1)} %collective-permute-done.25), channel_id=1, source_target_pairs={{8,0},{16,8},{9,1},{17,9},{10,2},{18,10},{11,3},{19,11},{12,4},{20... | collective-permute-start | bytes 2949128 | tf_op jit(solution)/shard_map/ppermute | solution.py:802
  555.1 22.7 %collective-permute-start.35 = (bf16[192,2560]{1,0:T(8,128)(2,1)}, bf16[192,2560]{1,0:T(8,128)(2,1)}, u32[]{:S(2)}, u32[]{:S(2)}) collective-permute-start(bf16[192,2560]{1,0:T(8,128)(2,1)} %get-tuple-element.321), channel_id=1, source_target_pairs={{8,0},{16,8},{24,16},{9,1},{17,9},{25,17},{10,2},{18,10},{26,18},{... | collective-permute-start | bytes 2949128 | tf_op jit(solution)/shard_map/ppermute | solution.py:822
  583.8 31.3 %collective-permute-start.36 = (bf16[192,2560]{1,0:T(8,128)(2,1)S(1)}, bf16[192,2560]{1,0:T(8,128)(2,1)}, u32[]{:S(2)}, u32[]{:S(2)}) collective-permute-start(bf16[192,2560]{1,0:T(8,128)(2,1)S(1)} %get-tuple-element.292), channel_id=1, source_target_pairs={{0,8},{8,16},{16,24},{1,9},{9,17},{17,25},{2,10},{10,18},{18,26},{... | collective-permute-start | bytes 2949128 | tf_op jit(solution)/shard_map/ppermute | solution.py:801
  592.5 22.6 %collective-permute-start.37 = (bf16[192,2560]{1,0:T(8,128)(2,1)S(1)}, bf16[192,2560]{1,0:T(8,128)(2,1)}, u32[]{:S(2)}, u32[]{:S(2)}) collective-permute-start(bf16[192,2560]{1,0:T(8,128)(2,1)S(1)} %get-tuple-element.292), channel_id=1, source_target_pairs={{8,0},{16,8},{24,16},{9,1},{17,9},{25,17},{10,2},{18,10},{26,18},{... | collective-permute-start | bytes 2949128 | tf_op jit(solution)/shard_map/ppermute | solution.py:802
  616.9 25.0 %collective-permute-start.39 = (bf16[192,2560]{1,0:T(8,128)(2,1)}, bf16[192,2560]{1,0:T(8,128)(2,1)}, u32[]{:S(2)}, u32[]{:S(2)}) collective-permute-start(bf16[192,2560]{1,0:T(8,128)(2,1)} %collective-permute-done.37), channel_id=1, source_target_pairs={{8,0},{16,8},{9,1},{17,9},{10,2},{18,10},{11,3},{19,11},{12,4},{20... | collective-permute-start | bytes 2949128 | tf_op jit(solution)/shard_map/ppermute | solution.py:802
  643.5 22.6 %collective-permute-start.42 = (bf16[192,2560]{1,0:T(8,128)(2,1)S(1)}, bf16[192,2560]{1,0:T(8,128)(2,1)S(1)}, u32[]{:S(2)}, u32[]{:S(2)}) collective-permute-start(bf16[192,2560]{1,0:T(8,128)(2,1)S(1)} %get-tuple-element.320), channel_id=1, source_target_pairs={{0,8},{1,9},{2,10},{3,11},{4,12},{5,13},{6,14},{7,15}} | collective-permute-start | bytes 2949128 | tf_op jit(solution)/shard_map/ppermute | solution.py:821
  672.6 28.0 %collective-permute-start.44 = (bf16[192,2560]{1,0:T(8,128)(2,1)}, bf16[192,2560]{1,0:T(8,128)(2,1)}, u32[]{:S(2)}, u32[]{:S(2)}) collective-permute-start(bf16[192,2560]{1,0:T(8,128)(2,1)} %get-tuple-element.318), channel_id=1, source_target_pairs={{0,8},{8,16},{1,9},{9,17},{2,10},{10,18},{3,11},{11,19},{4,12},{12... | collective-permute-start | bytes 2949128 | tf_op jit(solution)/shard_map/ppermute | solution.py:821
  678.0 22.7 %collective-permute-start.45 = (bf16[192,2560]{1,0:T(8,128)(2,1)}, bf16[192,2560]{1,0:T(8,128)(2,1)}, u32[]{:S(2)}, u32[]{:S(2)}) collective-permute-start(bf16[192,2560]{1,0:T(8,128)(2,1)} %get-tuple-element.317), channel_id=1, source_target_pairs={{16,8},{24,16},{17,9},{25,17},{18,10},{26,18},{19,11},{27,19},{20,... | collective-permute-start | bytes 2949128 | tf_op jit(solution)/shard_map/ppermute | solution.py:822
  700.7 226.7 %reduce-scatter.6.cloned.1.call-start = ((), (), s32[]{:S(2)}) async-start(), calls=%async_computation.9 | async-start | bytes 9584640 | tf_op jit(solution)/shard_map/reduce_scatter | solution.py:1092
  707.7 22.2 %collective-permute-start.46 = (bf16[192,2560]{1,0:T(8,128)(2,1)S(1)}, bf16[192,2560]{1,0:T(8,128)(2,1)S(1)}, u32[]{:S(2)}, u32[]{:S(2)}) collective-permute-start(bf16[192,2560]{1,0:T(8,128)(2,1)S(1)} %get-tuple-element.316), channel_id=1, source_target_pairs={{0,8},{8,16},{16,24},{1,9},{9,17},{17,25},{2,10},{10,18},{18,26},{... | collective-permute-start | bytes 2949128 | tf_op jit(solution)/shard_map/ppermute | solution.py:821
  760.0 25.6 %collective-permute-start.48 = (bf16[192,2560]{1,0:T(8,128)(2,1)}, bf16[192,2560]{1,0:T(8,128)(2,1)}, u32[]{:S(2)}, u32[]{:S(2)}) collective-permute-start(bf16[192,2560]{1,0:T(8,128)(2,1)} %get-tuple-element.314), channel_id=1, source_target_pairs={{0,8},{1,9},{2,10},{3,11},{4,12},{5,13},{6,14},{7,15}} | collective-permute-start | bytes 2949128 | tf_op jit(solution)/shard_map/ppermute | solution.py:821
  785.7 146.7 %reduce-scatter.8.cloned.1.call-start = ((), (), s32[]{:S(2)}) async-start(), calls=%async_computation.10 | async-start | bytes 9584640 | tf_op jit(solution)/shard_map/reduce_scatter | solution.py:1093
  789.4 24.5 %collective-permute-start.50 = (bf16[192,2560]{1,0:T(8,128)(2,1)}, bf16[192,2560]{1,0:T(8,128)(2,1)}, u32[]{:S(2)}, u32[]{:S(2)}) collective-permute-start(bf16[192,2560]{1,0:T(8,128)(2,1)} %get-tuple-element.312), channel_id=1, source_target_pairs={{0,8},{8,16},{1,9},{9,17},{2,10},{10,18},{3,11},{11,19},{4,12},{12... | collective-permute-start | bytes 2949128 | tf_op jit(solution)/shard_map/ppermute | solution.py:821
  814.0 243.4 %reduce-scatter.12.cloned.1.call-start = ((), (), s32[]{:S(2)}) async-start(), calls=%async_computation.12 | async-start | bytes 14745600 | tf_op jit(solution)/shard_map/reduce_scatter | solution.py:1104
  867.4 274.6 %reduce-scatter.14.cloned.1.call-start = ((), (), s32[]{:S(2)}) async-start(), calls=%async_computation.13 | async-start | bytes 11796480 | tf_op jit(solution)/shard_map/reduce_scatter | solution.py:1115
  (140 other events, 2354.1 us)
Sparse Core Ops, SparseCore 0:
  99.0 107.4 all-gather.4
  208.3 53.1 all-gather.6
  263.4 54.9 all-gather.8
  320.1 54.9 all-gather.10
  700.8 71.6 reduce-scatter.9
  785.8 70.9 reduce-scatter.5
  860.3 72.0 reduce-scatter.7
  936.0 95.1 reduce-scatter.11
  1034.7 105.1 reduce-scatter.13

commit v6 on v5

--- a/solution.py
+++ b/solution.py
@@ -272,7 +272,7 @@
     group = math.gcd(heads, 2)
     steps = heads // group
     length, local = bias_t.shape
-    tile = math.gcd(length, 256)
+    tile = math.gcd(length, 512)
     return pl.pallas_call(
         functools.partial(attend_back_kernel, query_rows, tile),
         grid=(steps,),

time: 1210 us -> 1200 us (level)
    pallas_call x4, Pallas kernels: 105 us -> 92.6 us  [attend_back(): pl.pallas_call(functools.partial(attend_back_kernel, query_rows, tile), g...]
  transfers between devices with their start and end apart: 75 -> 75, of which waited for: 33 -> 33; matrix products, arithmetic and copies ran while one was open for 25% -> 25% of each run, Pallas kernels for 25% -> 24%
where the time goes in v6:
time: 1200 us; the launch traced here: 1190 us
  Pallas kernels  366 us (30%)
  waiting for transfers between devices  282 us (24%)
  matrix products  193 us (16%)
  starting transfers between devices  156 us (13%)
  other arithmetic  116 us (10%)
  local copies, waits for them, and re-layouts  51.9 us (4%)
  between operations  26.3 us (2%)
    ppermute x15, waiting for transfers between devices, gather_steps(): lax.ppermute(ways[1], 'row', [(i, i - 1) for i in range(1, total - step +...  138 us
    dot_general x13, matrix products, dot_dims(): lax.dot_general(left_op, right_op, ((left_dims, right_dims), ((), ())), p...  110 us
    pallas_call x4, Pallas kernels, attend_back(): pl.pallas_call(functools.partial(attend_back_kernel, query_rows, tile), g...  92.6 us
    pallas_call x1, Pallas kernels, reduce_all(): pl.pallas_call(functools.partial(reduce_kernel, row_total, col_total), in...  84.2 us
    dot_general x7, matrix products, dot_plain(): return jnp.dot(left_op, right_op, preferred_element_type=F32)  82.9 us
    ppermute x18, starting transfers between devices, reduce_steps(): lax.ppermute(sends[0], 'row', [(i, i + 1) for i in range(step + 1)])  78.4 us
    pallas_call x1, Pallas kernels, gather_all(): pl.pallas_call(functools.partial(gather_kernel, row_total, col_total, arr...  75.6 us
    ppermute x18, waiting for transfers between devices, reduce_steps(): lax.ppermute(sends[0], 'row', [(i, i + 1) for i in range(step + 1)])  64.6 us
  transfers between devices with their start and end apart: 75, of which 33 were waited for; matrix products, arithmetic and copies ran while one was open for 25% of the time, Pallas kernels for 24%

profile of v6, /device:TPU:0, one launch (start us, length us, event | category | flops | bytes accessed | tf_op | source)
XLA Modules:
  0.0 1190.0 jit_solution(8798603528103407412)
XLA Ops:
  18.6 75.6 %gather_pack.1 = (bf16[4,8,80,1152]{3,2,1,0:T(8,128)(2,1)}, bf16[4,8,128,1280]{3,2,1,0:T(8,128)(2,1)}) custom-call(bf16[80,1152]{1,0:T(8,128)(2,1)} %pad.30.refs_0_, bf16[128,1280]{1,0:T(8,128)(2,1)} %pad_maximum_fusion.9.refs_1_), custom_call_target="tpu_custom_call" | custom-call | tf_op jit(solution)/shard_map/gather_pack/pallas_call | solution.py:539
  115.4 11.1 collective-permute-done.1
  128.5 15.4 %collective-permute-done.2 = bf16[384,384]{0,1:T(8,128)(2,1)S(1)} collective-permute-done((bf16[384,384]{0,1:T(8,128)(2,1)S(1)}, bf16[384,384]{0,1:T(8,128)(2,1)S(1)}, u32[]{:S(2)}, u32[]{:S(2)}) %collective-permute-start.2) | collective-permute-done | bytes 294944 | tf_op jit(solution)/shard_map/ppermute | solution.py:802
  146.0 14.9 %collective-permute-done.3 = bf16[384,384]{0,1:T(8,128)(2,1)S(1)} collective-permute-done((bf16[384,384]{0,1:T(8,128)(2,1)S(1)}, bf16[384,384]{0,1:T(8,128)(2,1)S(1)}, u32[]{:S(2)}, u32[]{:S(2)}) %collective-permute-start.3) | collective-permute-done | bytes 294944 | tf_op jit(solution)/shard_map/ppermute | solution.py:802
  229.3 11.4 attend.7
  250.9 20.0 %collective-permute-done.8 = bf16[192,2560]{1,0:T(8,128)(2,1)S(1)} collective-permute-done((bf16[192,2560]{1,0:T(8,128)(2,1)S(1)}, bf16[192,2560]{1,0:T(8,128)(2,1)S(1)}, u32[]{:S(2)}, u32[]{:S(2)}) %collective-permute-start.8) | collective-permute-done | bytes 983072 | tf_op jit(solution)/shard_map/ppermute | solution.py:801
  278.0 24.5 %collective-permute-done.11 = bf16[192,2560]{1,0:T(8,128)(2,1)} collective-permute-done((bf16[192,2560]{1,0:T(8,128)(2,1)S(1)}, bf16[192,2560]{1,0:T(8,128)(2,1)}, u32[]{:S(2)}, u32[]{:S(2)}) %collective-permute-start.11) | collective-permute-done | bytes 983072 | tf_op jit(solution)/shard_map/ppermute | solution.py:802
  317.1 13.9 %collective-permute-done.13 = bf16[192,2560]{1,0:T(8,128)(2,1)} collective-permute-done((bf16[192,2560]{1,0:T(8,128)(2,1)}, bf16[192,2560]{1,0:T(8,128)(2,1)}, u32[]{:S(2)}, u32[]{:S(2)}) %collective-permute-start.13) | collective-permute-done | bytes 983072 | tf_op jit(solution)/shard_map/ppermute | solution.py:802
  336.3 11.6 convolution_convert_fusion.3
  360.9 13.2 %collective-permute-done.15 = bf16[192,2560]{1,0:T(8,128)(2,1)} collective-permute-done((bf16[192,2560]{1,0:T(8,128)(2,1)}, bf16[192,2560]{1,0:T(8,128)(2,1)}, u32[]{:S(2)}, u32[]{:S(2)}) %collective-permute-start.15) | collective-permute-done | bytes 983072 | tf_op jit(solution)/shard_map/ppermute | solution.py:802
  426.2 14.2 %fusion.21 = (bf16[768,1600]{1,0:T(8,128)(2,1)S(1)}, bf16[768,1600]{1,0:T(8,128)(2,1)}) fusion(bf16[768,1600]{1,0:T(8,128)(2,1)S(1)} %convolution_convert_fusion.2, bf16[2560,1600]{1,0:T(8,128)(2,1)} %all-gather.9.cloned.1.call-done, bf16[192,2560]{1,0:T(8,128)(2,1)S(1)} %add.406, bf16[192,2560]{1,0:T(8,128)(2,1)S(1)} %copy-done.40, ...), kind=kOutput, calls=%fused_computation.35 | convolution fusion | flops 6317015040 | bytes 19496960 | tf_op jit(solution)/shard_map/dot_general | solution.py:30
  479.0 15.3 %collective-permute-done.24 = bf16[192,2560]{1,0:T(8,128)(2,1)S(1)} collective-permute-done((bf16[192,2560]{1,0:T(8,128)(2,1)S(1)}, bf16[192,2560]{1,0:T(8,128)(2,1)S(1)}, u32[]{:S(2)}, u32[]{:S(2)}) %collective-permute-start.24) | collective-permute-done | bytes 983072 | tf_op jit(solution)/shard_map/ppermute | solution.py:801
  496.4 14.0 %collective-permute-done.28 = bf16[192,2560]{1,0:T(8,128)(2,1)S(1)} collective-permute-done((bf16[192,2560]{1,0:T(8,128)(2,1)S(1)}, bf16[192,2560]{1,0:T(8,128)(2,1)S(1)}, u32[]{:S(2)}, u32[]{:S(2)}) %collective-permute-start.28) | collective-permute-done | bytes 983072 | tf_op jit(solution)/shard_map/ppermute | solution.py:821
  528.9 12.8 %collective-permute-done.32 = bf16[192,2560]{1,0:T(8,128)(2,1)S(1)} collective-permute-done((bf16[192,2560]{1,0:T(8,128)(2,1)S(1)}, bf16[192,2560]{1,0:T(8,128)(2,1)S(1)}, u32[]{:S(2)}, u32[]{:S(2)}) %collective-permute-start.32) | collective-permute-done | bytes 983072 | tf_op jit(solution)/shard_map/ppermute | solution.py:821
  556.4 15.2 %fusion.16 = (bf16[768,1600]{1,0:T(8,128)(2,1)S(1)}, bf16[768,1600]{1,0:T(8,128)(2,1)S(1)}) fusion(bf16[768,1600]{1,0:T(8,128)(2,1)} %copy-done.92, bf16[768,1600]{1,0:T(8,128)(2,1)} %get-tuple-element.372, bf16[2560,1600]{1,0:T(8,128)(2,1)} %all-gather.11.cloned.1.call-done, bf16[192,2560]{1,0:T(8,128)(2,1)} %add.424, bf16[192,2560]{1,0:T(8,128)(2,1)S(1)} %add.423, ...), kind=kOutput, calls=%fused_computation.30 | convolution fusion | flops 6325616640 | bytes 21954560 | tf_op jit(solution)/shard_map/dot_general | solution.py:30
  593.8 11.7 fusion.97
  626.9 15.0 %collective-permute-done.39 = bf16[192,2560]{1,0:T(8,128)(2,1)} collective-permute-done((bf16[192,2560]{1,0:T(8,128)(2,1)}, bf16[192,2560]{1,0:T(8,128)(2,1)}, u32[]{:S(2)}, u32[]{:S(2)}) %collective-permute-start.39) | collective-permute-done | bytes 983072 | tf_op jit(solution)/shard_map/ppermute | solution.py:802
  651.6 14.5 %collective-permute-done.42 = bf16[192,2560]{1,0:T(8,128)(2,1)S(1)} collective-permute-done((bf16[192,2560]{1,0:T(8,128)(2,1)S(1)}, bf16[192,2560]{1,0:T(8,128)(2,1)S(1)}, u32[]{:S(2)}, u32[]{:S(2)}) %collective-permute-start.42) | collective-permute-done | bytes 983072 | tf_op jit(solution)/shard_map/ppermute | solution.py:821
  681.8 18.9 %down_wg.1 = bf16[2560,1600]{1,0:T(8,128)(2,1)} custom-call(bf16[768,2560]{1,0:T(8,128)(2,1)} %pad_maximum_fusion.2.refs_0_, bf16[768,2560]{1,0:T(8,128)(2,1)} %pad_maximum_fusion.3.refs_1_, bf16[768,1600]{1,0:T(8,128)(2,1)S(1)} %copy-done.20, bf16[768,1600]{1,0:T(8,128)(2,1)S(1)} %get-tuple-element.172.refs_3_), custom_call_target="tpu_custom_call" | custom-call | flops 12582912000 | bytes 16056320 | tf_op jit(solution)/shard_map/down_wg/pallas_call | solution.py:340
  714.2 15.7 %fusion.26 = (bf16[768,1600]{1,0:T(8,128)(2,1)S(1)}, bf16[768,1600]{1,0:T(8,128)(2,1)S(1)}) fusion(bf16[768,1600]{1,0:T(8,128)(2,1)} %copy-done.93, bf16[768,1600]{1,0:T(8,128)(2,1)} %get-tuple-element.374, bf16[2560,1600]{1,0:T(8,128)(2,1)} %all-gather.11.cloned.1.call-done, bf16[192,2560]{1,0:T(8,128)(2,1)S(1)} %copy-done.55, ...), kind=kOutput, calls=%fused_computation.40 | convolution fusion | flops 6325616640 | bytes 21954560 | tf_op jit(solution)/shard_map/dot_general | solution.py:30
  731.1 12.0 %fusion.98 = f32[768,2560]{1,0:T(8,128)} fusion(bf16[768,1600]{1,0:T(8,128)(2,1)S(1)} %get-tuple-element.205.refs_3_, bf16[2560,1600]{1,0:T(8,128)(2,1)} %all-gather.9.cloned.1.call-done), kind=kOutput, calls=%fused_computation.257 | convolution fusion | flops 6291456000 | bytes 18513920 | tf_op jit(solution)/shard_map/dot_general | solution.py:34
  744.5 12.1 %add_convert_fusion = bf16[768,2560]{1,0:T(8,128)(2,1)S(1)} fusion(f32[768,2560]{1,0:T(8,128)} %fusion.98, bf16[768,1600]{1,0:T(8,128)(2,1)S(1)} %get-tuple-element.204.refs_3_, bf16[2560,1600]{1,0:T(8,128)(2,1)} %all-gather.7.cloned.1.call-done), kind=kOutput, calls=%fused_computation.12 | convolution fusion | flops 6295388160 | bytes 22446080 | tf_op jit(solution)/shard_map/dot_general | solution.py:34
  766.8 18.9 %gate_wg.1 = bf16[2560,1600]{1,0:T(8,128)(2,1)} custom-call(bf16[768,2560]{1,0:T(8,128)(2,1)} %pad_maximum_fusion.refs_0_, bf16[768,2560]{1,0:T(8,128)(2,1)} %pad_maximum_fusion.1.refs_1_, bf16[768,1600]{1,0:T(8,128)(2,1)S(1)} %copy-done.16, bf16[768,1600]{1,0:T(8,128)(2,1)S(1)} %get-tuple-element.204.refs_3_), custom_call_target="tpu_custom_call" | custom-call | flops 12582912000 | bytes 16056320 | tf_op jit(solution)/shard_map/gate_wg/pallas_call | solution.py:340
  795.1 18.7 %up_wg.1 = bf16[2560,1600]{1,0:T(8,128)(2,1)} custom-call(bf16[768,2560]{1,0:T(8,128)(2,1)} %pad_maximum_fusion.refs_0_, bf16[768,2560]{1,0:T(8,128)(2,1)} %pad_maximum_fusion.1.refs_1_, bf16[768,1600]{1,0:T(8,128)(2,1)S(1)} %get-tuple-element.192.refs_2_, bf16[768,1600]{1,0:T(8,128)(2,1)S(1)} %copy-done.18), custom_call_target="tpu_custom_call" | custom-call | flops 12582912000 | bytes 16056320 | tf_op jit(solution)/shard_map/up_wg/pallas_call | solution.py:340
  842.7 13.0 %out_wg.1 = bf16[2560,2560]{1,0:T(8,128)(2,1)} custom-call(bf16[384,2560]{1,0:T(8,128)(2,1)} %get-tuple-element.290.tokens_ref, bf16[2560,384]{1,0:T(8,128)(2,1)} %pad_maximum_fusion.6.mixed_ref), custom_call_target="tpu_custom_call" | custom-call | flops 5033164800 | bytes 13107200 | tf_op jit(solution)/shard_map/out_wg/pallas_call | solution.py:370
  855.8 11.7 fusion.59
  873.4 23.7 %attend_back.4 = (bf16[8,4,128,1280]{3,2,1,0:T(8,128)(2,1)}, f32[768,384]{1,0:T(8,128)S(1)}, f32[1024,384]{1,0:T(8,128)}) custom-call(bf16[4,8,128,1280]{3,2,1,0:T(8,128)(2,1)} %get-tuple-element.131.weights_ref, bf16[768,384]{1,0:T(8,128)(2,1)S(1)} %fusion.68.query_t_ref, bf16[1024,256]{1,0:T(8,128)(2,1)S(1)} %copy-done.11, ...), custom_call_target="tpu_custom_call" | custom-call | flops 24999999488 | bytes 5242880 | tf_op jit(solution)/shard_map/attend_back/pallas_call | solution.py:276
  897.0 23.1 %attend_back.5 = (bf16[8,4,128,1280]{3,2,1,0:T(8,128)(2,1)}, f32[768,384]{1,0:T(8,128)S(1)}, f32[1024,384]{1,0:T(8,128)}) custom-call(bf16[4,8,128,1280]{3,2,1,0:T(8,128)(2,1)} %get-tuple-element.131.weights_ref, bf16[768,384]{1,0:T(8,128)(2,1)S(1)} %fusion.68.query_t_ref, bf16[1024,256]{1,0:T(8,128)(2,1)S(1)} %copy-done.11, ...), custom_call_target="tpu_custom_call", output_to_operand_aliasing={{0}: (13, {})} | custom-call | flops 24999999488 | bytes 5242880 | tf_op jit(solution)/shard_map/attend_back/pallas_call | solution.py:276
  921.2 11.2 reduce-scatter.8.cloned.1.call-done
  934.7 22.8 %attend_back.6 = (bf16[8,4,128,1280]{3,2,1,0:T(8,128)(2,1)}, f32[768,384]{1,0:T(8,128)S(1)}, f32[1024,384]{1,0:T(8,128)}) custom-call(bf16[4,8,128,1280]{3,2,1,0:T(8,128)(2,1)} %get-tuple-element.131.weights_ref, bf16[768,384]{1,0:T(8,128)(2,1)S(1)} %fusion.68.query_t_ref, bf16[1024,256]{1,0:T(8,128)(2,1)S(1)} %copy-done.12, ...), custom_call_target="tpu_custom_call", output_to_operand_aliasing={{0}: (13, {})} | custom-call | flops 24999999488 | bytes 5242880 | tf_op jit(solution)/shard_map/attend_back/pallas_call | solution.py:276
  957.5 23.1 %attend_back.7 = (bf16[8,4,128,1280]{3,2,1,0:T(8,128)(2,1)}, f32[768,384]{1,0:T(8,128)S(1)}, f32[1024,384]{1,0:T(8,128)}) custom-call(bf16[4,8,128,1280]{3,2,1,0:T(8,128)(2,1)} %get-tuple-element.131.weights_ref, bf16[768,384]{1,0:T(8,128)(2,1)S(1)} %fusion.68.query_t_ref, bf16[1024,256]{1,0:T(8,128)(2,1)S(1)} %copy-done.12, ...), custom_call_target="tpu_custom_call", output_to_operand_aliasing={{0}: (13, {})} | custom-call | flops 24999999488 | bytes 5242880 | tf_op jit(solution)/shard_map/attend_back/pallas_call | solution.py:276
  1052.1 84.2 %reduce_down.1 = (f32[80,1152]{1,0:T(8,128)S(1)}, f32[320,640]{1,0:T(8,128)S(1)}) custom-call(bf16[4,4,2,80,1152]{4,3,2,1,0:T(8,128)(2,1)} %bitcast.137, bf16[4,320,640]{2,1,0:T(8,128)(2,1)S(1)} %pad_maximum_fusion.7.side_ref), custom_call_target="tpu_custom_call" | custom-call | tf_op jit(solution)/shard_map/reduce_down/pallas_call | solution.py:728
  (525 shorter events, 530.4 us)
Async XLA Ops:
  7.2 199.3 %all-gather.5.cloned.1.call-start = ((), (), s32[]{:S(2)}) async-start(), calls=%async_computation.5 | async-start | bytes 13516800 | tf_op jit(solution)/shard_map/all_gather | solution.py:899
  98.8 237.4 %all-gather.7.cloned.1.call-start = ((), (), s32[]{:S(2)}) async-start(), calls=%async_computation.6 | async-start | bytes 9584640 | tf_op jit(solution)/shard_map/all_gather | solution.py:933
  162.2 174.1 %all-gather.9.cloned.1.call-start = ((), (), s32[]{:S(2)}) async-start(), calls=%async_computation.7 | async-start | bytes 9584640 | tf_op jit(solution)/shard_map/all_gather | solution.py:934
  162.9 216.7 %all-gather.11.cloned.1.call-start = ((), (), s32[]{:S(2)}) async-start(), calls=%async_computation.8 | async-start | bytes 9584640 | tf_op jit(solution)/shard_map/all_gather | solution.py:935
  173.8 747.4 %reduce-scatter.10.cloned.1.call-start = ((), (), s32[]{:S(2)}) async-start(), calls=%async_computation.11 | async-start | bytes 9584640 | tf_op jit(solution)/shard_map/reduce_scatter | solution.py:1094
  246.8 24.1 %collective-permute-start.8 = (bf16[192,2560]{1,0:T(8,128)(2,1)S(1)}, bf16[192,2560]{1,0:T(8,128)(2,1)S(1)}, u32[]{:S(2)}, u32[]{:S(2)}) collective-permute-start(bf16[192,2560]{1,0:T(8,128)(2,1)S(1)} %get-tuple-element.334), channel_id=1, source_target_pairs={{0,8},{8,16},{16,24},{1,9},{9,17},{17,25},{2,10},{10,18},{18,26},{... | collective-permute-start | bytes 2949128 | tf_op jit(solution)/shard_map/ppermute | solution.py:801
  249.6 25.5 %collective-permute-start.9 = (bf16[192,2560]{1,0:T(8,128)(2,1)S(1)}, bf16[192,2560]{1,0:T(8,128)(2,1)S(1)}, u32[]{:S(2)}, u32[]{:S(2)}) collective-permute-start(bf16[192,2560]{1,0:T(8,128)(2,1)S(1)} %get-tuple-element.334), channel_id=1, source_target_pairs={{8,0},{16,8},{24,16},{9,1},{17,9},{25,17},{10,2},{18,10},{26,18},{... | collective-permute-start | bytes 2949128 | tf_op jit(solution)/shard_map/ppermute | solution.py:802
  276.7 25.8 %collective-permute-start.11 = (bf16[192,2560]{1,0:T(8,128)(2,1)S(1)}, bf16[192,2560]{1,0:T(8,128)(2,1)}, u32[]{:S(2)}, u32[]{:S(2)}) collective-permute-start(bf16[192,2560]{1,0:T(8,128)(2,1)S(1)} %collective-permute-done.9), channel_id=1, source_target_pairs={{8,0},{16,8},{9,1},{17,9},{10,2},{18,10},{11,3},{19,11},{12,4},{20... | collective-permute-start | bytes 2949128 | tf_op jit(solution)/shard_map/ppermute | solution.py:802
  304.1 26.9 %collective-permute-start.13 = (bf16[192,2560]{1,0:T(8,128)(2,1)}, bf16[192,2560]{1,0:T(8,128)(2,1)}, u32[]{:S(2)}, u32[]{:S(2)}) collective-permute-start(bf16[192,2560]{1,0:T(8,128)(2,1)} %collective-permute-done.11), channel_id=1, source_target_pairs={{8,0},{9,1},{10,2},{11,3},{12,4},{13,5},{14,6},{15,7}} | collective-permute-start | bytes 2949128 | tf_op jit(solution)/shard_map/ppermute | solution.py:802
  307.5 40.4 %collective-permute-start.6 = (bf16[192,2560]{1,0:T(8,128)(2,1)S(1)}, bf16[192,2560]{1,0:T(8,128)(2,1)}, u32[]{:S(2)}, u32[]{:S(2)}) collective-permute-start(bf16[192,2560]{1,0:T(8,128)(2,1)S(1)} %get-tuple-element.335), channel_id=1, source_target_pairs={{0,8},{8,16},{16,24},{1,9},{9,17},{17,25},{2,10},{10,18},{18,26},{... | collective-permute-start | bytes 2949128 | tf_op jit(solution)/shard_map/ppermute | solution.py:801
  314.1 35.2 %collective-permute-start.7 = (bf16[192,2560]{1,0:T(8,128)(2,1)S(1)}, bf16[192,2560]{1,0:T(8,128)(2,1)}, u32[]{:S(2)}, u32[]{:S(2)}) collective-permute-start(bf16[192,2560]{1,0:T(8,128)(2,1)S(1)} %get-tuple-element.335), channel_id=1, source_target_pairs={{8,0},{16,8},{24,16},{9,1},{17,9},{25,17},{10,2},{18,10},{26,18},{... | collective-permute-start | bytes 2949128 | tf_op jit(solution)/shard_map/ppermute | solution.py:802
  350.9 23.2 %collective-permute-start.15 = (bf16[192,2560]{1,0:T(8,128)(2,1)}, bf16[192,2560]{1,0:T(8,128)(2,1)}, u32[]{:S(2)}, u32[]{:S(2)}) collective-permute-start(bf16[192,2560]{1,0:T(8,128)(2,1)} %collective-permute-done.7), channel_id=1, source_target_pairs={{8,0},{16,8},{9,1},{17,9},{10,2},{18,10},{11,3},{19,11},{12,4},{20... | collective-permute-start | bytes 2949128 | tf_op jit(solution)/shard_map/ppermute | solution.py:802
  375.7 22.3 %collective-permute-start.17 = (bf16[192,2560]{1,0:T(8,128)(2,1)}, bf16[192,2560]{1,0:T(8,128)(2,1)}, u32[]{:S(2)}, u32[]{:S(2)}) collective-permute-start(bf16[192,2560]{1,0:T(8,128)(2,1)} %collective-permute-done.15), channel_id=1, source_target_pairs={{8,0},{9,1},{10,2},{11,3},{12,4},{13,5},{14,6},{15,7}} | collective-permute-start | bytes 2949128 | tf_op jit(solution)/shard_map/ppermute | solution.py:802
  470.0 24.3 %collective-permute-start.24 = (bf16[192,2560]{1,0:T(8,128)(2,1)S(1)}, bf16[192,2560]{1,0:T(8,128)(2,1)S(1)}, u32[]{:S(2)}, u32[]{:S(2)}) collective-permute-start(bf16[192,2560]{1,0:T(8,128)(2,1)S(1)} %get-tuple-element.296), channel_id=1, source_target_pairs={{0,8},{8,16},{16,24},{1,9},{9,17},{17,25},{2,10},{10,18},{18,26},{... | collective-permute-start | bytes 2949128 | tf_op jit(solution)/shard_map/ppermute | solution.py:801
  472.2 22.1 %collective-permute-start.25 = (bf16[192,2560]{1,0:T(8,128)(2,1)S(1)}, bf16[192,2560]{1,0:T(8,128)(2,1)S(1)}, u32[]{:S(2)}, u32[]{:S(2)}) collective-permute-start(bf16[192,2560]{1,0:T(8,128)(2,1)S(1)} %get-tuple-element.296), channel_id=1, source_target_pairs={{8,0},{16,8},{24,16},{9,1},{17,9},{25,17},{10,2},{18,10},{26,18},{... | collective-permute-start | bytes 2949128 | tf_op jit(solution)/shard_map/ppermute | solution.py:802
  473.7 36.7 %collective-permute-start.28 = (bf16[192,2560]{1,0:T(8,128)(2,1)S(1)}, bf16[192,2560]{1,0:T(8,128)(2,1)S(1)}, u32[]{:S(2)}, u32[]{:S(2)}) collective-permute-start(bf16[192,2560]{1,0:T(8,128)(2,1)S(1)} %get-tuple-element.326), channel_id=1, source_target_pairs={{0,8},{1,9},{2,10},{3,11},{4,12},{5,13},{6,14},{7,15}} | collective-permute-start | bytes 2949128 | tf_op jit(solution)/shard_map/ppermute | solution.py:821
  478.3 32.1 %collective-permute-start.29 = (bf16[192,2560]{1,0:T(8,128)(2,1)S(1)}, bf16[192,2560]{1,0:T(8,128)(2,1)S(1)}, u32[]{:S(2)}, u32[]{:S(2)}) collective-permute-start(bf16[192,2560]{1,0:T(8,128)(2,1)S(1)} %get-tuple-element.325), channel_id=1, source_target_pairs={{24,16},{25,17},{26,18},{27,19},{28,20},{29,21},{30,22},{31,23}} | collective-permute-start | bytes 2949128 | tf_op jit(solution)/shard_map/ppermute | solution.py:822
  495.1 24.3 %collective-permute-start.27 = (bf16[192,2560]{1,0:T(8,128)(2,1)S(1)}, bf16[192,2560]{1,0:T(8,128)(2,1)S(1)}, u32[]{:S(2)}, u32[]{:S(2)}) collective-permute-start(bf16[192,2560]{1,0:T(8,128)(2,1)S(1)} %collective-permute-done.25), channel_id=1, source_target_pairs={{8,0},{16,8},{9,1},{17,9},{10,2},{18,10},{11,3},{19,11},{12,4},{20... | collective-permute-start | bytes 2949128 | tf_op jit(solution)/shard_map/ppermute | solution.py:802
  555.1 22.7 %collective-permute-start.35 = (bf16[192,2560]{1,0:T(8,128)(2,1)}, bf16[192,2560]{1,0:T(8,128)(2,1)}, u32[]{:S(2)}, u32[]{:S(2)}) collective-permute-start(bf16[192,2560]{1,0:T(8,128)(2,1)} %get-tuple-element.321), channel_id=1, source_target_pairs={{8,0},{16,8},{24,16},{9,1},{17,9},{25,17},{10,2},{18,10},{26,18},{... | collective-permute-start | bytes 2949128 | tf_op jit(solution)/shard_map/ppermute | solution.py:822
  583.8 31.3 %collective-permute-start.36 = (bf16[192,2560]{1,0:T(8,128)(2,1)S(1)}, bf16[192,2560]{1,0:T(8,128)(2,1)}, u32[]{:S(2)}, u32[]{:S(2)}) collective-permute-start(bf16[192,2560]{1,0:T(8,128)(2,1)S(1)} %get-tuple-element.292), channel_id=1, source_target_pairs={{0,8},{8,16},{16,24},{1,9},{9,17},{17,25},{2,10},{10,18},{18,26},{... | collective-permute-start | bytes 2949128 | tf_op jit(solution)/shard_map/ppermute | solution.py:801
  592.5 22.6 %collective-permute-start.37 = (bf16[192,2560]{1,0:T(8,128)(2,1)S(1)}, bf16[192,2560]{1,0:T(8,128)(2,1)}, u32[]{:S(2)}, u32[]{:S(2)}) collective-permute-start(bf16[192,2560]{1,0:T(8,128)(2,1)S(1)} %get-tuple-element.292), channel_id=1, source_target_pairs={{8,0},{16,8},{24,16},{9,1},{17,9},{25,17},{10,2},{18,10},{26,18},{... | collective-permute-start | bytes 2949128 | tf_op jit(solution)/shard_map/ppermute | solution.py:802
  616.9 25.0 %collective-permute-start.39 = (bf16[192,2560]{1,0:T(8,128)(2,1)}, bf16[192,2560]{1,0:T(8,128)(2,1)}, u32[]{:S(2)}, u32[]{:S(2)}) collective-permute-start(bf16[192,2560]{1,0:T(8,128)(2,1)} %collective-permute-done.37), channel_id=1, source_target_pairs={{8,0},{16,8},{9,1},{17,9},{10,2},{18,10},{11,3},{19,11},{12,4},{20... | collective-permute-start | bytes 2949128 | tf_op jit(solution)/shard_map/ppermute | solution.py:802
  643.5 22.6 %collective-permute-start.42 = (bf16[192,2560]{1,0:T(8,128)(2,1)S(1)}, bf16[192,2560]{1,0:T(8,128)(2,1)S(1)}, u32[]{:S(2)}, u32[]{:S(2)}) collective-permute-start(bf16[192,2560]{1,0:T(8,128)(2,1)S(1)} %get-tuple-element.320), channel_id=1, source_target_pairs={{0,8},{1,9},{2,10},{3,11},{4,12},{5,13},{6,14},{7,15}} | collective-permute-start | bytes 2949128 | tf_op jit(solution)/shard_map/ppermute | solution.py:821
  672.6 28.1 %collective-permute-start.44 = (bf16[192,2560]{1,0:T(8,128)(2,1)}, bf16[192,2560]{1,0:T(8,128)(2,1)}, u32[]{:S(2)}, u32[]{:S(2)}) collective-permute-start(bf16[192,2560]{1,0:T(8,128)(2,1)} %get-tuple-element.318), channel_id=1, source_target_pairs={{0,8},{8,16},{1,9},{9,17},{2,10},{10,18},{3,11},{11,19},{4,12},{12... | collective-permute-start | bytes 2949128 | tf_op jit(solution)/shard_map/ppermute | solution.py:821
  677.9 22.7 %collective-permute-start.45 = (bf16[192,2560]{1,0:T(8,128)(2,1)}, bf16[192,2560]{1,0:T(8,128)(2,1)}, u32[]{:S(2)}, u32[]{:S(2)}) collective-permute-start(bf16[192,2560]{1,0:T(8,128)(2,1)} %get-tuple-element.317), channel_id=1, source_target_pairs={{16,8},{24,16},{17,9},{25,17},{18,10},{26,18},{19,11},{27,19},{20,... | collective-permute-start | bytes 2949128 | tf_op jit(solution)/shard_map/ppermute | solution.py:822
  700.7 220.5 %reduce-scatter.6.cloned.1.call-start = ((), (), s32[]{:S(2)}) async-start(), calls=%async_computation.9 | async-start | bytes 9584640 | tf_op jit(solution)/shard_map/reduce_scatter | solution.py:1092
  707.7 22.2 %collective-permute-start.46 = (bf16[192,2560]{1,0:T(8,128)(2,1)S(1)}, bf16[192,2560]{1,0:T(8,128)(2,1)S(1)}, u32[]{:S(2)}, u32[]{:S(2)}) collective-permute-start(bf16[192,2560]{1,0:T(8,128)(2,1)S(1)} %get-tuple-element.316), channel_id=1, source_target_pairs={{0,8},{8,16},{16,24},{1,9},{9,17},{17,25},{2,10},{10,18},{18,26},{... | collective-permute-start | bytes 2949128 | tf_op jit(solution)/shard_map/ppermute | solution.py:821
  760.0 25.6 %collective-permute-start.48 = (bf16[192,2560]{1,0:T(8,128)(2,1)}, bf16[192,2560]{1,0:T(8,128)(2,1)}, u32[]{:S(2)}, u32[]{:S(2)}) collective-permute-start(bf16[192,2560]{1,0:T(8,128)(2,1)} %get-tuple-element.314), channel_id=1, source_target_pairs={{0,8},{1,9},{2,10},{3,11},{4,12},{5,13},{6,14},{7,15}} | collective-permute-start | bytes 2949128 | tf_op jit(solution)/shard_map/ppermute | solution.py:821
  785.6 146.7 %reduce-scatter.8.cloned.1.call-start = ((), (), s32[]{:S(2)}) async-start(), calls=%async_computation.10 | async-start | bytes 9584640 | tf_op jit(solution)/shard_map/reduce_scatter | solution.py:1093
  789.3 24.5 %collective-permute-start.50 = (bf16[192,2560]{1,0:T(8,128)(2,1)}, bf16[192,2560]{1,0:T(8,128)(2,1)}, u32[]{:S(2)}, u32[]{:S(2)}) collective-permute-start(bf16[192,2560]{1,0:T(8,128)(2,1)} %get-tuple-element.312), channel_id=1, source_target_pairs={{0,8},{8,16},{1,9},{9,17},{2,10},{10,18},{3,11},{11,19},{4,12},{12... | collective-permute-start | bytes 2949128 | tf_op jit(solution)/shard_map/ppermute | solution.py:821
  813.9 236.0 %reduce-scatter.12.cloned.1.call-start = ((), (), s32[]{:S(2)}) async-start(), calls=%async_computation.12 | async-start | bytes 14745600 | tf_op jit(solution)/shard_map/reduce_scatter | solution.py:1104
  867.5 268.8 %reduce-scatter.14.cloned.1.call-start = ((), (), s32[]{:S(2)}) async-start(), calls=%async_computation.13 | async-start | bytes 11796480 | tf_op jit(solution)/shard_map/reduce_scatter | solution.py:1115
  (140 other events, 2356.7 us)
Sparse Core Ops, SparseCore 0:
  99.0 107.4 all-gather.4
  208.3 53.1 all-gather.6
  263.4 54.9 all-gather.8
  320.1 54.9 all-gather.10
  700.8 71.6 reduce-scatter.9
  785.8 70.9 reduce-scatter.5
  860.3 72.0 reduce-scatter.7
  936.0 95.1 reduce-scatter.11
  1034.7 99.4 reduce-scatter.13
